TPU v7x, 32 devices: a whole 2x2x4 slice. The times are simulated.
32 devices in a mesh: dp: 8 (over z, x), seq: 4 (over y, core).
Axes of the slice: x: 2, y: 2, z: 4, core: 2. Of those that a mesh axis runs over, the one named last changes fastest.
Arguments:
- inputs: bfloat16 [24, 1024, 1024], P('dp', 'seq'), may hold values from -6 to 6
- segment_ids: int32 [24, 1024], P('dp', 'seq'), may hold values from 0 to 7, as said below
- doc_times: int32 [24, 8], P('dp'), may hold values from 0 to 999
- time_weight: bfloat16 [256, 1024], replicated, may hold values from -0.375 to 0.375
- time_bias: bfloat16 [1024], replicated, may hold values from -3 to 3
- norm1_gain: bfloat16 [1024], replicated, may hold values from 0.099609375 to 1.8984375
- norm1_bias: bfloat16 [1024], replicated, may hold values from -3 to 3
- qkv_weight: bfloat16 [1024, 3072], replicated, may hold values from -0.1875 to 0.1875
- qkv_bias: bfloat16 [3072], replicated, may hold values from -3 to 3
- out_weight: bfloat16 [1024, 1024], replicated, may hold values from -1.5 to 1.5
- out_bias: bfloat16 [1024], replicated, may hold values from -3 to 3
- norm2_gain: bfloat16 [1024], replicated, may hold values from 0.099609375 to 1.8984375
- norm2_bias: bfloat16 [1024], replicated, may hold values from -3 to 3
- up_weight: bfloat16 [1024, 4096], replicated, may hold values from -0.1875 to 0.1875
- up_bias: bfloat16 [4096], replicated, may hold values from -3 to 3
- down_weight: bfloat16 [4096, 1024], replicated, may hold values from -0.09375 to 0.09375
- down_bias: bfloat16 [1024], replicated, may hold values from -3 to 3
- cotangent: bfloat16 [24, 1024, 1024], P('dp', 'seq'), may hold values from -6 to 6
Outputs:
- output: bfloat16 [24, 1024, 1024], P('dp', 'seq')
- input_grad: bfloat16 [24, 1024, 1024], P('dp', 'seq')
- time_weight_grad: float32 [256, 1024], P('dp')
- time_bias_grad: float32 [1024], P('dp')
- norm1_gain_grad: float32 [1024], P('dp')
- norm1_bias_grad: float32 [1024], P('dp')
- qkv_weight_grad: float32 [1024, 3072], P('dp')
- qkv_bias_grad: float32 [3072], P('dp')
- out_weight_grad: float32 [1024, 1024], P('dp')
- out_bias_grad: float32 [1024], P('dp')
- norm2_gain_grad: float32 [1024], P('dp')
- norm2_bias_grad: float32 [1024], P('dp')
- up_weight_grad: float32 [1024, 4096], P('dp')
- up_bias_grad: float32 [4096], P('dp')
- down_weight_grad: float32 [4096, 1024], P('dp')
- down_bias_grad: float32 [1024], P('dp')
Inputs may be any that keep to these rules, and one draw needn't show every extreme that they name: `segment_ids`: along each row the ids never fall and the last token has id 8 - 1. In each aligned block of 3 rows one row holds a document that begins among the first 256 tokens and ends among the last 256.
All inputs are finite; a program needn't handle non-finite values.
Results may differ from a plain program's by a relative error of at most 0.014.
Values may be sent and summed in bfloat16 or wider, within the bound.
No kernel may reach another device: no remote copies, remote signals or barrier semaphores. Data moves between devices by JAX's collectives and lax.ppermute only.
A program may use at most 320 MiB of HBM per device.

v0:
```python
import functools
import math

import jax
import jax.numpy as jnp
from jax import lax
from jax.experimental import pallas as pl
from jax.experimental.pallas import tpu as pltpu
from jax.sharding import Mesh, PartitionSpec as P

HEADS = 16
HEAD_DIM = 64
TEMB = 256
SEGS = 8
EPSILON = 1e-05
F32 = jnp.float32
BF16 = jnp.bfloat16
NEG = -1e30
LOG2E = math.log2(math.e)
GELU_A = math.sqrt(2.0 / math.pi)
GELU_B = GELU_A * 0.044715
BLOCK = 256
VMEM = 60 * 1024 * 1024


def swap(value, axis):
    return lax.ppermute(value, axis, [(0, 1), (1, 0)])


def time_features(doc_times, column, half_size):
    frequency = jnp.exp(-math.log(10000.0) * (column % half_size).astype(F32) / half_size)
    angles = doc_times.astype(F32)[..., None] * frequency
    return jnp.where(column < half_size, jnp.sin(angles), jnp.cos(angles)).astype(BF16)


def rotary_tables(positions, head_size):
    half_size = head_size // 2
    frequency = jnp.exp(-math.log(10000.0) * 2.0 * jnp.arange(half_size, dtype=F32) / head_size)
    angles = positions.astype(F32)[..., None] * frequency
    cos_tab, sin_tab = jnp.cos(angles), jnp.sin(angles)
    return (
        jnp.concatenate([cos_tab] * 4, axis=-1),
        jnp.concatenate([-sin_tab, sin_tab, -sin_tab, sin_tab], axis=-1),
    )


def dot(left_op, right_op, left_dim=1, right_dim=0):
    return lax.dot_general(
        left_op, right_op, (((left_dim,), (right_dim,)), ((), ())), preferred_element_type=F32
    )


def turn(values, cos_tab, sin_tab):
    slabs = []
    lane = lax.broadcasted_iota(jnp.int32, (values.shape[0], 128), 1)
    first = lane % HEAD_DIM < HEAD_DIM // 2
    for start in range(0, values.shape[1], 128):
        slab = values[:, start : start + 128]
        partner = jnp.where(
            first, pltpu.roll(slab, 128 - HEAD_DIM // 2, 1), pltpu.roll(slab, HEAD_DIM // 2, 1)
        )
        slabs.append(slab * cos_tab + partner * sin_tab)
    return jnp.concatenate(slabs, axis=1)


def split_low(values):
    high = values.astype(BF16)
    return jnp.concatenate([high, (values - high.astype(F32)).astype(BF16)], axis=0)


def centre(values):
    scale = 1.0 / values.shape[-1]
    centred = values - jnp.sum(values, axis=-1, keepdims=True) * scale
    spread = jnp.sum(centred * centred, axis=-1, keepdims=True) * scale
    inverse = lax.rsqrt(spread + EPSILON)
    return centred * inverse, inverse


def norm_back(grad, gain, hat, inverse):
    scale = 1.0 / grad.shape[-1]
    scaled = grad * gain
    mean = jnp.sum(scaled, axis=-1, keepdims=True) * scale
    along = jnp.sum(scaled * hat, axis=-1, keepdims=True) * scale
    return inverse * (scaled - mean - hat * along)


def call(body, name, prefetch, grid, ins, outs, scratch=(), deps=(), held=()):
    count = len(prefetch) + len(ins)
    extra = [array for array, _ in held] + list(deps)

    def kernel(*refs):
        body(*refs[:count], *refs[count + len(extra) :])

    return pl.pallas_call(
        kernel,
        grid_spec=pltpu.PrefetchScalarGridSpec(
            num_scalar_prefetch=len(prefetch),
            grid=grid,
            in_specs=[spec for _, spec in ins] + [pl.BlockSpec(memory_space=pl.ANY)] * len(extra),
            out_specs=[spec for _, _, spec in outs],
            scratch_shapes=list(scratch),
        ),
        out_shape=[jax.ShapeDtypeStruct(shape, kind) for shape, kind, _ in outs],
        input_output_aliases={count + n: out for n, (_, out) in enumerate(held)},
        compiler_params=pltpu.CompilerParams(vmem_limit_bytes=VMEM),
        name=name,
    )(*prefetch, *[array for array, _ in ins], *extra)


def fixed(shape):
    return pl.BlockSpec(shape, lambda *_: (0,) * len(shape))


def along(shape, axis=0, start=0):
    return pl.BlockSpec(shape, lambda g, *_: tuple(start + g if n == axis else 0 for n in range(len(shape))))


def norm1_body(x_ref, seg_ref, shift_ref, gain_ref, bias_ref, stream_ref, low_ref):
    slots = lax.broadcasted_iota(jnp.int32, (SEGS, seg_ref.shape[-1]), 0) == seg_ref[0]
    onehot = slots.astype(F32).astype(BF16)
    added = dot(jnp.concatenate([onehot, onehot], axis=0), split_low(shift_ref[0]), 0, 0)
    stream = x_ref[0].astype(F32) + added
    hat, _ = centre(stream)
    stream_ref[0] = stream
    low_ref[0] = (hat * gain_ref[...] + bias_ref[...]).astype(BF16)


def norm1(x, seg, shift, gain, bias):
    rows, shard, model = x.shape
    block = along((1, shard, model))
    return call(
        norm1_body, "norm1", (), (rows,),
        [(x, block), (seg, along((1, 1, shard))), (shift, along((1, SEGS, model))), (gain, fixed((1, model))), (bias, fixed((1, model)))],
        [(x.shape, F32, block), (x.shape, BF16, block)],
    )


def qkv_body(me_ref, a_ref, b_ref, w_ref, bias_ref, cos_ref, sin_ref, out_ref, all_ref, own_ref):
    rows, shard, model = a_ref.shape
    width = w_ref.shape[1]
    refs = (a_ref, b_ref)
    step = pl.program_id(0)

    @pl.when(step == 0)
    def _():
        for n, x_ref in enumerate(refs):
            all_ref[n] = x_ref[...]

    def run(turned):
        w, bias = w_ref[...], bias_ref[...].astype(F32)
        found = [dot(x_ref[...].reshape(rows * shard, model), w) for x_ref in refs]
        for n, full in enumerate(found):
            for r in range(rows):
                values = full[r * shard : (r + 1) * shard] + bias
                if turned:
                    values = turn(values, cos_ref[n], sin_ref[n]) * jnp.where(step == 0, LOG2E * HEAD_DIM**-0.5, 1.0)
                out_ref[0, n, r] = values.astype(BF16)

    own_ref[...] = w_ref[...].T

    @pl.when(step < 2)
    def _():
        run(True)

    @pl.when(step == 2)
    def _():
        run(False)


def project_qkv(pair, parts, me, first, second, weight, bias, cos_tab, sin_tab, held=(), deps=()):
    rows, shard, model = first.shape
    width = model // parts
    return call(
        qkv_body, "qkv", (me,), (3,),
        [(first, fixed(first.shape)), (second, fixed(first.shape))]
        + [
            (weight, pl.BlockSpec((model, width), lambda g, m: (0, g * parts + m[0]))),
            (bias, pl.BlockSpec((1, width), lambda g, m: (0, g * parts + m[0]))),
            (cos_tab, pl.BlockSpec((2, shard, 128), lambda g, m: (pair, 0, 0))),
            (sin_tab, pl.BlockSpec((2, shard, 128), lambda g, m: (pair, 0, 0))),
        ],
        [
            ((3, parts, rows, shard, width), BF16, pl.BlockSpec((1, 2, rows, shard, width), lambda g, m: (g, pair, 0, 0, 0))),
            ((parts, rows, shard, model), BF16, pl.BlockSpec((2, rows, shard, model), lambda g, m: (pair, 0, 0, 0))),
            ((3 * width, model), BF16, along((width, model))),
        ],
        held=[(array, n) for n, array in enumerate(held)], deps=deps
    )


def seg_columns(segq_all, segk):
    pieces, shard, _ = segk.shape
    for j in range(pieces):
        row = jnp.broadcast_to(segq_all[j:j+1].astype(F32), (128, shard))
        segk[j] = row.T

def attend_body(start, cnt_ref, idx_ref, qkv_ref, seg_ref, o_ref, one_ref, far_ref, lse_ref, vt, segk, qmt, acc):
    row = pl.program_id(0) + start
    _, pieces, _, shard, width = qkv_ref.shape
    heads = width // HEAD_DIM

    @pl.when(pl.program_id(0) == 0)
    def _():
        qmt[...] = jnp.zeros_like(qmt)

    for j in range(pieces):
        vt[j] = qkv_ref[2, j, 0].T
        qt = qkv_ref[0, j, 0].T
        for h in range(heads):
            at = slice(h * HEAD_DIM, (h + 1) * HEAD_DIM)
            qmt[j, at, h * shard : (h + 1) * shard] = qt[at]
    seg_columns(seg_ref[0], segk)

    @pl.loop(0, pieces)
    def _(piece):
        attend_piece(row * pieces + piece, piece, cnt_ref, idx_ref, qkv_ref.at[1], seg_ref, lse_ref, vt, segk, qmt, acc)

    for j in range(pieces):
        o_ref[j, 0] = acc[j].T.astype(BF16)
    one_ref[0] = o_ref[1, 0]
    far_ref[:, 0] = o_ref[2:, 0]


def attend_piece(at_q, piece, cnt_ref, idx_ref, k_ref, seg_ref, lse_ref, vt, segk, qmt, acc):
    pieces, _, shard, width = k_ref.shape
    heads = width // HEAD_DIM
    seg_q = seg_ref[0, pl.ds(piece, 1)].astype(F32)

    def run(count):
        @pl.when(cnt_ref[at_q] == count)
        def _():
            qm = qmt[piece]
            places = [idx_ref[at_q * pieces + t] for t in range(count)]
            top, tot, out = [None] * heads, [None] * heads, [None] * heads
            later = dot(k_ref[places[0], 0], qm)
            for t in range(count):
                s = later
                if t + 1 < count:
                    later = dot(k_ref[places[t + 1], 0], qm)
                col = segk[places[t]]
                same = jnp.concatenate([col] * (shard // 128), axis=1) == seg_q
                for h in range(heads):
                    at = slice(h * HEAD_DIM, (h + 1) * HEAD_DIM)
                    sh = jnp.where(same, s[:, h * shard : (h + 1) * shard], NEG)
                    best = jnp.max(sh, axis=0, keepdims=True)
                    if t:
                        best = jnp.maximum(top[h], best)
                        fade = jnp.exp2(top[h] - best)
                    p = jnp.exp2(sh - best)
                    total = jnp.sum(p, axis=0, keepdims=True)
                    found = dot(vt[places[t], at], p.astype(BF16))
                    if t:
                        total = tot[h] * fade + total
                        found = out[h] * fade + found
                    top[h], tot[h], out[h] = best, total, found
            for h in range(heads):
                acc[piece, h * HEAD_DIM : (h + 1) * HEAD_DIM] = out[h] / tot[h]
                lse_ref[0, piece, h : h + 1] = top[h] + jnp.log2(tot[h])

    for count in range(1, pieces + 1):
        run(count)


def attend(start, count, cnt, idx, qkv, seg, held=()):
    _, pieces, rows, shard, width = qkv.shape
    heads = width // HEAD_DIM
    pairs = count * (pieces * shard) ** 2
    return call(
        functools.partial(attend_body, start), "attend", (cnt, idx), (count,),
        [(qkv, along((3, pieces, 1, shard, width), 2, start)), (seg, along((1, pieces, shard), 0, start))],
        [
            ((pieces, rows, shard, width), BF16, along((pieces, 1, shard, width), 1, start)),
            ((count, shard, width), BF16, along((1, shard, width))),
            ((2, count, shard, width), BF16, along((2, 1, shard, width), 1)),
            ((rows, pieces, 8, shard), F32, along((1, pieces, 8, shard), 0, start)),
        ],
        [
            pltpu.VMEM((pieces, width, shard), BF16),
            pltpu.VMEM((pieces, shard, 128), F32),
            pltpu.VMEM((pieces, width, heads * shard), BF16),
            pltpu.VMEM((pieces, width, shard), F32),
        ],
        held=list(zip(held, (0, 3)))
    )


def attend_back_body(
    start, cnt_ref, idx_ref, qkv_ref, o_ref, do0, do1, do2, do3, lse_ref, seg_ref, cos_ref, sin_ref, w_ref,
    g_ref, p0_ref, p1_ref, p2_ref, p3_ref, kt, segk, dk, dv, dqt, qmt, gmt, qst, gst, low,
):
    row = pl.program_id(0) + start
    _, pieces, _, shard, width = qkv_ref.shape
    heads = width // HEAD_DIM

    @pl.when(pl.program_id(0) == 0)
    def _():
        qmt[...] = jnp.zeros_like(qmt)
        gmt[...] = jnp.zeros_like(gmt)

    seg_columns(seg_ref[0], segk)
    dk[...] = jnp.zeros_like(dk)
    dv[...] = jnp.zeros_like(dv)
    lane = lax.broadcasted_iota(jnp.int32, (shard, width), 1) // HEAD_DIM
    chosen = lax.broadcasted_iota(jnp.int32, (8, width), 1) // HEAD_DIM
    chosen = (chosen == lax.broadcasted_iota(jnp.int32, (8, width), 0)).astype(BF16)
    for j, do_ref in enumerate((do0, do1, do2, do3)):
        kt[j] = qkv_ref[1, j, 0].T
        q, do = qkv_ref[0, j, 0], do_ref[...].reshape(shard, width)
        qt, gt = q.T, do.T
        for h in range(heads):
            at, qa = slice(h * HEAD_DIM, (h + 1) * HEAD_DIM), slice(h * shard, (h + 1) * shard)
            qmt[j, at, qa] = qt[at]
            gmt[j, at, qa] = gt[at]
            qst[j, qa] = jnp.where(lane == h, q, jnp.zeros_like(q))
            gst[j, qa] = jnp.where(lane == h, do, jnp.zeros_like(do))
        prod = do.astype(F32) * o_ref[j, 0].astype(F32)
        high = prod.astype(BF16)
        low[j] = dot(chosen, high, 1, 1) + dot(chosen, (prod - high.astype(F32)).astype(BF16), 1, 1)

    @pl.loop(0, pieces)
    def _(piece):
        back_piece(
            row * pieces + piece, piece, cnt_ref, idx_ref, qkv_ref.at[1], qkv_ref.at[2], lse_ref, seg_ref,
            kt, segk, dk, dv, dqt, qmt, gmt, qst, gst, low,
        )

    for j, ref in ((1, p1_ref), (3, p3_ref), (0, p0_ref), (2, p2_ref)):
        grad_q = turn(dqt[j].T * HEAD_DIM**-0.5, cos_ref[j], -sin_ref[j]).astype(BF16)
        grad_k = turn(dk[j] * (1 / LOG2E), cos_ref[j], -sin_ref[j]).astype(BF16)
        grad = jnp.concatenate([grad_q, grad_k, dv[j].astype(BF16)], axis=1)
        g_ref[j, 0] = grad
        ref[0] = dot(grad, w_ref[...]).astype(BF16)


def back_piece(
    at_q, piece, cnt_ref, idx_ref, k_ref, v_ref, lse_ref, seg_ref, kt, segk, dk, dv, dqt, qmt, gmt, qst, gst, low
):
    pieces, _, shard, width = k_ref.shape
    heads = width // HEAD_DIM
    lse, delta = lse_ref[0, piece], low[piece]
    seg_q = seg_ref[0, pl.ds(piece, 1)].astype(F32)

    def run(count):
        @pl.when(cnt_ref[at_q] == count)
        def _():
            places = [idx_ref[at_q * pieces + t] for t in range(count)]
            qm, gm = qmt[piece], gmt[piece]
            later = dot(k_ref[places[0], 0], qm), dot(v_ref[places[0], 0], gm)
            out = [None] * heads
            for t in range(count):
                s, dp = later
                j = places[t]
                if t + 1 < count:
                    later = dot(k_ref[places[t + 1], 0], qm), dot(v_ref[places[t + 1], 0], gm)
                col = segk[j]
                same = jnp.concatenate([col] * (shard // 128), axis=1) == seg_q
                ps, dss = [], []
                for h in range(heads):
                    at, qa = slice(h * HEAD_DIM, (h + 1) * HEAD_DIM), slice(h * shard, (h + 1) * shard)
                    p = jnp.exp2(jnp.where(same, s[:, qa] - lse[h : h + 1], NEG))
                    ds = (p * (dp[:, qa] - delta[h : h + 1])).astype(BF16)
                    ps.append(p.astype(BF16))
                    dss.append(ds)
                    found = dot(kt[j, at], ds)
                    out[h] = found if t == 0 else out[h] + found
                dv[j] += dot(jnp.concatenate(ps, axis=1), gst[piece])
                dk[j] += dot(jnp.concatenate(dss, axis=1), qst[piece])
            for h in range(heads):
                dqt[piece, h * HEAD_DIM : (h + 1) * HEAD_DIM] = out[h]

    for count in range(1, pieces + 1):
        run(count)


def attend_back(start, count, cnt, idx, qkv, o, do, lse, seg, cos_tab, sin_tab, weight, held=(), deps=()):
    _, pieces, rows, shard, width = qkv.shape
    model = weight.shape[1]
    heads = width // HEAD_DIM
    table = fixed((pieces, shard, 128))
    pairs = count * (pieces * shard) ** 2
    square, wide = (pieces, width, heads * shard), (pieces, shard, width)
    one = along((1, shard, width), 0, start)
    return call(
        functools.partial(attend_back_body, start), "attend_back", (cnt, idx), (count,),
        [(qkv, along((3, pieces, 1, shard, width), 2, start)), (o, along((pieces, 1, shard, width), 1, start))]
        + [(do[0], one), (do[1], one), (do[2], along((1, 1, shard, width), 1, start)), (do[3], one)]
        + [(lse, along((1, pieces, 8, shard), 0, start)), (seg, along((1, pieces, shard), 0, start))]
        + [(cos_tab, table), (sin_tab, table), (weight, fixed(weight.shape))],
        [((pieces, rows, shard, 3 * width), BF16, along((pieces, 1, shard, 3 * width), 1, start))]
        + [((count, shard, model), BF16, along((1, shard, model)))] * pieces,
        [
            pltpu.VMEM((pieces, width, shard), BF16),
            pltpu.VMEM((pieces, shard, 128), F32),
            pltpu.VMEM(wide, F32),
            pltpu.VMEM(wide, F32),
            pltpu.VMEM((pieces, width, shard), F32),
            pltpu.VMEM(square, BF16),
            pltpu.VMEM(square, BF16),
            pltpu.VMEM((pieces, heads * shard, width), BF16),
            pltpu.VMEM((pieces, heads * shard, width), BF16),
            pltpu.VMEM((pieces, 8, shard), F32),
        ],
        held=[(array, 0) for array in held], deps=deps
    )


def middle_body(
    order_ref, a0, a1, a2, a3, w0, w1, w2, w3, stream_ref, bias_ref, gain_ref, shift_ref, mid_ref, low_ref, all_ref,
):
    _, shard, model = stream_ref.shape
    total = 0.0
    for n, (a, w) in enumerate(((a0, w0), (a1, w1), (a2, w2), (a3, w3))):
        values = a[...].reshape(shard, a.shape[-1])
        total = total + dot(values, w[...])
        all_ref[0, :, n * a.shape[-1] : (n + 1) * a.shape[-1]] = values
    mid = stream_ref[0] + (total + bias_ref[...])
    hat, _ = centre(mid)
    mid_ref[0] = mid
    low_ref[0] = (hat * gain_ref[...] + shift_ref[...]).astype(BF16)


def out_blocks(weight, parts):
    width = weight.shape[0] // parts

    def block(i):
        return pl.BlockSpec((width, weight.shape[1]), lambda g, o: (o[i], 0))

    return [(weight, block(i)) for i in range(parts)]


def middle_norm(start, count, order, attended, weight, stream, bias, gain, shift, held=()):
    rows, shard, model = stream.shape
    parts = len(attended)
    width = model // parts
    block, line, one = along((1, shard, model), 0, start), fixed((1, model)), along((1, shard, width))
    first = [along((1, 1, shard, width), 1, start), one, along((1, 1, shard, width), 1), one]
    return call(
        middle_body, "middle", (order,), (count,),
        list(zip(attended, first)) + out_blocks(weight, parts) + [(stream, block), (bias, line), (gain, line), (shift, line)],
        [
            (stream.shape, F32, block),
            ((count, shard, model), BF16, along((1, shard, model))),
            (stream.shape, BF16, block),
        ],
        held=list(zip(held, (0, 2)))
    )


def cot_body(blk_ref, a_ref, b_ref, up_ref, down_ref, g_ref, up_out, down_out, both_ref):
    tokens = a_ref.shape[0]
    down = down_ref[...]

    @pl.when(pl.program_id(0) == 0)
    def _():
        both_ref[0:tokens] = a_ref[...]
        both_ref[tokens:] = b_ref[...]

    g_ref[0:tokens] = dot(a_ref[...], down, 1, 1).astype(BF16)
    g_ref[tokens:] = dot(b_ref[...], down, 1, 1).astype(BF16)
    up_out[...] = up_ref[...]
    down_out[...] = down


def cot_down(blk, own, other, up, down, picked, half):
    tokens, model = own.shape
    steps = half // BLOCK
    column = along((2 * tokens, BLOCK), 1)
    if picked:
        up_at, down_at = along((model, BLOCK), 1), along((BLOCK, model))
    else:
        up_at = pl.BlockSpec((model, BLOCK), lambda g, b: (0, b[g]))
        down_at = pl.BlockSpec((BLOCK, model), lambda g, b: (b[g], 0))
    return call(
        cot_body, "cot_down", (blk,), (steps,),
        [(own, fixed(own.shape)), (other, fixed(own.shape)), (up, up_at), (down, down_at)],
        [
            ((2 * tokens, half), BF16, column),
            ((model, half), BF16, along((model, BLOCK), 1)),
            ((half, model), BF16, along((BLOCK, model))),
            ((2 * tokens, model), BF16, fixed((2 * tokens, model))),
        ]
    )


def hidden_body(blocks, *refs):
    pieces, refs = refs[:-10], refs[-10:]
    g_ref, up_ref, row_ref, bias_ref, act_ref, grad_ref, sum_ref, both_ref, part_ref, held = refs
    sizes = [ref.shape[0] * ref.shape[1] for ref in pieces]
    starts = [sum(sizes[:n]) for n in range(len(sizes))]
    step = pl.program_id(0)

    @pl.when(step == 0)
    def _():
        for ref, at, size in zip(pieces, starts, sizes):
            both_ref[at : at + size] = ref[...].reshape(size, ref.shape[2])

    @pl.when(step < blocks)
    def _():
        up, bias = up_ref[...], bias_ref[...]
        total = 0.0
        later = dot(pieces[0][...].reshape(sizes[0], -1), up)
        for n, (start, size) in enumerate(zip(starts, sizes)):
            at = slice(start, start + size)
            v = later + bias
            if n + 1 < len(pieces):
                later = dot(pieces[n + 1][...].reshape(sizes[n + 1], -1), up)
            square = v * v
            tanh = jnp.tanh(v * (GELU_A + GELU_B * square))
            gate = 0.5 + 0.5 * tanh
            act = v * gate
            slope = gate + act * ((1.0 - tanh) * (GELU_A + 3.0 * GELU_B * square))
            grad = (slope * g_ref[at].astype(F32)).astype(BF16)
            act_ref[at] = act.astype(BF16)
            grad_ref[at] = grad
            held[step, at] = grad
            total = total + jnp.sum(grad.astype(F32), axis=0, keepdims=True)
        sum_ref[...] = total

    @pl.when(step >= blocks)
    def _():
        grad = jnp.concatenate([held[n] for n in range(blocks)], axis=1)
        part_ref[...] = dot(grad, row_ref[...], 1, 1).astype(BF16)


def hidden_units(pieces, grads, up, bias):
    model = pieces[0].shape[2]
    tokens, half = grads.shape
    blocks, more = half // BLOCK, model // BLOCK

    def first(g):
        return jnp.minimum(g, blocks - 1)

    def second(g):
        return jnp.maximum(g - blocks, 0)

    column, line = pl.BlockSpec((tokens, BLOCK), lambda g: (0, first(g))), pl.BlockSpec((1, BLOCK), lambda g: (0, first(g)))
    return call(
        functools.partial(hidden_body, blocks), "hidden", (), (blocks + more,),
        [(piece, fixed(piece.shape)) for piece in pieces]
        + [
            (grads, column),
            (up, pl.BlockSpec((model, BLOCK), lambda g: (0, first(g)))),
            (up, pl.BlockSpec((BLOCK, half), lambda g: (second(g), 0))),
            (bias, line),
        ],
        [
            (grads.shape, BF16, column),
            (grads.shape, BF16, column),
            ((1, half), F32, line),
            ((tokens, model), BF16, fixed((tokens, model))),
            ((tokens, model), BF16, pl.BlockSpec((tokens, BLOCK), lambda g: (0, second(g)))),
        ],
        [pltpu.VMEM((blocks, tokens, BLOCK), BF16)]
    )


def sent_body(half_ref, both_ref, cot_ref, out_ref, keep_ref, act_ref, up_out, up_keep, down_out):
    both = both_ref[...]
    down_out[...] = dot(act_ref[...], cot_ref[...], 0, 0).astype(BF16)
    up_out[...] = dot(both, out_ref[...], 0, 0).astype(BF16)
    up_keep[...] = dot(both, keep_ref[...], 0, 0).astype(BF16)


def sent_grads(kept, both, cot, grad, act):
    tokens, model = both.shape
    half = grad.shape[1] // 2
    steps = half // BLOCK
    column = along((model, BLOCK), 1)
    return call(
        sent_body, "sent_grads", (kept,), (steps,),
        [
            (both, fixed(both.shape)),
            (cot, fixed(cot.shape)),
            (grad, pl.BlockSpec((tokens, BLOCK), lambda g, k: (0, (1 - k[0]) * steps + g))),
            (grad, pl.BlockSpec((tokens, BLOCK), lambda g, k: (0, k[0] * steps + g))),
            (act, along((tokens, BLOCK), 1)),
        ],
        [((model, half), BF16, column), ((model, half), BF16, column), ((half, model), BF16, along((BLOCK, model)))],
    )


def kept_body(order_ref, act_ref, half_ref, cot_ref, down_ref, att_ref, low_ref, kept_ref, feed_ref, out_ref, keep_ref):
    parts = order_ref.shape[0]
    width = att_ref.shape[1] // parts
    kept_ref[...] = dot(half_ref[...], cot_ref[...], 0, 0).astype(BF16)
    feed_ref[...] = dot(act_ref[...], down_ref[...]).astype(BF16)
    grad = dot(att_ref[...], low_ref[...], 0, 0).astype(BF16)
    step, steps = pl.program_id(0), pl.num_programs(0)

    def write(ref):
        for n in range(parts):
            at = pl.multiple_of(order_ref[n] * width, width)
            ref[pl.ds(at, width)] = grad[n * width : (n + 1) * width]

    @pl.when(2 * step < steps)
    def _():
        write(out_ref)

    @pl.when(2 * step >= steps)
    def _():
        write(keep_ref)


def kept_grads(order, act, cot, down, attended, low, c_at, deps=()):
    tokens, half = act.shape
    model = cot.shape[1]
    steps = model // BLOCK
    rows = half // (2 * steps)
    own = attended.shape[0]
    place = jnp.concatenate([order, c_at.astype(jnp.int32)[None]])

    def body(place_ref, *refs):
        kept_body(place_ref.at[0 : order.shape[0]], *refs)

    def low_at(g, p):
        c = p[order.shape[0]]
        mine = 2 * g >= steps
        return 0, jnp.where(mine, c * (steps // 2) + g - steps // 2, (1 - c) * (steps // 2) + g)

    return call(
        body, "kept_grads", (place,), (steps,),
        [
            (act, fixed(act.shape)),
            (act, along((tokens, rows), 1, steps)),
            (cot, fixed(cot.shape)),
            (down, along((half, BLOCK), 1)),
            (attended, fixed(attended.shape)),
            (low, pl.BlockSpec((own, BLOCK), low_at)),
        ],
        [
            ((half // 2, model), BF16, along((rows, model))),
            ((tokens, model), BF16, along((tokens, BLOCK), 1)),
            ((model, model // 2), BF16, pl.BlockSpec((model, BLOCK), lambda g, p: (0, jnp.minimum(g, steps // 2 - 1)))),
            ((model, model // 2), BF16, pl.BlockSpec((model, BLOCK), lambda g, p: (0, jnp.maximum(g - steps // 2, 0)))),
        ],
        deps=deps,
    )


def middle_back_body(
    order_ref, part_ref, sent_ref, mid_ref, cot_ref, gain_ref, w0, w1, w2, w3,
    grad_ref, low_ref, att0_ref, att1_ref, far_ref, sums_ref,
):
    grad = part_ref[...].astype(F32) + sent_ref[...].astype(F32)
    hat, inverse = centre(mid_ref[0])
    cot = cot_ref[0].astype(F32)
    total = cot + norm_back(grad, gain_ref[...], hat, inverse)
    low = total.astype(BF16)
    grad_ref[0] = total
    low_ref[0] = low
    far_ref[0, 0] = dot(low, w2[...], 1, 1).astype(BF16)
    far_ref[1, 0] = dot(low, w3[...], 1, 1).astype(BF16)
    att1_ref[0] = dot(low, w1[...], 1, 1).astype(BF16)
    att0_ref[0] = dot(low, w0[...], 1, 1).astype(BF16)

    @pl.when(pl.program_id(0) == 0)
    def _():
        sums_ref[...] = jnp.zeros_like(sums_ref)

    sums_ref[0:1] += jnp.sum(grad * hat, axis=0, keepdims=True)
    sums_ref[1:2] += jnp.sum(grad, axis=0, keepdims=True)
    sums_ref[2:3] += jnp.sum(low.astype(F32), axis=0, keepdims=True)
    sums_ref[3:4] += jnp.sum(cot, axis=0, keepdims=True)


def middle_back(order, both, sent, mid, cot, gain, weight, parts, deps=()):
    rows, shard, model = mid.shape
    width = model // parts
    block, one = along((1, shard, model)), along((1, shard, width))
    flat = pl.BlockSpec((shard, model), lambda g, o: (g, 0))
    return call(
        middle_back_body, "middle_back", (order,), (rows,),
        [(both, flat), (sent, flat), (mid, block), (cot, block), (gain, fixed((1, model)))] + out_blocks(weight, parts),
        [
            (mid.shape, F32, block),
            (mid.shape, BF16, block),
            ((rows, shard, width), BF16, one),
            ((rows, shard, width), BF16, one),
            ((2, rows, shard, width), BF16, along((2, 1, shard, width), 1)),
            ((8, model), F32, fixed((8, model))),
        ],
        deps=deps
    )


def norm1_back_body(part_ref, near_ref, far_ref, stream_ref, mid_ref, gain_ref, seg_ref, in_ref, shift_ref, sums_ref):
    grad = part_ref[0].astype(F32) + near_ref[0].astype(F32) + far_ref[0].astype(F32)
    hat, inverse = centre(stream_ref[0])
    total = mid_ref[0] + norm_back(grad, gain_ref[...], hat, inverse)
    in_ref[0] = total.astype(BF16)
    slots = lax.broadcasted_iota(jnp.int32, (SEGS, seg_ref.shape[-1]), 0) == seg_ref[0]
    onehot = slots.astype(F32).astype(BF16)
    shift_ref[0] = dot(jnp.concatenate([onehot, onehot], axis=1), split_low(total))

    @pl.when(pl.program_id(0) == 0)
    def _():
        sums_ref[...] = jnp.zeros_like(sums_ref)

    sums_ref[0:1] += jnp.sum(grad * hat, axis=0, keepdims=True)
    sums_ref[1:2] += jnp.sum(grad, axis=0, keepdims=True)


def norm1_back(start, count, own, near, far, stream, mid, gain, seg, held=(), deps=()):
    rows, shard, model = stream.shape
    block, own_block = along((1, shard, model), 0, start), along((1, shard, model))
    return call(
        norm1_back_body, "norm1_back", (), (count,),
        [(own, own_block), (near, own_block), (far, own_block), (stream, block), (mid, block), (gain, fixed((1, model)))]
        + [(seg, along((1, 1, shard), 0, start))],
        [
            (stream.shape, BF16, block),
            ((count, SEGS, model), F32, along((1, SEGS, model))),
            ((8, model), F32, fixed((8, model))),
        ],
        held=[(array, 0) for array in held], deps=deps
    )


def exchange(own, one, far):
    return [own, swap(one, "c"), far, swap(far[1], "c")]


def tie(*values):
    return lax.optimization_barrier(values)


def cut(values, index, size, axis):
    return lax.dynamic_slice_in_dim(values, index * size, size, axis)


def add_low(kept, sent):
    return (kept.astype(F32) + sent.astype(F32)).astype(BF16)


def over_z(values, at, depth):
    if depth != 4:
        return lax.psum_scatter(values, "z", scatter_dimension=0, tiled=False)
    parts = [lax.dynamic_index_in_dim(values, at ^ n, 0, keepdims=False) for n in range(depth)]
    own = parts[0].astype(F32)
    sent = [lax.ppermute(parts[n], "z", [(i, i ^ n) for i in range(depth)]) for n in range(1, depth)]
    return (own + sent[0].astype(F32) + sent[1].astype(F32) + sent[2].astype(F32)).astype(BF16)


def ordered(at, own, other, axis):
    return jnp.where(at == 0, jnp.concatenate([own, other], axis), jnp.concatenate([other, own], axis))


def finish_body(blocks, at_ref, d0, d1, u0, u1, l0, l1, down_ref, up_ref, qkv_ref, out_ref):
    c_at = at_ref[0]
    width = u0.shape[1] // (2 * blocks)
    depth = d0.shape[0]
    for c in range(2):
        mine = c_at == c
        down_ref[c * depth : (c + 1) * depth] = jnp.where(mine, d0[...], d1[...]).astype(F32)
        up = jnp.where(mine, u0[...], u1[...]).astype(F32)
        for x in range(2):
            for z in range(blocks):
                at, place = ((2 * z + x) * 2 + c) * width, (x * blocks + z) * width
                up_ref[:, at : at + width] = up[:, place : place + width]
        late = jnp.where(mine, l0[...], l1[...]).astype(F32)
        half = out_ref.shape[1] // 2
        size = half // 2
        out_ref[:, c * half : (c + 1) * half] = late[:, 6 * size :]
        for y in range(2):
            for n in range(3):
                at = n * 4 * size + (2 * y + c) * size
                qkv_ref[:, at : at + size] = late[:, (3 * y + n) * size : (3 * y + n + 1) * size]


def finish(c_at, dp, piece, down, up, late, parts):
    rows, model = up[0].shape[0], down[0].shape[1]
    depth = dp // 2
    if piece % 128 == 0:
        at = c_at.astype(jnp.int32)[None]
        shapes = [(2 * down[0].shape[0], model), (rows, 2 * up[0].shape[1]), (rows, 3 * model), (rows, model)]
        arrays = list(down) + list(up) + list(late)
        return call(
            functools.partial(finish_body, depth), "finish", (at,), (1,),
            [(array, fixed(array.shape)) for array in arrays], [(shape, F32, fixed(shape)) for shape in shapes],
        )
    down_done = ordered(c_at, *down, 0).astype(F32)
    up_done = ordered(c_at, up[0][None], up[1][None], 0).reshape(2, rows, 2, depth, piece)
    up_done = up_done.transpose(1, 3, 2, 0, 4).reshape(rows, -1).astype(F32)
    both = ordered(c_at, late[0][None], late[1][None], 0)
    width = model // parts
    qkv_done = both[:, :, : 6 * width].reshape(2, rows, 2, 3, width).transpose(1, 3, 2, 0, 4)
    qkv_done = qkv_done.reshape(rows, 3 * model).astype(F32)
    out_done = jnp.concatenate([both[0, :, 6 * width :], both[1, :, 6 * width :]], axis=1).astype(F32)
    return down_done, up_done, qkv_done, out_done


def local(
    inputs, segment_ids, doc_times, time_weight, time_bias, norm1_gain, norm1_bias, qkv_weight, qkv_bias,
    out_weight, out_bias, norm2_gain, norm2_bias, up_weight, up_bias, down_weight, down_bias, cotangent,
    *, dp,
):
    rows, shard, model = inputs.shape
    parts = 4
    tokens = rows * shard
    hidden_width = up_weight.shape[1]
    width = model // parts
    depth = dp // 2
    half = hidden_width // 2
    piece = half // dp
    z_at, x_at, y_at, c_at = (lax.axis_index(name) for name in ("z", "x", "y", "c"))
    me = 2 * y_at + c_at

    def line(vector):
        return vector.astype(F32)[None]

    seg_two = swap(segment_ids, "y")
    segs = jnp.stack([segment_ids, swap(segment_ids, "c"), seg_two, swap(seg_two, "c")], axis=1)

    groups = [(0, rows - 1), (rows - 1, 1)] if rows > 1 else [(0, 1)]
    seg = segment_ids[:, None, :]
    features = time_features(doc_times.reshape(rows * SEGS), jnp.arange(TEMB), TEMB // 2)
    time_shift = dot(features, time_weight).reshape(rows, SEGS, model) + time_bias.astype(F32)
    stream, own1 = norm1(inputs, seg, time_shift, line(norm1_gain), line(norm1_bias))
    own1, segs = tie(own1, segs)
    two1 = swap(own1, "y")
    one1 = swap(own1, "c")

    me, x_at, z_at, c_at, y_at, own1 = tie(me, x_at, z_at, c_at, y_at, own1)
    order = [me ^ i for i in range(parts)]
    order_list = jnp.stack(order).astype(jnp.int32)
    me_list = order_list[:1]
    low_id, high_id = segs.min(axis=2), segs.max(axis=2)
    act = (low_id[:, :, None] <= high_id[:, None, :]) & (low_id[:, None, :] <= high_id[:, :, None])
    places = jnp.arange(parts, dtype=jnp.int32)
    rank = jnp.cumsum(act.astype(jnp.int32), axis=2) - 1
    chosen = act[..., None] & (rank[..., None] == places)
    idx = jnp.sum(jnp.where(chosen, places[:, None], 0), axis=2).astype(jnp.int32).reshape(-1)
    cnt = jnp.sum(act.astype(jnp.int32), axis=2).reshape(-1)
    positions = jnp.stack([o * shard + jnp.arange(shard, dtype=jnp.int32) for o in order])
    cos_tab, sin_tab = rotary_tables(positions, HEAD_DIM)

    cot = cotangent.reshape(tokens, model)
    cot_other = swap(cot, "c")
    turned = jnp.stack([1 - x_at, x_at])
    if piece % BLOCK == 0:
        blk = ((jnp.arange(depth)[None, :] * 2 + turned[:, None]) * 2 + c_at) * (piece // BLOCK)
        blk = (blk[..., None] + jnp.arange(piece // BLOCK)).reshape(-1).astype(jnp.int32)
        up_from, down_from = up_weight, down_weight
    else:
        blk = jnp.zeros((half // BLOCK,), jnp.int32)
        up_from = up_weight.reshape(model, depth, 2, 2, piece)
        up_from = lax.dynamic_index_in_dim(up_from, c_at, 3, keepdims=False)
        up_from = jnp.where(x_at == 1, up_from, up_from[:, :, ::-1]).transpose(0, 2, 1, 3).reshape(model, half)
        down_from = down_weight.reshape(depth, 2, 2, piece, model)
        down_from = lax.dynamic_index_in_dim(down_from, c_at, 2, keepdims=False)
        down_from = jnp.where(x_at == 1, down_from, down_from[:, ::-1]).transpose(1, 0, 2, 3).reshape(half, model)
    grad_act, up_own, down_own, cot_both = cot_down(
        blk, cot, cot_other, up_from, down_from, piece % BLOCK != 0, half
    )
    up_bias_own = lax.dynamic_index_in_dim(up_bias.reshape(depth, 2, 2, piece), c_at, 2, keepdims=False)
    up_bias_own = jnp.where(x_at == 1, up_bias_own, up_bias_own[:, ::-1]).transpose(1, 0, 2).reshape(half)

    bias_line = qkv_bias.reshape(1, 3 * model)
    qkv, normed1_all, qkv_own = project_qkv(
        0, parts, me_list, own1, one1, qkv_weight, bias_line, cos_tab, sin_tab, (), (grad_act,)
    )
    two1, qkv = tie(two1, qkv)
    qkv, normed1_all, _ = project_qkv(
        1, parts, me_list, two1, swap(two1, "c"), qkv_weight, bias_line, cos_tab, sin_tab, (qkv, normed1_all)
    )
    o, lse, attended = None, None, []
    for start, count in groups:
        held = () if o is None else (o, lse)
        o, out_one, out_far, lse = attend(start, count, cnt, idx, qkv, segs, held)
        attended.append((out_one, swap(out_far, "y")))
    held, normed2, normed2_other = (), [], []
    for (start, count), values in zip(groups, attended):
        far, o = tie(values[1], o)
        values = exchange(o, values[0], far)
        middle, low, attended_all = middle_norm(
            start, count, order_list, values, out_weight, stream, line(out_bias), line(norm2_gain), line(norm2_bias), held
        )
        held = (middle, attended_all)
        normed2.append(low)
        normed2_other.append(swap(low, "c"))

    active, grad_hidden, up_b, normed2_both, part2 = hidden_units(
        normed2 + normed2_other, grad_act, up_own, line(up_bias_own)
    )
    part2_sent = swap(part2[tokens:], "c")
    grad_middle, grad_middle_low, att0, att1, far, sums2 = middle_back(
        order_list, part2, part2_sent, middle, cotangent, line(norm2_gain), out_weight, parts
    )
    far = swap(far, "y")
    sums2 = sums2[:4]

    active, grad_hidden, att0 = tie(active, grad_hidden, att0)
    up_half = (x_at == y_at).astype(jnp.int32)
    up_out, up_grad, down_out = sent_grads(up_half[None], normed2_both, cot_both, grad_hidden, active)
    up_sent, down_sent = swap(up_out, "y"), swap(down_out, "x")
    down_kept, feed, out_sent, out_grad = kept_grads(
        order_list, active, cot_both, down_own, attended_all.reshape(tokens, model),
        grad_middle_low.reshape(tokens, model), c_at, (down_out, far),
    )
    out_sent = swap(out_sent, "c")
    feed = feed[:tokens].astype(F32) + swap(feed[tokens:], "c").astype(F32) + line(down_bias)
    output = (middle + feed.reshape(rows, shard, model)).astype(BF16)

    up_rows = model // dp
    down_kept, output, out_grad, far = tie(down_kept, output, out_grad, far)
    grad_o = exchange(att0, att1, far)
    grad_qkv, back = (), []
    for start, count in groups:
        grad_qkv, own, one, two, three = attend_back(
            start, count, cnt, idx, qkv, o, grad_o, lse, segs, cos_tab, sin_tab, qkv_own, grad_qkv,
            (there, down_x, up_out) if back else (),
        )
        grad_qkv = (grad_qkv,)
        if not back:
            own, up_grad, down_kept, out_grad = tie(own, up_grad, down_kept, out_grad)
            down_x = add_low(down_kept, down_sent)
            down_z = lax.psum_scatter(down_x, "z", scatter_dimension=0, tiled=True)
            up_y = add_low(up_grad, up_sent).reshape(depth, 2 * up_rows, half // 2)
            up_out = cut(up_y, 1 - x_at, up_rows, 1)
            up_sent = swap(up_out, "x")
        there = add_low(two, swap(three, "c"))
        if not back:
            there, up_out = tie(there, up_out)
        back.append((own, swap(one, "c"), swap(there, "y")))
    out_c = add_low(out_grad, out_sent)
    out_c = out_c.reshape(depth, 2 * up_rows, model // 2)
    out_x = add_low(cut(out_c, x_at, up_rows, 1), swap(cut(out_c, 1 - x_at, up_rows, 1), "x"))
    grad_qkv, there, far = tie(grad_qkv[0], there, back[0][2])
    back[0] = back[0][:2] + (far,)
    back[-1] = back[-1][:2] + (swap(there, "y"),)
    grad_qkv = grad_qkv.reshape(parts * tokens, 3 * width)
    qkv_grad = dot(normed1_all.reshape(parts * tokens, model), grad_qkv, 0, 0).astype(BF16)
    qkv_b = jnp.sum(grad_qkv.astype(F32), axis=0)
    qkv_grad, up_y = tie(qkv_grad.reshape(depth, 2 * up_rows, 3 * width), up_y)
    qkv_sent = swap(cut(qkv_grad, 1 - x_at, up_rows, 1), "x")
    held, grad_shift, sums1 = (), [], 0.0
    deps = (qkv_grad,)
    for (start, count), values in zip(groups, back):
        input_grad, found, sums = norm1_back(
            start, count, *values, stream, grad_middle, line(norm1_gain), seg, held, deps
        )
        if not held:
            input_grad, up_y = tie(input_grad, up_y)
            up_x = add_low(cut(up_y, x_at, up_rows, 1), up_sent)
            up_z = lax.psum_scatter(up_x, "z", scatter_dimension=0, tiled=False)
            deps = (up_x,)
        held = (input_grad,)
        grad_shift.append(found.reshape(count * SEGS, model))
        sums1 = sums1 + sums[:2]
    qkv_x = add_low(cut(qkv_grad, x_at, up_rows, 1), qkv_sent)

    up_b = up_b.reshape(2, depth, 1, piece)
    up_b = jnp.where(x_at == 1, up_b, up_b[::-1]).transpose(1, 0, 2, 3)
    up_b = jnp.where(jnp.arange(2)[:, None] == c_at, up_b, 0.0).reshape(-1, model)
    qkv_b = jnp.where(jnp.arange(parts)[:, None] == me, qkv_b.reshape(3, 1, width), 0.0).reshape(3, model)
    times = doc_times.reshape(1, rows * SEGS)
    times = jnp.concatenate([times // 32, times % 32], axis=1).astype(F32)
    times = jnp.pad(times, ((0, 0), (0, model - times.shape[1])))
    small = jnp.concatenate(grad_shift + [sums1, sums2, qkv_b, up_b, times], axis=0)
    small, qkv_x, out_x = tie(add_low(small, swap(small.astype(BF16), "c")), qkv_x, out_x)
    late = jnp.concatenate([qkv_x, out_x], axis=2)
    small = add_low(small, swap(small, "y"))
    small = ordered(x_at, small[None], swap(small, "x")[None], 0)
    if depth == 4:
        others = [lax.ppermute(small, "z", [(i, i ^ n) for i in range(depth)]) for n in range(1, depth)]
        small = jnp.stack([small] + others)
        small = jnp.stack([lax.dynamic_index_in_dim(small, z_at ^ n, 0, keepdims=False) for n in range(depth)])
    else:
        small = lax.all_gather(small, "z")
    small = small.reshape(dp, small.shape[2], model)

    small, down_z, up_z = tie(small, down_z, up_z)
    late = over_z(late, z_at, depth)
    late_sent = swap(late, "y")
    qkv_y = ordered(y_at, late[None, :, : 3 * width], late_sent[None, :, : 3 * width], 0)
    out_y = add_low(late[:, 3 * width :], late_sent[:, 3 * width :])
    late = jnp.concatenate([qkv_y[0], qkv_y[1], out_y], axis=1)
    late_other = swap(late, "c")
    down_y = add_low(down_z, swap(down_z, "y"))
    down_other = swap(down_y, "c")
    up_done = ordered(y_at, up_z, swap(up_z, "y"), 1)
    up_other = swap(up_done, "c")

    down_done, up_done, qkv_done, out_done = finish(
        c_at, dp, piece, (down_y, down_other), (up_done, up_other), (late, late_other), parts
    )

    all_times = small[:, -1, : 2 * rows * SEGS].astype(F32) * 0.25
    all_times = all_times[:, : rows * SEGS] * 32.0 + all_times[:, rows * SEGS :]
    shifts = small[:, : rows * SEGS].reshape(dp * rows * SEGS, model)
    columns = (2 * z_at + x_at) * (TEMB // dp) + jnp.arange(TEMB // dp)
    wanted = time_features(all_times.reshape(-1), columns, TEMB // 2)
    time_w_done = dot(wanted, shifts, 0, 0)
    sums = jnp.sum(small[:, rows * SEGS :].astype(F32), axis=0)
    dp_at = 2 * z_at + x_at

    def share(vector):
        return cut(vector.reshape(-1), dp_at, vector.size // dp, 0)

    time_b_done = jnp.sum(cut(shifts, dp_at, up_rows, 1).astype(F32), axis=0)
    return (
        output, input_grad, time_w_done, time_b_done, share(sums[0]), share(sums[1]), qkv_done, share(sums[6:9]),
        out_done, share(sums[4]), share(sums[2]), share(sums[3]), up_done, share(sums[9:-1]), down_done, share(sums[5]),
    )


def solution(mesh):
    dp, seq = mesh.shape["dp"], mesh.shape["seq"]
    fine = Mesh(mesh.devices.reshape(dp // 2, 2, seq // 2, 2), ("z", "x", "y", "c"))
    rows, seqs = ("z", "x"), ("y", "c")
    placed = (P(rows, seqs, None), P(rows, seqs), P(rows, None)) + (P(),) * 14 + (P(rows, seqs, None),)
    vec, mat = P(rows), P(rows, None)
    return jax.shard_map(
        functools.partial(local, dp=dp),
        mesh=fine,
        in_specs=placed,
        out_specs=(
            P(rows, seqs, None), P(rows, seqs, None), mat, vec, vec, vec, mat, vec, mat, vec, vec, vec, mat, vec, mat, vec,
        ),
        check_vma=False,
    )
```

profile of v0, /device:TPU:0, one launch (start us, length us, event | category | flops | bytes accessed | tf_op | source)
XLA Modules:
  0.0 450.3 jit_solution(9319980022148055324)
XLA Ops:
  17.1 4.6 %norm1.1 = (f32[3,256,1024]{2,1,0:T(8,128)}, bf16[3,256,1024]{2,1,0:T(8,128)(2,1)}) custom-call(bf16[3,256,1024]{2,1,0:T(8,128)(2,1)} %refs_0_.1, s32[3,1,256]{2,1,0:T(1,128)} %broadcast_in_dim.151.refs_1_.refs_6_, f32[3,8,1024]{2,1,0:T(8,128)} %fusion.refs_2_, f32[1,1024]{1,0:T(1,128)} %bitcast.130, f32[1,1024]{1,0:T(1,128)} %bitcast.145), custom_call_target="tpu_custom_call" | custom-call | tf_op jit(solution)/shard_map/norm1/pallas_call | solution.py:94
  31.8 15.7 %cot_down.1 = (bf16[1536,2048]{1,0:T(8,128)(2,1)}, bf16[1024,2048]{1,0:T(8,128)(2,1)}, bf16[2048,1024]{1,0:T(8,128)(2,1)}, bf16[1536,1024]{1,0:T(8,128)(2,1)}) custom-call(s32[8]{0:T(128)} %add.295.refs_0_, bf16[768,1024]{1,0:T(8,128)(2,1)} %bitcast.108, bf16[768,1024]{1,0:T(8,128)(2,1)} %copy-done.14, bf16[1024,4096]{1,0:T(8,128)(2,1)} %refs_3_.3, ...), custom_call_target="tpu_custom_call" | custom-call | tf_op jit(solution)/shard_map/cot_down/pallas_call | solution.py:94
  47.6 9.5 %qkv.2 = (bf16[3,4,3,256,256]{4,3,2,1,0:T(8,128)(2,1)}, bf16[4,3,256,1024]{3,2,1,0:T(8,128)(2,1)}, bf16[768,1024]{1,0:T(8,128)(2,1)}) custom-call(s32[1]{0:T(128)} %bitcast.4.refs_0_, bf16[3,256,1024]{2,1,0:T(8,128)(2,1)} %get-tuple-element.124.refs_1_, bf16[3,256,1024]{2,1,0:T(8,128)(2,1)} %collective-permute-done.4.refs_2_, bf16[1024,3072]{1,0:T(8,128)(2,1)} %refs_3_.5, ...), custom_call_target="tpu_custom_call" | custom-call | tf_op jit(solution)/shard_map/qkv/pallas_call | solution.py:94
  64.6 9.5 %qkv.3 = (bf16[3,4,3,256,256]{4,3,2,1,0:T(8,128)(2,1)}, bf16[4,3,256,1024]{3,2,1,0:T(8,128)(2,1)}, bf16[768,1024]{1,0:T(8,128)(2,1)}) custom-call(s32[1]{0:T(128)} %bitcast.4.refs_0_, bf16[3,256,1024]{2,1,0:T(8,128)(2,1)} %collective-permute-done.3.refs_1_, bf16[3,256,1024]{2,1,0:T(8,128)(2,1)} %copy-done.15, ...), custom_call_target="tpu_custom_call", output_to_operand_aliasing={{0}: (7, {}), {1}: (8, {})} | custom-call | tf_op jit(solution)/shard_map/qkv/pallas_call | solution.py:94
  74.0 13.8 %attend.2 = (bf16[4,3,256,256]{3,2,1,0:T(8,128)(2,1)}, bf16[2,256,256]{2,1,0:T(8,128)(2,1)}, bf16[2,2,256,256]{3,2,1,0:T(8,128)(2,1)}, f32[3,4,8,256]{3,2,1,0:T(8,128)}) custom-call(s32[12]{0:T(128)} %reshape.402.refs_0_, s32[48]{0:T(128)} %reshape.403.refs_1_, bf16[3,4,3,256,256]{4,3,2,1,0:T(8,128)(2,1)} %get-tuple-element.131.refs_2_, s32[3,4,256]{2,1,0:T(4,128)} %copy-done.30), custom_call_target="tpu_custom_call" | custom-call | tf_op jit(solution)/shard_map/attend/pallas_call | solution.py:94
  89.6 10.6 %attend.3 = (bf16[4,3,256,256]{3,2,1,0:T(8,128)(2,1)}, bf16[1,256,256]{2,1,0:T(8,128)(2,1)}, bf16[2,1,256,256]{3,2,1,0:T(8,128)(2,1)}, f32[3,4,8,256]{3,2,1,0:T(8,128)}) custom-call(s32[12]{0:T(128)} %reshape.402.refs_0_, s32[48]{0:T(128)} %reshape.403.refs_1_, ...), custom_call_target="tpu_custom_call", output_to_operand_aliasing={{0}: (4, {}), {3}: (5, {})} | custom-call | tf_op jit(solution)/shard_map/attend/pallas_call | solution.py:94
  107.1 6.1 %middle.2 = (f32[3,256,1024]{2,1,0:T(8,128)}, bf16[2,256,1024]{2,1,0:T(8,128)(2,1)}, bf16[3,256,1024]{2,1,0:T(8,128)(2,1)}) custom-call(s32[4]{0:T(128)} %pad_add_fusion.1.refs_0_, bf16[4,3,256,256]{3,2,1,0:T(8,128)(2,1)} %get-tuple-element.142.refs_1_.refs_3_, bf16[2,256,256]{2,1,0:T(8,128)(2,1)} %copy-done.31, bf16[2,2,256,256]{3,2,1,0:T(8,128)(2,1)} %copy-done.19, ...), custom_call_target="tpu_custom_call" | custom-call | tf_op jit(solution)/shard_map/middle/pallas_call | solution.py:94
  116.9 4.9 %middle.3 = (f32[3,256,1024]{2,1,0:T(8,128)}, bf16[1,256,1024]{2,1,0:T(8,128)(2,1)}, bf16[3,256,1024]{2,1,0:T(8,128)(2,1)}) custom-call(s32[4]{0:T(128)} %pad_add_fusion.1.refs_0_, bf16[4,3,256,256]{3,2,1,0:T(8,128)(2,1)} %get-tuple-element.142.refs_1_.refs_3_, bf16[1,256,256]{2,1,0:T(8,128)(2,1)} %copy-done.33, ...), custom_call_target="tpu_custom_call", output_to_operand_aliasing={{0}: (13, {}), {2}: (14, {})} | custom-call | tf_op jit(solution)/shard_map/middle/pallas_call | solution.py:94
  125.1 28.5 %hidden.1 = (bf16[1536,2048]{1,0:T(8,128)(2,1)}, bf16[1536,2048]{1,0:T(8,128)(2,1)}, f32[1,2048]{1,0:T(1,128)}, bf16[1536,1024]{1,0:T(8,128)(2,1)}, bf16[1536,1024]{1,0:T(8,128)(2,1)}) custom-call(bf16[2,256,1024]{2,1,0:T(8,128)(2,1)} %get-tuple-element.140.refs_0_, bf16[1,256,1024]{2,1,0:T(8,128)(2,1)} %get-tuple-element.147.refs_1_, ...), custom_call_target="tpu_custom_call" | custom-call | tf_op jit(solution)/shard_map/hidden/pallas_call | solution.py:94
  159.7 9.8 %middle_back.1 = (f32[3,256,1024]{2,1,0:T(8,128)}, bf16[3,256,1024]{2,1,0:T(8,128)(2,1)}, bf16[3,256,256]{2,1,0:T(8,128)(2,1)}, bf16[3,256,256]{2,1,0:T(8,128)(2...) custom-call(s32[4]{0:T(128)} %pad_add_fusion.1.refs_0_, bf16[1536,1024]{1,0:T(8,128)(2,1)} %get-tuple-element.151.refs_1_, ...), custom_call_target="tpu_custom_call" | custom-call | tf_op jit(solution)/shard_map/middle_back/pallas_call | solution.py:94
  170.4 15.6 %sent_grads.1 = (bf16[1024,1024]{1,0:T(8,128)(2,1)}, bf16[1024,1024]{1,0:T(8,128)(2,1)}, bf16[1024,1024]{1,0:T(8,128)(2,1)}) custom-call(s32[1]{0:T(128)} %bitcast.20.refs_0_, bf16[1536,1024]{1,0:T(8,128)(2,1)} %get-tuple-element.160.refs_1_, bf16[1536,1024]{1,0:T(8,128)(2,1)} %get-tuple-element.155.refs_2_.refs_3_, ...), custom_call_target="tpu_custom_call" | custom-call | tf_op jit(solution)/shard_map/sent_grads/pallas_call | solution.py:94
  190.3 20.2 %kept_grads.1 = (bf16[1024,1024]{1,0:T(8,128)(2,1)}, bf16[1536,1024]{1,0:T(8,128)(2,1)}, bf16[1024,512]{1,0:T(8,128)(2,1)}, bf16[1024,512]{1,0:T(8,128)(2,1)}) custom-call(s32[5]{0:T(128)} %concatenate.78.refs_0_, bf16[1536,2048]{1,0:T(8,128)(2,1)} %get-tuple-element.154.refs_5_.refs_1_.refs_2_, ...), custom_call_target="tpu_custom_call" | custom-call | tf_op jit(solution)/shard_map/kept_grads/pallas_call | solution.py:94
  222.7 26.7 %attend_back.2 = (bf16[4,3,256,768]{3,2,1,0:T(8,128)(2,1)}, bf16[2,256,1024]{2,1,0:T(8,128)(2,1)}, bf16[2,256,1024]{2,1,0:T(8,128)(2,1)}, bf16[2,256,1024]{2,1,0:T(8,128)(2,1)}, bf16[2,256,1024]{2,1,0:T(8,128)(2,1)}) custom-call(s32[12]{0:T(128)} %reshape.402.refs_0_, s32[48]{0:T(128)} %reshape.403.refs_1_, ...), custom_call_target="tpu_custom_call" | custom-call | tf_op jit(solution)/shard_map/attend_back/pallas_call | solution.py:94
  251.5 9.1 %collective-permute-done.21 = bf16[1024,1024]{1,0:T(8,128)(2,1)} collective-permute-done((bf16[1024,1024]{1,0:T(8,128)(2,1)}, bf16[1024,1024]{1,0:T(8,128)(2,1)}, u32[]{:S(2)}, u32[]{:S(2)}) %collective-permute-start.21) | collective-permute-done | bytes 2097184 | tf_op jit(solution)/shard_map/ppermute | solution.py:27
  272.3 20.2 %attend_back.3 = (bf16[4,3,256,768]{3,2,1,0:T(8,128)(2,1)}, bf16[1,256,1024]{2,1,0:T(8,128)(2,1)}, bf16[1,256,1024]{2,1,0:T(8,128)(2,1)}, bf16[1,256,1024]{2,1,0:T(8,128)(2,1)}, bf16[1,256,1024]{2,1,0:T(8,128)(2,1)}) custom-call(s32[12]{0:T(128)} %reshape.402.refs_0_, s32[48]{0:T(128)} %reshape.403.refs_1_, ...), custom_call_target="tpu_custom_call", output_to_operand_aliasing={{0}: (13, {})} | custom-call | tf_op jit(solution)/shard_map/attend_back/pallas_call | solution.py:94
  301.5 8.1 %bitcast_convert_fusion = bf16[1024,768]{1,0:T(8,128)(2,1)} fusion(bf16[4,3,256,1024]{3,2,1,0:T(8,128)(2,1)} %get-tuple-element.195, bf16[4,3,256,768]{3,2,1,0:T(8,128)(2,1)S(1)} %copy-done.3), kind=kOutput, calls=%fused_computation.3 | convolution fusion | flops 4832624640 | bytes 12582912 | tf_op jit(solution)/shard_map/dot_general | solution.py:48
  309.7 5.8 %norm1_back.2 = (bf16[3,256,1024]{2,1,0:T(8,128)(2,1)}, f32[2,8,1024]{2,1,0:T(8,128)}, f32[8,1024]{1,0:T(8,128)}) custom-call(bf16[2,256,1024]{2,1,0:T(8,128)(2,1)} %get-tuple-element.192.refs_0_, bf16[2,256,1024]{2,1,0:T(8,128)(2,1)} %collective-permute-done.27.refs_1_, bf16[2,256,1024]{2,1,0:T(8,128)(2,1)} %collective-permute-done.25.refs_2_, ...), custom_call_target="tpu_custom_call" | custom-call | tf_op jit(solution)/shard_map/norm1_back/pallas_call | solution.py:94
  331.7 14.9 %collective-permute-done.30 = bf16[4,128,768]{2,1,0:T(8,128)(2,1)} collective-permute-done((bf16[4,128,768]{2,1,0:T(8,128)(2,1)}, bf16[4,128,768]{2,1,0:T(8,128)(2,1)}, u32[]{:S(2)}, u32[]{:S(2)}) %collective-permute-start.30) | collective-permute-done | bytes 786464 | tf_op jit(solution)/shard_map/ppermute | solution.py:27
  366.0 17.7 %collective-permute-start.42 = (bf16[128,1280]{1,0:T(8,128)(2,1)S(1)}, bf16[128,1280]{1,0:T(8,128)(2,1)S(1)}, u32[]{:S(2)}, u32[]{:S(2)}) collective-permute-start(bf16[128,1280]{1,0:T(8,128)(2,1)S(1)} %get-tuple-element.226), channel_id=1, source_target_pairs={{0,8},{8,0},{16,24},{24,16},{1,9},{9,1},{17,25},{25,17},{2,10},{10... | collective-permute-start | bytes 983048 | tf_op jit(solution)/shard_map/ppermute | solution.py:740
  383.7 4.9 %collective-permute-done.36 = bf16[2,38,1024]{2,1,0:T(8,128)(2,1)S(1)} collective-permute-done((bf16[2,38,1024]{2,1,0:T(8,128)(2,1)S(1)}, bf16[2,38,1024]{2,1,0:T(8,128)(2,1)S(1)}, u32[]{:S(2)}, u32[]{:S(2)}) %collective-permute-start.36) | collective-permute-done | bytes 155680 | tf_op jit(solution)/shard_map/ppermute | solution.py:965
  388.8 13.2 %collective-permute-done.43 = bf16[128,1280]{1,0:T(8,128)(2,1)S(1)} collective-permute-done((bf16[128,1280]{1,0:T(8,128)(2,1)S(1)}, bf16[128,1280]{1,0:T(8,128)(2,1)S(1)}, u32[]{:S(2)}, u32[]{:S(2)}) %collective-permute-start.43) | collective-permute-done | bytes 327712 | tf_op jit(solution)/shard_map/ppermute | solution.py:740
  403.9 7.4 %collective-permute-done.45 = bf16[128,1280]{1,0:T(8,128)(2,1)S(1)} collective-permute-done((bf16[128,1280]{1,0:T(8,128)(2,1)S(1)}, bf16[128,1280]{1,0:T(8,128)(2,1)S(1)}, u32[]{:S(2)}, u32[]{:S(2)}) %collective-permute-start.45) | collective-permute-done | bytes 327712 | tf_op jit(solution)/shard_map/ppermute | solution.py:27
  417.4 14.5 %collective-permute-done.40 = bf16[128,1024]{1,0:T(8,128)(2,1)S(1)} collective-permute-done((bf16[128,1024]{1,0:T(8,128)(2,1)}, bf16[128,1024]{1,0:T(8,128)(2,1)S(1)}, u32[]{:S(2)}, u32[]{:S(2)}) %collective-permute-start.40) | collective-permute-done | bytes 262176 | tf_op jit(solution)/shard_map/ppermute | solution.py:27
  438.4 4.7 %finish.1 = (f32[512,1024]{1,0:T(8,128)}, f32[128,4096]{1,0:T(8,128)}, f32[128,3072]{1,0:T(8,128)}, f32[128,1024]{1,0:T(8,128)}) custom-call(s32[1]{0:T(128)} %bitcast.8.refs_0_, bf16[256,1024]{1,0:T(8,128)(2,1)} %copy-done.11, bf16[256,1024]{1,0:T(8,128)(2,1)} %copy-done.29, bf16[128,2048]{1,0:T(8,128)(2,1)} %copy-done.13, bf16[128,2048]{1,0:T(8,128)(2,1)} %copy-done.28, ...), custom_call_target="tpu_custom_call" | custom-call | tf_op jit(solution)/shard_map/finish/pallas_call | solution.py:94
  (316 shorter events, 138.9 us)
Async XLA Ops:
  7.2 404.4 %reduce-scatter.3.cloned.1.call-start = ((), (), s32[]{:S(2)}) async-start(), calls=%async_computation.2 | async-start | bytes 2621440 | tf_op jit(solution)/shard_map/reduce_scatter | solution.py:917
  10.3 20.4 %collective-permute-start.5 = (bf16[768,1024]{1,0:T(8,128)(2,1)}, bf16[768,1024]{1,0:T(8,128)(2,1)S(1)}, u32[]{:S(2)}, u32[]{:S(2)}) collective-permute-start(bf16[768,1024]{1,0:T(8,128)(2,1)} %bitcast.107), channel_id=1, source_target_pairs={{0,1},{1,0},{2,3},{3,2},{4,5},{5,4},{6,7},{7,6},{8,9},{9,8},{10,11... | collective-permute-start | bytes 4718600 | tf_op jit(solution)/shard_map/ppermute | solution.py:27
  22.4 25.2 %collective-permute-start.4 = (bf16[3,256,1024]{2,1,0:T(8,128)(2,1)}, bf16[3,256,1024]{2,1,0:T(8,128)(2,1)}, u32[]{:S(2)}, u32[]{:S(2)}) collective-permute-start(bf16[3,256,1024]{2,1,0:T(8,128)(2,1)} %get-tuple-element.124.refs_1_), channel_id=1, source_target_pairs={{0,1},{1,0},{2,3},{3,2},{4,5},{5,4},{6,7},{7,6},{8,9},{9,8},{10,11... | collective-permute-start | bytes 4718600 | tf_op jit(solution)/shard_map/ppermute | solution.py:27
  23.0 36.8 %collective-permute-start.3 = (bf16[3,256,1024]{2,1,0:T(8,128)(2,1)}, bf16[3,256,1024]{2,1,0:T(8,128)(2,1)}, u32[]{:S(2)}, u32[]{:S(2)}) collective-permute-start(bf16[3,256,1024]{2,1,0:T(8,128)(2,1)} %get-tuple-element.124.refs_1_), channel_id=1, source_target_pairs={{0,2},{2,0},{1,3},{3,1},{4,6},{6,4},{5,7},{7,5},{8,10},{10,8},{9,1... | collective-permute-start | bytes 4718600 | tf_op jit(solution)/shard_map/ppermute | solution.py:27
  169.5 19.9 %collective-permute-start.16 = (bf16[2,3,256,256]{3,2,1,0:T(8,128)(2,1)}, bf16[2,3,256,256]{3,2,1,0:T(8,128)(2,1)S(1)}, u32[]{:S(2)}, u32[]{:S(2)}) collective-permute-start(bf16[2,3,256,256]{3,2,1,0:T(8,128)(2,1)} %get-tuple-element.163), channel_id=1, source_target_pairs={{0,2},{2,0},{1,3},{3,1},{4,6},{6,4},{5,7},{7,5},{8,10},{10,8},{9,1... | collective-permute-start | bytes 2359304 | tf_op jit(solution)/shard_map/ppermute | solution.py:27
  212.3 48.4 %collective-permute-start.21 = (bf16[1024,1024]{1,0:T(8,128)(2,1)}, bf16[1024,1024]{1,0:T(8,128)(2,1)}, u32[]{:S(2)}, u32[]{:S(2)}) collective-permute-start(bf16[1024,1024]{1,0:T(8,128)(2,1)} %get-tuple-element.181), channel_id=1, source_target_pairs={{0,2},{2,0},{1,3},{3,1},{4,6},{6,4},{5,7},{7,5},{8,10},{10,8},{9,1... | collective-permute-start | bytes 6291464 | tf_op jit(solution)/shard_map/ppermute | solution.py:27
  212.6 55.8 %collective-permute-start.22 = (bf16[1024,1024]{1,0:T(8,128)(2,1)}, bf16[1024,1024]{1,0:T(8,128)(2,1)}, u32[]{:S(2)}, u32[]{:S(2)}) collective-permute-start(bf16[1024,1024]{1,0:T(8,128)(2,1)} %get-tuple-element.162.refs_7_), channel_id=1, source_target_pairs={{0,4},{4,0},{1,5},{5,1},{2,6},{6,2},{3,7},{7,3},{8,12},{12,8},{9,1... | collective-permute-start | bytes 6291464 | tf_op jit(solution)/shard_map/ppermute | solution.py:27
  251.1 42.1 %collective-permute-start.31 = (bf16[1024,512]{1,0:T(8,128)(2,1)}, bf16[1024,512]{1,0:T(8,128)(2,1)}, u32[]{:S(2)}, u32[]{:S(2)}) collective-permute-start(bf16[1024,512]{1,0:T(8,128)(2,1)} %get-tuple-element.211), channel_id=1, source_target_pairs={{0,1},{1,0},{2,3},{3,2},{4,5},{5,4},{6,7},{7,6},{8,9},{9,8},{10,11... | collective-permute-start | bytes 3145736 | tf_op jit(solution)/shard_map/ppermute | solution.py:27
  268.1 31.7 %collective-permute-start.25 = (bf16[2,256,1024]{2,1,0:T(8,128)(2,1)}, bf16[2,256,1024]{2,1,0:T(8,128)(2,1)}, u32[]{:S(2)}, u32[]{:S(2)}) collective-permute-start(bf16[2,256,1024]{2,1,0:T(8,128)(2,1)} %add_convert_fusion.5.refs_14_), channel_id=1, source_target_pairs={{0,2},{2,0},{1,3},{3,1},{4,6},{6,4},{5,7},{7,5},{8,10},{10,8},{9,1... | collective-permute-start | bytes 3145736 | tf_op jit(solution)/shard_map/ppermute | solution.py:27
  272.3 139.3 %reduce-scatter.5.cloned.1.call-start = ((), (), s32[]{:S(2)}) async-start(), calls=%async_computation.3 | async-start | bytes 1310720 | tf_op jit(solution)/shard_map/reduce_scatter | solution.py:945
  292.5 28.4 %collective-permute-start.28 = (bf16[4,128,1024]{2,1,0:T(8,128)(2,1)}, bf16[4,128,1024]{2,1,0:T(8,128)(2,1)}, u32[]{:S(2)}, u32[]{:S(2)}) collective-permute-start(bf16[4,128,1024]{2,1,0:T(8,128)(2,1)} %constant_dynamic-slice_fusion.12.refs_16_), channel_id=1, source_target_pairs={{0,4},{4,0},{1,5},{5,1},{2,6},{6,2},{3,7},{7,3},{8,12},{12,8},{9,1... | collective-permute-start | bytes 3145736 | tf_op jit(solution)/shard_map/ppermute | solution.py:27
  292.6 17.0 %collective-permute-start.27 = (bf16[2,256,1024]{2,1,0:T(8,128)(2,1)}, bf16[2,256,1024]{2,1,0:T(8,128)(2,1)}, u32[]{:S(2)}, u32[]{:S(2)}) collective-permute-start(bf16[2,256,1024]{2,1,0:T(8,128)(2,1)} %get-tuple-element.193), channel_id=1, source_target_pairs={{0,1},{1,0},{2,3},{3,2},{4,5},{5,4},{6,7},{7,6},{8,9},{9,8},{10,11... | collective-permute-start | bytes 3145736 | tf_op jit(solution)/shard_map/ppermute | solution.py:27
  297.1 33.3 %collective-permute-start.32 = (bf16[4,128,512]{2,1,0:T(8,128)(2,1)}, bf16[4,128,512]{2,1,0:T(8,128)(2,1)}, u32[]{:S(2)}, u32[]{:S(2)}) collective-permute-start(bf16[4,128,512]{2,1,0:T(8,128)(2,1)} %constant_dynamic-slice_fusion.10), channel_id=1, source_target_pairs={{0,4},{4,0},{1,5},{5,1},{2,6},{6,2},{3,7},{7,3},{8,12},{12,8},{9,1... | collective-permute-start | bytes 1572872 | tf_op jit(solution)/shard_map/ppermute | solution.py:27
  298.8 24.8 %collective-permute-start.23 = (bf16[1,256,1024]{2,1,0:T(8,128)(2,1)}, bf16[1,256,1024]{2,1,0:T(8,128)(2,1)S(1)}, u32[]{:S(2)}, u32[]{:S(2)}) collective-permute-start(bf16[1,256,1024]{2,1,0:T(8,128)(2,1)} %get-tuple-element.186), channel_id=1, source_target_pairs={{0,1},{1,0},{2,3},{3,2},{4,5},{5,4},{6,7},{7,6},{8,9},{9,8},{10,11... | collective-permute-start | bytes 1572872 | tf_op jit(solution)/shard_map/ppermute | solution.py:27
  299.8 23.8 %collective-permute-start.26 = (bf16[1,256,1024]{2,1,0:T(8,128)(2,1)}, bf16[1,256,1024]{2,1,0:T(8,128)(2,1)S(1)}, u32[]{:S(2)}, u32[]{:S(2)}) collective-permute-start(bf16[1,256,1024]{2,1,0:T(8,128)(2,1)} %add_convert_fusion.9), channel_id=1, source_target_pairs={{0,2},{2,0},{1,3},{3,1},{4,6},{6,4},{5,7},{7,5},{8,10},{10,8},{9,1... | collective-permute-start | bytes 1572872 | tf_op jit(solution)/shard_map/ppermute | solution.py:27
  317.6 29.0 %collective-permute-start.30 = (bf16[4,128,768]{2,1,0:T(8,128)(2,1)}, bf16[4,128,768]{2,1,0:T(8,128)(2,1)}, u32[]{:S(2)}, u32[]{:S(2)}) collective-permute-start(bf16[4,128,768]{2,1,0:T(8,128)(2,1)} %constant_dynamic-slice_fusion.11), channel_id=1, source_target_pairs={{0,4},{4,0},{1,5},{5,1},{2,6},{6,2},{3,7},{7,3},{8,12},{12,8},{9,1... | collective-permute-start | bytes 2359304 | tf_op jit(solution)/shard_map/ppermute | solution.py:27
  360.0 28.5 %collective-permute-start.36 = (bf16[2,38,1024]{2,1,0:T(8,128)(2,1)S(1)}, bf16[2,38,1024]{2,1,0:T(8,128)(2,1)S(1)}, u32[]{:S(2)}, u32[]{:S(2)}) collective-permute-start(bf16[2,38,1024]{2,1,0:T(8,128)(2,1)S(1)} %maximum_select_fusion.3), channel_id=1, source_target_pairs={{0,16},{8,24},{16,0},{24,8},{1,17},{9,25},{17,1},{25,9},{2,18},{10... | collective-permute-start | bytes 466952 | tf_op jit(solution)/shard_map/ppermute | solution.py:965
  362.3 26.3 %collective-permute-start.35 = (bf16[2,38,1024]{2,1,0:T(8,128)(2,1)S(1)}, bf16[2,38,1024]{2,1,0:T(8,128)(2,1)S(1)}, u32[]{:S(2)}, u32[]{:S(2)}) collective-permute-start(bf16[2,38,1024]{2,1,0:T(8,128)(2,1)S(1)} %maximum_select_fusion.3), channel_id=1, source_target_pairs={{0,8},{8,0},{16,24},{24,16},{1,9},{9,1},{17,25},{25,17},{2,10},{10... | collective-permute-start | bytes 466952 | tf_op jit(solution)/shard_map/ppermute | solution.py:965
  362.3 26.4 %collective-permute-start.44 = (bf16[128,1280]{1,0:T(8,128)(2,1)S(1)}, bf16[128,1280]{1,0:T(8,128)(2,1)S(1)}, u32[]{:S(2)}, u32[]{:S(2)}) collective-permute-start(bf16[128,1280]{1,0:T(8,128)(2,1)S(1)} %get-tuple-element.227), channel_id=1, source_target_pairs={{0,24},{8,16},{16,8},{24,0},{1,25},{9,17},{17,9},{25,1},{2,26},{10... | collective-permute-start | bytes 983048 | tf_op jit(solution)/shard_map/ppermute | solution.py:740
  364.6 37.4 %collective-permute-start.43 = (bf16[128,1280]{1,0:T(8,128)(2,1)S(1)}, bf16[128,1280]{1,0:T(8,128)(2,1)S(1)}, u32[]{:S(2)}, u32[]{:S(2)}) collective-permute-start(bf16[128,1280]{1,0:T(8,128)(2,1)S(1)} %get-tuple-element.228), channel_id=1, source_target_pairs={{0,16},{8,24},{16,0},{24,8},{1,17},{9,25},{17,1},{25,9},{2,18},{10... | collective-permute-start | bytes 983048 | tf_op jit(solution)/shard_map/ppermute | solution.py:740
  366.0 36.0 %collective-permute-start.42 = (bf16[128,1280]{1,0:T(8,128)(2,1)S(1)}, bf16[128,1280]{1,0:T(8,128)(2,1)S(1)}, u32[]{:S(2)}, u32[]{:S(2)}) collective-permute-start(bf16[128,1280]{1,0:T(8,128)(2,1)S(1)} %get-tuple-element.226), channel_id=1, source_target_pairs={{0,8},{8,0},{16,24},{24,16},{1,9},{9,1},{17,25},{25,17},{2,10},{10... | collective-permute-start | bytes 983048 | tf_op jit(solution)/shard_map/ppermute | solution.py:740
  411.5 25.3 %collective-permute-start.46 = (bf16[128,2048]{1,0:T(8,128)(2,1)S(1)}, bf16[128,2048]{1,0:T(8,128)(2,1)}, u32[]{:S(2)}, u32[]{:S(2)}) collective-permute-start(bf16[128,2048]{1,0:T(8,128)(2,1)S(1)} %pad_maximum_fusion.4.refs_5_), channel_id=1, source_target_pairs={{0,1},{1,0},{2,3},{3,2},{4,5},{5,4},{6,7},{7,6},{8,9},{9,8},{10,11... | collective-permute-start | bytes 1572872 | tf_op jit(solution)/shard_map/ppermute | solution.py:27
  411.8 21.4 %collective-permute-start.38 = (bf16[256,1024]{1,0:T(8,128)(2,1)}, bf16[256,1024]{1,0:T(8,128)(2,1)S(1)}, u32[]{:S(2)}, u32[]{:S(2)}) collective-permute-start(bf16[256,1024]{1,0:T(8,128)(2,1)} %reduce-scatter.3.cloned.1.call-done), channel_id=1, source_target_pairs={{0,2},{2,0},{1,3},{3,1},{4,6},{6,4},{5,7},{7,5},{8,10},{10,8},{9,1... | collective-permute-start | bytes 1572872 | tf_op jit(solution)/shard_map/ppermute | solution.py:27
  413.5 18.4 %collective-permute-start.40 = (bf16[128,1024]{1,0:T(8,128)(2,1)}, bf16[128,1024]{1,0:T(8,128)(2,1)S(1)}, u32[]{:S(2)}, u32[]{:S(2)}) collective-permute-start(bf16[128,1024]{1,0:T(8,128)(2,1)} %bitcast.125), channel_id=1, source_target_pairs={{0,2},{2,0},{1,3},{3,1},{4,6},{6,4},{5,7},{7,5},{8,10},{10,8},{9,1... | collective-permute-start | bytes 786440 | tf_op jit(solution)/shard_map/ppermute | solution.py:27
  (71 other events, 497.3 us)
Sparse Core Ops, SparseCore 0:
  272.4 47.5 reduce-scatter.2
  331.7 28.4 reduce-scatter.4
where the time goes:
time: 458 us; the launch traced here: 450 us
  Pallas kernels  210 us (46%)
  waiting for transfers between devices  88.4 us (19%)
  starting transfers between devices  53.9 us (12%)
  other arithmetic  39.6 us (9%)
  local copies, waits for them, and re-layouts  32.6 us (7%)
  between operations  15.3 us (3%)
  matrix products  10.4 us (2%)
    pallas_call x17, Pallas kernels, call(): pl.pallas_call(kernel, grid_spec=pltpu.PrefetchScalarGridSpec(num_scalar_...  210 us
    ppermute x41, waiting for transfers between devices, swap(): return lax.ppermute(value, axis, [(0, 1), (1, 0)])  70.1 us
    ppermute x41, starting transfers between devices, swap(): return lax.ppermute(value, axis, [(0, 1), (1, 0)])  27.3 us
    ppermute x3, starting transfers between devices, over_z(): lax.ppermute(parts[n], 'z', [(i, i ^ n) for i in range(depth)])  21.3 us
    convert_element_type x12, other arithmetic, add_low(): return (kept.astype(F32) + sent.astype(F32)).astype(BF16)  18.1 us
    ppermute x3, waiting for transfers between devices, over_z(): lax.ppermute(parts[n], 'z', [(i, i ^ n) for i in range(depth)])  13.2 us
    unnamed x98, local copies, waits for them, and re-layouts  13.1 us
    dot_general x3, matrix products, dot(): lax.dot_general(left_op, right_op, (((left_dim,), (right_dim,)), ((), ())...  10.4 us
  transfers between devices with their start and end apart: 49, of which 18 were waited for; matrix products, arithmetic and copies ran while one was open for 15% of the time, Pallas kernels for 27%

commit v1 on v0

--- a/solution.py
+++ b/solution.py
@@ -21,6 +21,7 @@
 GELU_B = GELU_A * 0.044715
 BLOCK = 256
 VMEM = 60 * 1024 * 1024
+TIME_BIAS, GAIN1, BIAS1, OUT_BIAS, GAIN2, BIAS2, DOWN_BIAS, QKV_BIAS, UP_BIAS = (slice(n, n + 1) for n in (0, 1, 2, 3, 4, 5, 6, 7, 10))
 
 
 def swap(value, axis):
@@ -115,46 +116,46 @@
     return pl.BlockSpec(shape, lambda g, *_: tuple(start + g if n == axis else 0 for n in range(len(shape))))
 
 
-def norm1_body(x_ref, seg_ref, shift_ref, gain_ref, bias_ref, stream_ref, low_ref):
-    slots = lax.broadcasted_iota(jnp.int32, (SEGS, seg_ref.shape[-1]), 0) == seg_ref[0]
+def norm1_body(x_ref, seg_ref, shift_ref, vec_ref, stream_ref, low_ref):
+    seg = seg_ref[pl.ds(pl.program_id(0), 1)]
+    slots = lax.broadcasted_iota(jnp.int32, (SEGS, seg.shape[-1]), 0) == seg
     onehot = slots.astype(F32).astype(BF16)
-    added = dot(jnp.concatenate([onehot, onehot], axis=0), split_low(shift_ref[0]), 0, 0)
+    shift = shift_ref[0] + vec_ref[TIME_BIAS]
+    added = dot(jnp.concatenate([onehot, onehot], axis=0), split_low(shift), 0, 0)
     stream = x_ref[0].astype(F32) + added
     hat, _ = centre(stream)
     stream_ref[0] = stream
-    low_ref[0] = (hat * gain_ref[...] + bias_ref[...]).astype(BF16)
-
-
-def norm1(x, seg, shift, gain, bias):
+    low_ref[0] = (hat * vec_ref[GAIN1] + vec_ref[BIAS1]).astype(BF16)
+
+
+def norm1(x, seg, shift, vecs):
     rows, shard, model = x.shape
     block = along((1, shard, model))
     return call(
         norm1_body, "norm1", (), (rows,),
-        [(x, block), (seg, along((1, 1, shard))), (shift, along((1, SEGS, model))), (gain, fixed((1, model))), (bias, fixed((1, model)))],
+        [(x, block), (seg, fixed(seg.shape)), (shift, along((1, SEGS, model))), (vecs, fixed(vecs.shape))],
         [(x.shape, F32, block), (x.shape, BF16, block)],
     )
 
 
-def qkv_body(me_ref, a_ref, b_ref, w_ref, bias_ref, cos_ref, sin_ref, out_ref, all_ref, own_ref):
+def qkv_body(me_ref, a_ref, b_ref, w_ref, vec_ref, cos_ref, sin_ref, out_ref, own_ref):
     rows, shard, model = a_ref.shape
     width = w_ref.shape[1]
-    refs = (a_ref, b_ref)
+    places = [(n, r) for n in range(2) for r in range(rows)]
     step = pl.program_id(0)
 
-    @pl.when(step == 0)
-    def _():
-        for n, x_ref in enumerate(refs):
-            all_ref[n] = x_ref[...]
-
     def run(turned):
-        w, bias = w_ref[...], bias_ref[...].astype(F32)
-        found = [dot(x_ref[...].reshape(rows * shard, model), w) for x_ref in refs]
-        for n, full in enumerate(found):
-            for r in range(rows):
-                values = full[r * shard : (r + 1) * shard] + bias
-                if turned:
-                    values = turn(values, cos_ref[n], sin_ref[n]) * jnp.where(step == 0, LOG2E * HEAD_DIM**-0.5, 1.0)
-                out_ref[0, n, r] = values.astype(BF16)
+        w = w_ref[...]
+        bias = vec_ref[pl.ds(QKV_BIAS.start + step, 1), pl.ds(pl.multiple_of(me_ref[0] * width, width), width)]
+        later = dot(a_ref[0], w)
+        for at, (n, r) in enumerate(places):
+            values = later + bias
+            if at + 1 < len(places):
+                x_ref = (a_ref, b_ref)[places[at + 1][0]]
+                later = dot(x_ref[places[at + 1][1]], w)
+            if turned:
+                values = turn(values, cos_ref[n], sin_ref[n]) * jnp.where(step == 0, LOG2E * HEAD_DIM**-0.5, 1.0)
+            out_ref[0, n, r] = values.astype(BF16)
 
     own_ref[...] = w_ref[...].T
 
@@ -167,7 +168,7 @@
         run(False)
 
 
-def project_qkv(pair, parts, me, first, second, weight, bias, cos_tab, sin_tab, held=(), deps=()):
+def project_qkv(pair, parts, me, first, second, weight, vecs, cos_tab, sin_tab, held=(), deps=()):
     rows, shard, model = first.shape
     width = model // parts
     return call(
@@ -175,16 +176,51 @@
         [(first, fixed(first.shape)), (second, fixed(first.shape))]
         + [
             (weight, pl.BlockSpec((model, width), lambda g, m: (0, g * parts + m[0]))),
-            (bias, pl.BlockSpec((1, width), lambda g, m: (0, g * parts + m[0]))),
+            (vecs, fixed(vecs.shape)),
             (cos_tab, pl.BlockSpec((2, shard, 128), lambda g, m: (pair, 0, 0))),
             (sin_tab, pl.BlockSpec((2, shard, 128), lambda g, m: (pair, 0, 0))),
         ],
         [
             ((3, parts, rows, shard, width), BF16, pl.BlockSpec((1, 2, rows, shard, width), lambda g, m: (g, pair, 0, 0, 0))),
-            ((parts, rows, shard, model), BF16, pl.BlockSpec((2, rows, shard, model), lambda g, m: (pair, 0, 0, 0))),
             ((3 * width, model), BF16, along((width, model))),
         ],
-        held=[(array, n) for n, array in enumerate(held)], deps=deps
+        held=[(array, n) for n, array in enumerate(held)], deps=deps,
+    )
+
+
+def qkv_grads(x_at, pieces, grad, blocks):
+    rows, shard, model = pieces[0].shape
+    tokens = rows * shard
+    parts, columns = len(pieces), grad.shape[3]
+    size = model // (2 * blocks)
+
+    def body(at_ref, x0, x1, x2, x3, g_ref, out_ref, keep_ref, sum_ref):
+        total, sums = 0.0, 0.0
+        for n, x_ref in enumerate((x0, x1, x2, x3)):
+            g = g_ref[n].reshape(tokens, g_ref.shape[3])
+            total = total + dot(x_ref[...].reshape(tokens, model), g, 0, 0)
+            sums = sums + jnp.sum(g.astype(F32), axis=0, keepdims=True)
+        low = total.astype(BF16)
+        for x in range(2):
+            for b in range(blocks):
+                values = low[(2 * b + x) * size : (2 * b + x + 1) * size]
+
+                @pl.when(at_ref[0] == x)
+                def _():
+                    keep_ref[b] = values
+
+                @pl.when(at_ref[0] != x)
+                def _():
+                    out_ref[b] = values
+
+        sum_ref[...] = sums
+
+    block = along((blocks, size, BLOCK), 2)
+    shape = (blocks, size, columns)
+    return call(
+        body, "qkv_grads", (x_at.astype(jnp.int32)[None],), (columns // BLOCK,),
+        [(x, fixed(x.shape)) for x in pieces] + [(grad, along((parts, rows, shard, BLOCK), 3))],
+        [(shape, BF16, block), (shape, BF16, block), ((1, columns), F32, along((1, BLOCK), 1))],
     )
 
 
@@ -405,7 +441,7 @@
 
 
 def middle_body(
-    order_ref, a0, a1, a2, a3, w0, w1, w2, w3, stream_ref, bias_ref, gain_ref, shift_ref, mid_ref, low_ref, all_ref,
+    order_ref, a0, a1, a2, a3, w0, w1, w2, w3, stream_ref, vec_ref, mid_ref, low_ref, all_ref,
 ):
     _, shard, model = stream_ref.shape
     total = 0.0
@@ -413,10 +449,10 @@
         values = a[...].reshape(shard, a.shape[-1])
         total = total + dot(values, w[...])
         all_ref[0, :, n * a.shape[-1] : (n + 1) * a.shape[-1]] = values
-    mid = stream_ref[0] + (total + bias_ref[...])
+    mid = stream_ref[0] + (total + vec_ref[OUT_BIAS])
     hat, _ = centre(mid)
     mid_ref[0] = mid
-    low_ref[0] = (hat * gain_ref[...] + shift_ref[...]).astype(BF16)
+    low_ref[0] = (hat * vec_ref[GAIN2] + vec_ref[BIAS2]).astype(BF16)
 
 
 def out_blocks(weight, parts):
@@ -428,15 +464,15 @@
     return [(weight, block(i)) for i in range(parts)]
 
 
-def middle_norm(start, count, order, attended, weight, stream, bias, gain, shift, held=()):
+def middle_norm(start, count, order, attended, weight, stream, vecs, held=()):
     rows, shard, model = stream.shape
     parts = len(attended)
     width = model // parts
-    block, line, one = along((1, shard, model), 0, start), fixed((1, model)), along((1, shard, width))
+    block, one = along((1, shard, model), 0, start), along((1, shard, width))
     first = [along((1, 1, shard, width), 1, start), one, along((1, 1, shard, width), 1), one]
     return call(
         middle_body, "middle", (order,), (count,),
-        list(zip(attended, first)) + out_blocks(weight, parts) + [(stream, block), (bias, line), (gain, line), (shift, line)],
+        list(zip(attended, first)) + out_blocks(weight, parts) + [(stream, block), (vecs, fixed(vecs.shape))],
         [
             (stream.shape, F32, block),
             ((count, shard, model), BF16, along((1, shard, model))),
@@ -482,7 +518,7 @@
     )
 
 
-def hidden_body(blocks, *refs):
+def hidden_body(blocks, blk_ref, *refs):
     pieces, refs = refs[:-10], refs[-10:]
     g_ref, up_ref, row_ref, bias_ref, act_ref, grad_ref, sum_ref, both_ref, part_ref, held = refs
     sizes = [ref.shape[0] * ref.shape[1] for ref in pieces]
@@ -496,7 +532,13 @@
 
     @pl.when(step < blocks)
     def _():
-        up, bias = up_ref[...], bias_ref[...]
+        up = up_ref[...]
+        if bias_ref.shape[1] == BLOCK:
+            bias = bias_ref[...]
+        else:
+            per = bias_ref.shape[1] // BLOCK
+            at = pl.multiple_of(blk_ref[step] % per * BLOCK, BLOCK)
+            bias = bias_ref[pl.ds(UP_BIAS.start + blk_ref[step] // per, 1), pl.ds(at, BLOCK)]
         total = 0.0
         later = dot(pieces[0][...].reshape(sizes[0], -1), up)
         for n, (start, size) in enumerate(zip(starts, sizes)):
@@ -522,7 +564,7 @@
         part_ref[...] = dot(grad, row_ref[...], 1, 1).astype(BF16)
 
 
-def hidden_units(pieces, grads, up, bias):
+def hidden_units(blk, pieces, grads, up, bias):
     model = pieces[0].shape[2]
     tokens, half = grads.shape
     blocks, more = half // BLOCK, model // BLOCK
@@ -533,31 +575,43 @@
     def second(g):
         return jnp.maximum(g - blocks, 0)
 
-    column, line = pl.BlockSpec((tokens, BLOCK), lambda g: (0, first(g))), pl.BlockSpec((1, BLOCK), lambda g: (0, first(g)))
-    return call(
-        functools.partial(hidden_body, blocks), "hidden", (), (blocks + more,),
+    column = pl.BlockSpec((tokens, BLOCK), lambda g, b: (0, first(g)))
+    line = pl.BlockSpec((1, BLOCK), lambda g, b: (0, first(g)))
+    return call(
+        functools.partial(hidden_body, blocks), "hidden", (blk,), (blocks + more,),
         [(piece, fixed(piece.shape)) for piece in pieces]
         + [
             (grads, column),
-            (up, pl.BlockSpec((model, BLOCK), lambda g: (0, first(g)))),
-            (up, pl.BlockSpec((BLOCK, half), lambda g: (second(g), 0))),
-            (bias, line),
+            (up, pl.BlockSpec((model, BLOCK), lambda g, b: (0, first(g)))),
+            (up, pl.BlockSpec((BLOCK, half), lambda g, b: (second(g), 0))),
+            (bias, line if bias.shape[0] == 1 else fixed(bias.shape)),
         ],
         [
             (grads.shape, BF16, column),
             (grads.shape, BF16, column),
             ((1, half), F32, line),
             ((tokens, model), BF16, fixed((tokens, model))),
-            ((tokens, model), BF16, pl.BlockSpec((tokens, BLOCK), lambda g: (0, second(g)))),
+            ((tokens, model), BF16, pl.BlockSpec((tokens, BLOCK), lambda g, b: (0, second(g)))),
         ],
         [pltpu.VMEM((blocks, tokens, BLOCK), BF16)]
     )
 
 
-def sent_body(half_ref, both_ref, cot_ref, out_ref, keep_ref, act_ref, up_out, up_keep, down_out):
+def sent_body(half_ref, both_ref, cot_ref, out_ref, keep_ref, act_ref, up0, up1, up_keep, down0, down1):
     both = both_ref[...]
-    down_out[...] = dot(act_ref[...], cot_ref[...], 0, 0).astype(BF16)
-    up_out[...] = dot(both, out_ref[...], 0, 0).astype(BF16)
+    down = dot(act_ref[...], cot_ref[...], 0, 0).astype(BF16)
+    up = dot(both, out_ref[...], 0, 0).astype(BF16)
+
+    @pl.when(2 * pl.program_id(0) < pl.num_programs(0))
+    def _():
+        down0[...] = down
+        up0[...] = up
+
+    @pl.when(2 * pl.program_id(0) >= pl.num_programs(0))
+    def _():
+        down1[...] = down
+        up1[...] = up
+
     up_keep[...] = dot(both, keep_ref[...], 0, 0).astype(BF16)
 
 
@@ -565,7 +619,14 @@
     tokens, model = both.shape
     half = grad.shape[1] // 2
     steps = half // BLOCK
-    column = along((model, BLOCK), 1)
+    cut = steps // 2
+
+    def first(g):
+        return jnp.minimum(g, cut - 1)
+
+    def second(g):
+        return jnp.maximum(g - cut, 0)
+
     return call(
         sent_body, "sent_grads", (kept,), (steps,),
         [
@@ -575,7 +636,13 @@
             (grad, pl.BlockSpec((tokens, BLOCK), lambda g, k: (0, k[0] * steps + g))),
             (act, along((tokens, BLOCK), 1)),
         ],
-        [((model, half), BF16, column), ((model, half), BF16, column), ((half, model), BF16, along((BLOCK, model)))],
+        [
+            ((model, half // 2), BF16, pl.BlockSpec((model, BLOCK), lambda g, k: (0, first(g)))),
+            ((model, half // 2), BF16, pl.BlockSpec((model, BLOCK), lambda g, k: (0, second(g)))),
+            ((model, half), BF16, along((model, BLOCK), 1)),
+            ((half // 2, model), BF16, pl.BlockSpec((BLOCK, model), lambda g, k: (first(g), 0))),
+            ((half // 2, model), BF16, pl.BlockSpec((BLOCK, model), lambda g, k: (second(g), 0))),
+        ],
     )
 
 
@@ -638,13 +705,13 @@
 
 
 def middle_back_body(
-    order_ref, part_ref, sent_ref, mid_ref, cot_ref, gain_ref, w0, w1, w2, w3,
+    order_ref, part_ref, sent_ref, mid_ref, cot_ref, vec_ref, w0, w1, w2, w3,
     grad_ref, low_ref, att0_ref, att1_ref, far_ref, sums_ref,
 ):
     grad = part_ref[...].astype(F32) + sent_ref[...].astype(F32)
     hat, inverse = centre(mid_ref[0])
     cot = cot_ref[0].astype(F32)
-    total = cot + norm_back(grad, gain_ref[...], hat, inverse)
+    total = cot + norm_back(grad, vec_ref[GAIN2], hat, inverse)
     low = total.astype(BF16)
     grad_ref[0] = total
     low_ref[0] = low
@@ -663,14 +730,14 @@
     sums_ref[3:4] += jnp.sum(cot, axis=0, keepdims=True)
 
 
-def middle_back(order, both, sent, mid, cot, gain, weight, parts, deps=()):
+def middle_back(order, both, sent, mid, cot, vecs, weight, parts, deps=()):
     rows, shard, model = mid.shape
     width = model // parts
     block, one = along((1, shard, model)), along((1, shard, width))
     flat = pl.BlockSpec((shard, model), lambda g, o: (g, 0))
     return call(
         middle_back_body, "middle_back", (order,), (rows,),
-        [(both, flat), (sent, flat), (mid, block), (cot, block), (gain, fixed((1, model)))] + out_blocks(weight, parts),
+        [(both, flat), (sent, flat), (mid, block), (cot, block), (vecs, fixed(vecs.shape))] + out_blocks(weight, parts),
         [
             (mid.shape, F32, block),
             (mid.shape, BF16, block),
@@ -683,12 +750,13 @@
     )
 
 
-def norm1_back_body(part_ref, near_ref, far_ref, stream_ref, mid_ref, gain_ref, seg_ref, in_ref, shift_ref, sums_ref):
+def norm1_back_body(start, part_ref, near_ref, far_ref, stream_ref, mid_ref, vec_ref, seg_ref, in_ref, shift_ref, sums_ref):
     grad = part_ref[0].astype(F32) + near_ref[0].astype(F32) + far_ref[0].astype(F32)
     hat, inverse = centre(stream_ref[0])
-    total = mid_ref[0] + norm_back(grad, gain_ref[...], hat, inverse)
+    total = mid_ref[0] + norm_back(grad, vec_ref[GAIN1], hat, inverse)
     in_ref[0] = total.astype(BF16)
-    slots = lax.broadcasted_iota(jnp.int32, (SEGS, seg_ref.shape[-1]), 0) == seg_ref[0]
+    seg = seg_ref[pl.ds(pl.program_id(0) + start, 1)]
+    slots = lax.broadcasted_iota(jnp.int32, (SEGS, seg.shape[-1]), 0) == seg
     onehot = slots.astype(F32).astype(BF16)
     shift_ref[0] = dot(jnp.concatenate([onehot, onehot], axis=1), split_low(total))
 
@@ -700,13 +768,13 @@
     sums_ref[1:2] += jnp.sum(grad, axis=0, keepdims=True)
 
 
-def norm1_back(start, count, own, near, far, stream, mid, gain, seg, held=(), deps=()):
+def norm1_back(start, count, own, near, far, stream, mid, vecs, seg, held=(), deps=()):
     rows, shard, model = stream.shape
     block, own_block = along((1, shard, model), 0, start), along((1, shard, model))
     return call(
-        norm1_back_body, "norm1_back", (), (count,),
-        [(own, own_block), (near, own_block), (far, own_block), (stream, block), (mid, block), (gain, fixed((1, model)))]
-        + [(seg, along((1, 1, shard), 0, start))],
+        functools.partial(norm1_back_body, start), "norm1_back", (), (count,),
+        [(own, own_block), (near, own_block), (far, own_block), (stream, block), (mid, block), (vecs, fixed(vecs.shape))]
+        + [(seg, fixed(seg.shape))],
         [
             (stream.shape, BF16, block),
             ((count, SEGS, model), F32, along((1, SEGS, model))),
@@ -805,17 +873,16 @@
     z_at, x_at, y_at, c_at = (lax.axis_index(name) for name in ("z", "x", "y", "c"))
     me = 2 * y_at + c_at
 
-    def line(vector):
-        return vector.astype(F32)[None]
+    vecs = [time_bias, norm1_gain, norm1_bias, out_bias, norm2_gain, norm2_bias, down_bias, qkv_bias, up_bias]
+    vecs = jnp.concatenate(vecs).astype(F32).reshape(-1, model)
 
     seg_two = swap(segment_ids, "y")
     segs = jnp.stack([segment_ids, swap(segment_ids, "c"), seg_two, swap(seg_two, "c")], axis=1)
 
     groups = [(0, rows - 1), (rows - 1, 1)] if rows > 1 else [(0, 1)]
-    seg = segment_ids[:, None, :]
     features = time_features(doc_times.reshape(rows * SEGS), jnp.arange(TEMB), TEMB // 2)
-    time_shift = dot(features, time_weight).reshape(rows, SEGS, model) + time_bias.astype(F32)
-    stream, own1 = norm1(inputs, seg, time_shift, line(norm1_gain), line(norm1_bias))
+    time_shift = dot(features, time_weight).reshape(rows, SEGS, model)
+    stream, own1 = norm1(inputs, segment_ids, time_shift, vecs)
     own1, segs = tie(own1, segs)
     two1 = swap(own1, "y")
     one1 = swap(own1, "c")
@@ -852,17 +919,16 @@
     grad_act, up_own, down_own, cot_both = cot_down(
         blk, cot, cot_other, up_from, down_from, piece % BLOCK != 0, half
     )
-    up_bias_own = lax.dynamic_index_in_dim(up_bias.reshape(depth, 2, 2, piece), c_at, 2, keepdims=False)
-    up_bias_own = jnp.where(x_at == 1, up_bias_own, up_bias_own[:, ::-1]).transpose(1, 0, 2).reshape(half)
-
-    bias_line = qkv_bias.reshape(1, 3 * model)
-    qkv, normed1_all, qkv_own = project_qkv(
-        0, parts, me_list, own1, one1, qkv_weight, bias_line, cos_tab, sin_tab, (), (grad_act,)
-    )
+    up_bias_own = vecs
+    if piece % BLOCK:
+        up_bias_own = lax.dynamic_index_in_dim(up_bias.reshape(depth, 2, 2, piece), c_at, 2, keepdims=False)
+        up_bias_own = jnp.where(x_at == 1, up_bias_own, up_bias_own[:, ::-1]).transpose(1, 0, 2)
+        up_bias_own = up_bias_own.reshape(1, half).astype(F32)
+
+    qkv, qkv_own = project_qkv(0, parts, me_list, own1, one1, qkv_weight, vecs, cos_tab, sin_tab, (), (grad_act,))
     two1, qkv = tie(two1, qkv)
-    qkv, normed1_all, _ = project_qkv(
-        1, parts, me_list, two1, swap(two1, "c"), qkv_weight, bias_line, cos_tab, sin_tab, (qkv, normed1_all)
-    )
+    three1 = swap(two1, "c")
+    qkv, _ = project_qkv(1, parts, me_list, two1, three1, qkv_weight, vecs, cos_tab, sin_tab, (qkv,))
     o, lse, attended = None, None, []
     for start, count in groups:
         held = () if o is None else (o, lse)
@@ -873,36 +939,46 @@
         far, o = tie(values[1], o)
         values = exchange(o, values[0], far)
         middle, low, attended_all = middle_norm(
-            start, count, order_list, values, out_weight, stream, line(out_bias), line(norm2_gain), line(norm2_bias), held
+            start, count, order_list, values, out_weight, stream, vecs, held
         )
         held = (middle, attended_all)
         normed2.append(low)
         normed2_other.append(swap(low, "c"))
 
     active, grad_hidden, up_b, normed2_both, part2 = hidden_units(
-        normed2 + normed2_other, grad_act, up_own, line(up_bias_own)
+        blk, normed2 + normed2_other, grad_act, up_own, up_bias_own
     )
     part2_sent = swap(part2[tokens:], "c")
     grad_middle, grad_middle_low, att0, att1, far, sums2 = middle_back(
-        order_list, part2, part2_sent, middle, cotangent, line(norm2_gain), out_weight, parts
+        order_list, part2, part2_sent, middle, cotangent, vecs, out_weight, parts
     )
     far = swap(far, "y")
     sums2 = sums2[:4]
 
     active, grad_hidden, att0 = tie(active, grad_hidden, att0)
     up_half = (x_at == y_at).astype(jnp.int32)
-    up_out, up_grad, down_out = sent_grads(up_half[None], normed2_both, cot_both, grad_hidden, active)
+    up_out, up_late, up_grad, down_out, down_late = sent_grads(
+        up_half[None], normed2_both, cot_both, grad_hidden, active
+    )
+    up_out, down_out, far = tie(up_out, down_out, far)
     up_sent, down_sent = swap(up_out, "y"), swap(down_out, "x")
     down_kept, feed, out_sent, out_grad = kept_grads(
         order_list, active, cot_both, down_own, attended_all.reshape(tokens, model),
         grad_middle_low.reshape(tokens, model), c_at, (down_out, far),
     )
     out_sent = swap(out_sent, "c")
-    feed = feed[:tokens].astype(F32) + swap(feed[tokens:], "c").astype(F32) + line(down_bias)
+    down_kept, feed, up_sent, down_sent, up_late, down_late = tie(
+        down_kept, feed, up_sent, down_sent, up_late, down_late
+    )
+    up_sent = [up_sent, swap(up_late, "y")]
+    down_sent = [down_sent, swap(down_late, "x")]
+    feed = feed[:tokens].astype(F32) + swap(feed[tokens:], "c").astype(F32) + down_bias.astype(F32)
     output = (middle + feed.reshape(rows, shard, model)).astype(BF16)
-
     up_rows = model // dp
-    down_kept, output, out_grad, far = tie(down_kept, output, out_grad, far)
+    out_c = add_low(out_grad, out_sent)
+
+    down_kept, output, out_c, far = tie(down_kept, output, out_c, far)
+    out_z = lax.psum_scatter(out_c, "z", scatter_dimension=0, tiled=True)
     grad_o = exchange(att0, att1, far)
     grad_qkv, back = (), []
     for start, count in groups:
@@ -912,42 +988,34 @@
         )
         grad_qkv = (grad_qkv,)
         if not back:
-            own, up_grad, down_kept, out_grad = tie(own, up_grad, down_kept, out_grad)
-            down_x = add_low(down_kept, down_sent)
+            own, up_grad, down_kept = tie(own, up_grad, down_kept)
+            down_x = add_low(down_kept, jnp.concatenate(down_sent, axis=0))
             down_z = lax.psum_scatter(down_x, "z", scatter_dimension=0, tiled=True)
-            up_y = add_low(up_grad, up_sent).reshape(depth, 2 * up_rows, half // 2)
+            up_y = add_low(up_grad, jnp.concatenate(up_sent, axis=1)).reshape(depth, 2 * up_rows, half // 2)
             up_out = cut(up_y, 1 - x_at, up_rows, 1)
             up_sent = swap(up_out, "x")
         there = add_low(two, swap(three, "c"))
         if not back:
             there, up_out = tie(there, up_out)
         back.append((own, swap(one, "c"), swap(there, "y")))
-    out_c = add_low(out_grad, out_sent)
-    out_c = out_c.reshape(depth, 2 * up_rows, model // 2)
-    out_x = add_low(cut(out_c, x_at, up_rows, 1), swap(cut(out_c, 1 - x_at, up_rows, 1), "x"))
-    grad_qkv, there, far = tie(grad_qkv[0], there, back[0][2])
+    grad_qkv, there, far, up_sent, up_y = tie(grad_qkv[0], there, back[0][2], up_sent, up_y)
     back[0] = back[0][:2] + (far,)
     back[-1] = back[-1][:2] + (swap(there, "y"),)
-    grad_qkv = grad_qkv.reshape(parts * tokens, 3 * width)
-    qkv_grad = dot(normed1_all.reshape(parts * tokens, model), grad_qkv, 0, 0).astype(BF16)
-    qkv_b = jnp.sum(grad_qkv.astype(F32), axis=0)
-    qkv_grad, up_y = tie(qkv_grad.reshape(depth, 2 * up_rows, 3 * width), up_y)
-    qkv_sent = swap(cut(qkv_grad, 1 - x_at, up_rows, 1), "x")
+    qkv_out, qkv_kept, qkv_b = qkv_grads(x_at, [own1, one1, two1, three1], grad_qkv, depth)
+    qkv_sent = swap(qkv_out, "x")
+    qkv_kept, up_y, up_sent, out_z = tie(qkv_kept, up_y, up_sent, out_z)
+    up_x = add_low(cut(up_y, x_at, up_rows, 1), up_sent)
+    up_z = lax.psum_scatter(up_x, "z", scatter_dimension=0, tiled=False)
+    out_x = add_low(cut(out_z, x_at, up_rows, 0), swap(cut(out_z, 1 - x_at, up_rows, 0), "x"))
     held, grad_shift, sums1 = (), [], 0.0
-    deps = (qkv_grad,)
     for (start, count), values in zip(groups, back):
         input_grad, found, sums = norm1_back(
-            start, count, *values, stream, grad_middle, line(norm1_gain), seg, held, deps
+            start, count, *values, stream, grad_middle, vecs, segment_ids, held, (up_x if held else qkv_kept,)
         )
-        if not held:
-            input_grad, up_y = tie(input_grad, up_y)
-            up_x = add_low(cut(up_y, x_at, up_rows, 1), up_sent)
-            up_z = lax.psum_scatter(up_x, "z", scatter_dimension=0, tiled=False)
-            deps = (up_x,)
         held = (input_grad,)
         grad_shift.append(found.reshape(count * SEGS, model))
         sums1 = sums1 + sums[:2]
-    qkv_x = add_low(cut(qkv_grad, x_at, up_rows, 1), qkv_sent)
+    qkv_x = add_low(qkv_kept, qkv_sent)
 
     up_b = up_b.reshape(2, depth, 1, piece)
     up_b = jnp.where(x_at == 1, up_b, up_b[::-1]).transpose(1, 0, 2, 3)
@@ -957,10 +1025,12 @@
     times = jnp.concatenate([times // 32, times % 32], axis=1).astype(F32)
     times = jnp.pad(times, ((0, 0), (0, model - times.shape[1])))
     small = jnp.concatenate(grad_shift + [sums1, sums2, qkv_b, up_b, times], axis=0)
-    small, qkv_x, out_x = tie(add_low(small, swap(small.astype(BF16), "c")), qkv_x, out_x)
-    late = jnp.concatenate([qkv_x, out_x], axis=2)
+    small, qkv_x = tie(add_low(small, swap(small.astype(BF16), "c")), qkv_x)
     small = add_low(small, swap(small, "y"))
-    small = ordered(x_at, small[None], swap(small, "x")[None], 0)
+    small, down_z = tie(small, down_z)
+    down_y = add_low(down_z, swap(down_z, "y"))
+    small, down_y = tie(ordered(x_at, small[None], swap(small, "x")[None], 0), down_y)
+    down_other = swap(down_y, "c")
     if depth == 4:
         others = [lax.ppermute(small, "z", [(i, i ^ n) for i in range(depth)]) for n in range(1, depth)]
         small = jnp.stack([small] + others)
@@ -969,17 +1039,15 @@
         small = lax.all_gather(small, "z")
     small = small.reshape(dp, small.shape[2], model)
 
-    small, down_z, up_z = tie(small, down_z, up_z)
-    late = over_z(late, z_at, depth)
+    small, up_z = tie(small, up_z)
+    up_done = ordered(y_at, up_z, swap(up_z, "y"), 1)
+    up_other = swap(up_done, "c")
+    late = jnp.concatenate([over_z(qkv_x, z_at, depth), out_x], axis=1)
     late_sent = swap(late, "y")
     qkv_y = ordered(y_at, late[None, :, : 3 * width], late_sent[None, :, : 3 * width], 0)
     out_y = add_low(late[:, 3 * width :], late_sent[:, 3 * width :])
     late = jnp.concatenate([qkv_y[0], qkv_y[1], out_y], axis=1)
     late_other = swap(late, "c")
-    down_y = add_low(down_z, swap(down_z, "y"))
-    down_other = swap(down_y, "c")
-    up_done = ordered(y_at, up_z, swap(up_z, "y"), 1)
-    up_other = swap(up_done, "c")
 
     down_done, up_done, qkv_done, out_done = finish(
         c_at, dp, piece, (down_y, down_other), (up_done, up_other), (late, late_other), parts

time: 458 us -> 463 us (1.011)
  waiting for transfers between devices: 88.4 us -> 115 us
  starting transfers between devices: 53.9 us -> 34 us
  Pallas kernels: 210 us -> 224 us
  matrix products: 10.4 us -> 2.24 us
  other arithmetic: 39.6 us -> 31.6 us
    ppermute x3, starting transfers between devices: 21.3 us -> 4.45 us  [over_z(): lax.ppermute(parts[n], 'z', [(i, i ^ n) for i in range(depth)])]
    pallas_call x17 -> x18, Pallas kernels: 210 us -> 224 us  [call(): pl.pallas_call(kernel, grid_spec=pltpu.PrefetchScalarGridSpec(num_scalar_...]
    ppermute x41 -> x43, waiting for transfers between devices: 70.1 us -> 83.1 us  [swap(): return lax.ppermute(value, axis, [(0, 1), (1, 0)])]
    ppermute x3, waiting for transfers between devices: 13.2 us -> 22.7 us  [over_z(): lax.ppermute(parts[n], 'z', [(i, i ^ n) for i in range(depth)])]
    dot_general x3 -> x2, matrix products: 10.4 us -> 2.24 us  [dot(): lax.dot_general(left_op, right_op, (((left_dim,), (right_dim,)), ((), ())...]
    unnamed x98 -> x101, local copies, waits for them, and re-layouts: 13.1 us -> 16 us
    ppermute x41 -> x43, starting transfers between devices: 27.3 us -> 24.7 us  [swap(): return lax.ppermute(value, axis, [(0, 1), (1, 0)])]
  transfers between devices with their start and end apart: 49 -> 52, of which waited for: 18 -> 28; matrix products, arithmetic and copies ran while one was open for 15% -> 10% of each run, Pallas kernels for 27% -> 35%
where the time goes in v1:
time: 463 us; the launch traced here: 455 us
  Pallas kernels  224 us (48%)
  waiting for transfers between devices  115 us (25%)
  starting transfers between devices  34 us (7%)
  local copies, waits for them, and re-layouts  33 us (7%)
  other arithmetic  31.6 us (7%)
  between operations  15 us (3%)
    pallas_call x18, Pallas kernels, call(): pl.pallas_call(kernel, grid_spec=pltpu.PrefetchScalarGridSpec(num_scalar_...  224 us
    ppermute x43, waiting for transfers between devices, swap(): return lax.ppermute(value, axis, [(0, 1), (1, 0)])  83.1 us
    ppermute x43, starting transfers between devices, swap(): return lax.ppermute(value, axis, [(0, 1), (1, 0)])  24.7 us
    ppermute x3, waiting for transfers between devices, over_z(): lax.ppermute(parts[n], 'z', [(i, i ^ n) for i in range(depth)])  22.7 us
    unnamed x101, local copies, waits for them, and re-layouts  16 us
    convert_element_type x12, other arithmetic, add_low(): return (kept.astype(F32) + sent.astype(F32)).astype(BF16)  15.5 us
  transfers between devices with their start and end apart: 52, of which 28 were waited for; matrix products, arithmetic and copies ran while one was open for 10% of the time, Pallas kernels for 35%

profile of v1, /device:TPU:0, one launch (start us, length us, event | category | flops | bytes accessed | tf_op | source)
XLA Modules:
  0.0 454.5 jit_solution(10924436513293961481)
XLA Ops:
  31.3 15.8 %cot_down.1 = (bf16[1536,2048]{1,0:T(8,128)(2,1)}, bf16[1024,2048]{1,0:T(8,128)(2,1)}, bf16[2048,1024]{1,0:T(8,128)(2,1)}, bf16[1536,1024]{1,0:T(8,128)(2,1)}) custom-call(s32[8]{0:T(128)} %add.273.refs_0_, bf16[768,1024]{1,0:T(8,128)(2,1)} %bitcast.84, bf16[768,1024]{1,0:T(8,128)(2,1)} %collective-permute-done.5.refs_2_, bf16[1024,4096]{1,0:T(8,128)(2,1)} %refs_3_.3, ...), custom_call_target="tpu_custom_call" | custom-call | tf_op jit(solution)/shard_map/cot_down/pallas_call | solution.py:95
  48.3 7.4 %qkv.2 = (bf16[3,4,3,256,256]{4,3,2,1,0:T(8,128)(2,1)}, bf16[768,1024]{1,0:T(8,128)(2,1)}) custom-call(s32[1]{0:T(128)} %bitcast.2.refs_0_, bf16[3,256,1024]{2,1,0:T(8,128)(2,1)} %get-tuple-element.140.refs_1_, bf16[3,256,1024]{2,1,0:T(8,128)(2,1)} %copy-done.5, bf16[1024,3072]{1,0:T(8,128)(2,1)} %refs_3_.5, ...), custom_call_target="tpu_custom_call" | custom-call | tf_op jit(solution)/shard_map/qkv/pallas_call | solution.py:95
  55.7 6.9 %collective-permute-done.3.refs_1_.refs_3_ = bf16[3,256,1024]{2,1,0:T(8,128)(2,1)S(1)} collective-permute-done((bf16[3,256,1024]{2,1,0:T(8,128)(2,1)}, bf16[3,256,1024]{2,1,0:T(8,128)(2,1)S(1)}, u32[]{:S(2)}, u32[]{:S(2)}) %collective-permute-start.3) | collective-permute-done | bytes 1572896 | tf_op jit(solution)/shard_map/ppermute | solution.py:28
  67.1 7.4 %qkv.3 = (bf16[3,4,3,256,256]{4,3,2,1,0:T(8,128)(2,1)}, bf16[768,1024]{1,0:T(8,128)(2,1)}) custom-call(s32[1]{0:T(128)} %bitcast.2.refs_0_, bf16[3,256,1024]{2,1,0:T(8,128)(2,1)} %copy-done.6, bf16[3,256,1024]{2,1,0:T(8,128)(2,1)} %copy-done.7, bf16[1024,3072]{1,0:T(8,128)(2,1)} %refs_3_.5, ...), custom_call_target="tpu_custom_call", output_to_operand_aliasing={{0}: (7, {})} | custom-call | tf_op jit(solution)/shard_map/qkv/pallas_call | solution.py:95
  74.5 16.1 %attend.2 = (bf16[4,3,256,256]{3,2,1,0:T(8,128)(2,1)}, bf16[2,256,256]{2,1,0:T(8,128)(2,1)}, bf16[2,2,256,256]{3,2,1,0:T(8,128)(2,1)}, f32[3,4,8,256]{3,2,1,0:T(8,128)}) custom-call(s32[12]{0:T(128)} %reshape.319.refs_0_, s32[48]{0:T(128)} %reshape.320.refs_1_, bf16[3,4,3,256,256]{4,3,2,1,0:T(8,128)(2,1)} %get-tuple-element.145.refs_2_, s32[3,4,256]{2,1,0:T(4,128)} %copy-done.31), custom_call_target="tpu_custom_call" | custom-call | tf_op jit(solution)/shard_map/attend/pallas_call | solution.py:95
  90.9 8.2 %attend.3 = (bf16[4,3,256,256]{3,2,1,0:T(8,128)(2,1)}, bf16[1,256,256]{2,1,0:T(8,128)(2,1)}, bf16[2,1,256,256]{3,2,1,0:T(8,128)(2,1)}, f32[3,4,8,256]{3,2,1,0:T(8,128)}) custom-call(s32[12]{0:T(128)} %reshape.319.refs_0_, s32[48]{0:T(128)} %reshape.320.refs_1_, ...), custom_call_target="tpu_custom_call", output_to_operand_aliasing={{0}: (4, {}), {3}: (5, {})} | custom-call | tf_op jit(solution)/shard_map/attend/pallas_call | solution.py:95
  99.1 5.6 %collective-permute-done.7.refs_3_ = bf16[2,2,256,256]{3,2,1,0:T(8,128)(2,1)S(1)} collective-permute-done((bf16[2,2,256,256]{3,2,1,0:T(8,128)(2,1)}, bf16[2,2,256,256]{3,2,1,0:T(8,128)(2,1)S(1)}, u32[]{:S(2)}, u32[]{:S(2)}) %collective-permute-start.7) | collective-permute-done | bytes 524320 | tf_op jit(solution)/shard_map/ppermute | solution.py:28
  107.1 6.1 %middle.2 = (f32[3,256,1024]{2,1,0:T(8,128)}, bf16[2,256,1024]{2,1,0:T(8,128)(2,1)}, bf16[3,256,1024]{2,1,0:T(8,128)(2,1)}) custom-call(s32[4]{0:T(128)} %pad_add_fusion.2.refs_0_, bf16[4,3,256,256]{3,2,1,0:T(8,128)(2,1)} %get-tuple-element.156.refs_1_.refs_3_, bf16[2,256,256]{2,1,0:T(8,128)(2,1)} %copy-done.32, bf16[2,2,256,256]{3,2,1,0:T(8,128)(2,1)} %copy-done.18, ...), custom_call_target="tpu_custom_call" | custom-call | tf_op jit(solution)/shard_map/middle/pallas_call | solution.py:95
  116.9 4.8 %middle.3 = (f32[3,256,1024]{2,1,0:T(8,128)}, bf16[1,256,1024]{2,1,0:T(8,128)(2,1)}, bf16[3,256,1024]{2,1,0:T(8,128)(2,1)}) custom-call(s32[4]{0:T(128)} %pad_add_fusion.2.refs_0_, bf16[4,3,256,256]{3,2,1,0:T(8,128)(2,1)} %get-tuple-element.156.refs_1_.refs_3_, bf16[1,256,256]{2,1,0:T(8,128)(2,1)} %copy-done.35, ...), custom_call_target="tpu_custom_call", output_to_operand_aliasing={{0}: (11, {}), {2}: (12, {})} | custom-call | tf_op jit(solution)/shard_map/middle/pallas_call | solution.py:95
  124.9 29.0 %hidden.1 = (bf16[1536,2048]{1,0:T(8,128)(2,1)}, bf16[1536,2048]{1,0:T(8,128)(2,1)}, f32[1,2048]{1,0:T(1,128)}, bf16[1536,1024]{1,0:T(8,128)(2,1)}, bf16[1536,1024]{1,0:T(8,128)(2,1)}) custom-call(s32[8]{0:T(128)} %add.273.refs_0_, bf16[2,256,1024]{2,1,0:T(8,128)(2,1)} %get-tuple-element.154.refs_1_, bf16[1,256,1024]{2,1,0:T(8,128)(2,1)} %get-tuple-element.161.refs_2_, ...), custom_call_target="tpu_custom_call" | custom-call | tf_op jit(solution)/shard_map/hidden/pallas_call | solution.py:95
  160.0 9.8 %middle_back.1 = (f32[3,256,1024]{2,1,0:T(8,128)}, bf16[3,256,1024]{2,1,0:T(8,128)(2,1)}, bf16[3,256,256]{2,1,0:T(8,128)(2,1)}, bf16[3,256,256]{2,1,0:T(8,128)(2...) custom-call(s32[4]{0:T(128)} %pad_add_fusion.2.refs_0_, bf16[1536,1024]{1,0:T(8,128)(2,1)} %get-tuple-element.165.refs_1_, ...), custom_call_target="tpu_custom_call" | custom-call | tf_op jit(solution)/shard_map/middle_back/pallas_call | solution.py:95
  171.2 23.0 %sent_grads.1 = (bf16[1024,512]{1,0:T(8,128)(2,1)}, bf16[1024,512]{1,0:T(8,128)(2,1)}, bf16[1024,1024]{1,0:T(8,128)(2,1)}, bf16[512,1024]{1,0:T(8,128)(2,1)}, bf16[512,1024]{1,0:T(8,128)(2,1)}) custom-call(s32[1]{0:T(128)} %bitcast.14.refs_0_, bf16[1536,1024]{1,0:T(8,128)(2,1)} %get-tuple-element.174.refs_1_, ...), custom_call_target="tpu_custom_call" | custom-call | tf_op jit(solution)/shard_map/sent_grads/pallas_call | solution.py:95
  195.6 20.2 %kept_grads.1 = (bf16[1024,1024]{1,0:T(8,128)(2,1)}, bf16[1536,1024]{1,0:T(8,128)(2,1)}, bf16[1024,512]{1,0:T(8,128)(2,1)}, bf16[1024,512]{1,0:T(8,128)(2,1)}) custom-call(s32[5]{0:T(128)} %concatenate.66.refs_0_, bf16[1536,2048]{1,0:T(8,128)(2,1)} %get-tuple-element.168.refs_5_.refs_1_.refs_2_, ...), custom_call_target="tpu_custom_call" | custom-call | tf_op jit(solution)/shard_map/kept_grads/pallas_call | solution.py:95
  237.2 30.8 %attend_back.2 = (bf16[4,3,256,768]{3,2,1,0:T(8,128)(2,1)}, bf16[2,256,1024]{2,1,0:T(8,128)(2,1)}, bf16[2,256,1024]{2,1,0:T(8,128)(2,1)}, bf16[2,256,1024]{2,1,0:T(8,128)(2,1)}, bf16[2,256,1024]{2,1,0:T(8,128)(2,1)}) custom-call(s32[12]{0:T(128)} %reshape.319.refs_0_, s32[48]{0:T(128)} %reshape.320.refs_1_, ...), custom_call_target="tpu_custom_call" | custom-call | tf_op jit(solution)/shard_map/attend_back/pallas_call | solution.py:95
  274.3 23.9 %collective-permute-done.24 = bf16[1024,512]{1,0:T(8,128)(2,1)} collective-permute-done((bf16[1024,512]{1,0:T(8,128)(2,1)S(1)}, bf16[1024,512]{1,0:T(8,128)(2,1)}, u32[]{:S(2)}, u32[]{:S(2)}) %collective-permute-start.24) | collective-permute-done | bytes 1048608 | tf_op jit(solution)/shard_map/ppermute | solution.py:28
  305.9 15.7 %attend_back.3 = (bf16[4,3,256,768]{3,2,1,0:T(8,128)(2,1)}, bf16[1,256,1024]{2,1,0:T(8,128)(2,1)}, bf16[1,256,1024]{2,1,0:T(8,128)(2,1)}, bf16[1,256,1024]{2,1,0:T(8,128)(2,1)}, bf16[1,256,1024]{2,1,0:T(8,128)(2,1)}) custom-call(s32[12]{0:T(128)} %reshape.319.refs_0_, s32[48]{0:T(128)} %reshape.320.refs_1_, ...), custom_call_target="tpu_custom_call", output_to_operand_aliasing={{0}: (13, {})} | custom-call | tf_op jit(solution)/shard_map/attend_back/pallas_call | solution.py:95
  330.1 10.5 %qkv_grads.1 = (bf16[4,128,768]{2,1,0:T(8,128)(2,1)}, bf16[4,128,768]{2,1,0:T(8,128)(2,1)}, f32[1,768]{1,0:T(1,128)}) custom-call(s32[1]{0:T(128)} %bitcast.8.refs_0_, bf16[3,256,1024]{2,1,0:T(8,128)(2,1)} %get-tuple-element.140.refs_1_, bf16[3,256,1024]{2,1,0:T(8,128)(2,1)} %copy-done.5, bf16[3,256,1024]{2,1,0:T(8,128)(2,1)} %copy-done.6, ...), custom_call_target="tpu_custom_call" | custom-call | tf_op jit(solution)/shard_map/qkv_grads/pallas_call | solution.py:95
  346.5 5.8 %norm1_back.2 = (bf16[3,256,1024]{2,1,0:T(8,128)(2,1)}, f32[2,8,1024]{2,1,0:T(8,128)}, f32[8,1024]{1,0:T(8,128)}) custom-call(bf16[2,256,1024]{2,1,0:T(8,128)(2,1)} %get-tuple-element.217.refs_0_, bf16[2,256,1024]{2,1,0:T(8,128)(2,1)} %collective-permute-done.31.refs_1_, bf16[2,256,1024]{2,1,0:T(8,128)(2,1)} %collective-permute-done.28.refs_2_, ...), custom_call_target="tpu_custom_call" | custom-call | tf_op jit(solution)/shard_map/norm1_back/pallas_call | solution.py:95
  368.0 8.1 %collective-permute-done.45 = bf16[128,768]{1,0:T(8,128)(2,1)S(1)} collective-permute-done((bf16[128,768]{1,0:T(8,128)(2,1)S(1)}, bf16[128,768]{1,0:T(8,128)(2,1)S(1)}, u32[]{:S(2)}, u32[]{:S(2)}) %collective-permute-start.45) | collective-permute-done | bytes 196640 | tf_op jit(solution)/shard_map/ppermute | solution.py:808
  376.1 14.6 %collective-permute-done.44 = bf16[128,768]{1,0:T(8,128)(2,1)S(1)} collective-permute-done((bf16[128,768]{1,0:T(8,128)(2,1)S(1)}, bf16[128,768]{1,0:T(8,128)(2,1)S(1)}, u32[]{:S(2)}, u32[]{:S(2)}) %collective-permute-start.44) | collective-permute-done | bytes 196640 | tf_op jit(solution)/shard_map/ppermute | solution.py:808
  392.5 8.1 %collective-permute-done.47 = bf16[128,1280]{1,0:T(8,128)(2,1)S(1)} collective-permute-done((bf16[128,1280]{1,0:T(8,128)(2,1)S(1)}, bf16[128,1280]{1,0:T(8,128)(2,1)S(1)}, u32[]{:S(2)}, u32[]{:S(2)}) %collective-permute-start.47) | collective-permute-done | bytes 327712 | tf_op jit(solution)/shard_map/ppermute | solution.py:28
  406.7 7.2 %collective-permute-done.36 = bf16[256,1024]{1,0:T(8,128)(2,1)S(1)} collective-permute-done((bf16[256,1024]{1,0:T(8,128)(2,1)}, bf16[256,1024]{1,0:T(8,128)(2,1)S(1)}, u32[]{:S(2)}, u32[]{:S(2)}) %collective-permute-start.36) | collective-permute-done | bytes 524320 | tf_op jit(solution)/shard_map/ppermute | solution.py:28
  424.2 4.9 %collective-permute-done.38 = bf16[2,38,1024]{2,1,0:T(8,128)(2,1)S(1)} collective-permute-done((bf16[2,38,1024]{2,1,0:T(8,128)(2,1)S(1)}, bf16[2,38,1024]{2,1,0:T(8,128)(2,1)S(1)}, u32[]{:S(2)}, u32[]{:S(2)}) %collective-permute-start.38) | collective-permute-done | bytes 155680 | tf_op jit(solution)/shard_map/ppermute | solution.py:1035
  442.9 4.7 %finish.1 = (f32[512,1024]{1,0:T(8,128)}, f32[128,4096]{1,0:T(8,128)}, f32[128,3072]{1,0:T(8,128)}, f32[128,1024]{1,0:T(8,128)}) custom-call(s32[1]{0:T(128)} %bitcast.6.refs_0_, bf16[256,1024]{1,0:T(8,128)(2,1)} %copy-done.12, bf16[256,1024]{1,0:T(8,128)(2,1)} %copy-done.29, bf16[128,2048]{1,0:T(8,128)(2,1)} %copy-done.14, ...), custom_call_target="tpu_custom_call" | custom-call | tf_op jit(solution)/shard_map/finish/pallas_call | solution.py:95
  (312 shorter events, 145.0 us)
Async XLA Ops:
  7.2 334.1 %reduce-scatter.4.cloned.1.call-start = ((), (), s32[]{:S(2)}) async-start(), calls=%async_computation.3 | async-start | bytes 1310720 | tf_op jit(solution)/shard_map/reduce_scatter | solution.py:981
  10.3 15.1 %collective-permute-start = (s32[3,256]{1,0:T(4,128)}, s32[3,256]{1,0:T(4,128)S(1)}, u32[]{:S(2)}, u32[]{:S(2)}) collective-permute-start(s32[3,256]{1,0:T(4,128)} %refs_6_.9), channel_id=1, source_target_pairs={{0,1},{1,0},{2,3},{3,2},{4,5},{5,4},{6,7},{7,6},{8,9},{9,8},{10,11... | collective-permute-start | bytes 9224 | tf_op jit(solution)/shard_map/ppermute | solution.py:28
  10.3 21.0 %collective-permute-start.5 = (bf16[768,1024]{1,0:T(8,128)(2,1)}, bf16[768,1024]{1,0:T(8,128)(2,1)}, u32[]{:S(2)}, u32[]{:S(2)}) collective-permute-start(bf16[768,1024]{1,0:T(8,128)(2,1)} %bitcast.83), channel_id=1, source_target_pairs={{0,1},{1,0},{2,3},{3,2},{4,5},{5,4},{6,7},{7,6},{8,9},{9,8},{10,11... | collective-permute-start | bytes 4718600 | tf_op jit(solution)/shard_map/ppermute | solution.py:28
  25.4 21.7 %collective-permute-start.4 = (bf16[3,256,1024]{2,1,0:T(8,128)(2,1)}, bf16[3,256,1024]{2,1,0:T(8,128)(2,1)S(1)}, u32[]{:S(2)}, u32[]{:S(2)}) collective-permute-start(bf16[3,256,1024]{2,1,0:T(8,128)(2,1)} %get-tuple-element.140.refs_1_), channel_id=1, source_target_pairs={{0,1},{1,0},{2,3},{3,2},{4,5},{5,4},{6,7},{7,6},{8,9},{9,8},{10,11... | collective-permute-start | bytes 4718600 | tf_op jit(solution)/shard_map/ppermute | solution.py:28
  26.0 36.6 %collective-permute-start.3 = (bf16[3,256,1024]{2,1,0:T(8,128)(2,1)}, bf16[3,256,1024]{2,1,0:T(8,128)(2,1)S(1)}, u32[]{:S(2)}, u32[]{:S(2)}) collective-permute-start(bf16[3,256,1024]{2,1,0:T(8,128)(2,1)} %get-tuple-element.140.refs_1_), channel_id=1, source_target_pairs={{0,2},{2,0},{1,3},{3,1},{4,6},{6,4},{5,7},{7,5},{8,10},{10,8},{9,1... | collective-permute-start | bytes 4718600 | tf_op jit(solution)/shard_map/ppermute | solution.py:28
  169.8 24.4 %collective-permute-start.16 = (bf16[2,3,256,256]{3,2,1,0:T(8,128)(2,1)}, bf16[2,3,256,256]{3,2,1,0:T(8,128)(2,1)S(1)}, u32[]{:S(2)}, u32[]{:S(2)}) collective-permute-start(bf16[2,3,256,256]{3,2,1,0:T(8,128)(2,1)} %get-tuple-element.178), channel_id=1, source_target_pairs={{0,2},{2,0},{1,3},{3,1},{4,6},{6,4},{5,7},{7,5},{8,10},{10,8},{9,1... | collective-permute-start | bytes 2359304 | tf_op jit(solution)/shard_map/ppermute | solution.py:28
  194.2 25.2 %collective-permute-start.17 = (bf16[1024,512]{1,0:T(8,128)(2,1)}, bf16[1024,512]{1,0:T(8,128)(2,1)S(1)}, u32[]{:S(2)}, u32[]{:S(2)}) collective-permute-start(bf16[1024,512]{1,0:T(8,128)(2,1)} %get-tuple-element.183), channel_id=1, source_target_pairs={{0,2},{2,0},{1,3},{3,1},{4,6},{6,4},{5,7},{7,5},{8,10},{10,8},{9,1... | collective-permute-start | bytes 3145736 | tf_op jit(solution)/shard_map/ppermute | solution.py:28
  194.9 24.9 %collective-permute-start.18 = (bf16[512,1024]{1,0:T(8,128)(2,1)}, bf16[512,1024]{1,0:T(8,128)(2,1)S(1)}, u32[]{:S(2)}, u32[]{:S(2)}) collective-permute-start(bf16[512,1024]{1,0:T(8,128)(2,1)} %get-tuple-element.179.refs_7_), channel_id=1, source_target_pairs={{0,4},{4,0},{1,5},{5,1},{2,6},{6,2},{3,7},{7,3},{8,12},{12,8},{9,1... | collective-permute-start | bytes 3145736 | tf_op jit(solution)/shard_map/ppermute | solution.py:28
  233.7 166.9 %reduce-scatter.6.cloned.1.call-start = ((), (), s32[]{:S(2)}) async-start(), calls=%async_computation.4 | async-start | bytes 2621440 | tf_op jit(solution)/shard_map/reduce_scatter | solution.py:993
  233.8 34.2 %collective-permute-start.25 = (bf16[512,1024]{1,0:T(8,128)(2,1)}, bf16[512,1024]{1,0:T(8,128)(2,1)}, u32[]{:S(2)}, u32[]{:S(2)}) collective-permute-start(bf16[512,1024]{1,0:T(8,128)(2,1)} %get-tuple-element.208), channel_id=1, source_target_pairs={{0,4},{4,0},{1,5},{5,1},{2,6},{6,2},{3,7},{7,3},{8,12},{12,8},{9,1... | collective-permute-start | bytes 3145736 | tf_op jit(solution)/shard_map/ppermute | solution.py:28
  271.6 157.8 %reduce-scatter.8.cloned.1.call-start = ((), (), s32[]{:S(2)}) async-start(), calls=%async_computation.5 | async-start | bytes 1310720 | tf_op jit(solution)/shard_map/reduce_scatter | solution.py:1008
  272.8 25.3 %collective-permute-start.24 = (bf16[1024,512]{1,0:T(8,128)(2,1)S(1)}, bf16[1024,512]{1,0:T(8,128)(2,1)}, u32[]{:S(2)}, u32[]{:S(2)}) collective-permute-start(bf16[1024,512]{1,0:T(8,128)(2,1)S(1)} %copy-done.41), channel_id=1, source_target_pairs={{0,2},{2,0},{1,3},{3,1},{4,6},{6,4},{5,7},{7,5},{8,10},{10,8},{9,1... | collective-permute-start | bytes 3145736 | tf_op jit(solution)/shard_map/ppermute | solution.py:28
  274.2 27.8 %collective-permute-start.23 = (bf16[2,256,1024]{2,1,0:T(8,128)(2,1)}, bf16[2,256,1024]{2,1,0:T(8,128)(2,1)}, u32[]{:S(2)}, u32[]{:S(2)}) collective-permute-start(bf16[2,256,1024]{2,1,0:T(8,128)(2,1)} %get-tuple-element.198), channel_id=1, source_target_pairs={{0,1},{1,0},{2,3},{3,2},{4,5},{5,4},{6,7},{7,6},{8,9},{9,8},{10,11... | collective-permute-start | bytes 3145736 | tf_op jit(solution)/shard_map/ppermute | solution.py:28
  302.0 24.7 %collective-permute-start.29 = (bf16[4,128,1024]{2,1,0:T(8,128)(2,1)}, bf16[4,128,1024]{2,1,0:T(8,128)(2,1)}, u32[]{:S(2)}, u32[]{:S(2)}) collective-permute-start(bf16[4,128,1024]{2,1,0:T(8,128)(2,1)} %constant_dynamic-slice_fusion.11.refs_16_), channel_id=1, source_target_pairs={{0,4},{4,0},{1,5},{5,1},{2,6},{6,2},{3,7},{7,3},{8,12},{12,8},{9,1... | collective-permute-start | bytes 3145736 | tf_op jit(solution)/shard_map/ppermute | solution.py:28
  304.2 24.5 %collective-permute-start.28 = (bf16[2,256,1024]{2,1,0:T(8,128)(2,1)S(1)}, bf16[2,256,1024]{2,1,0:T(8,128)(2,1)}, u32[]{:S(2)}, u32[]{:S(2)}) collective-permute-start(bf16[2,256,1024]{2,1,0:T(8,128)(2,1)S(1)} %add_convert_fusion.4.refs_14_), channel_id=1, source_target_pairs={{0,2},{2,0},{1,3},{3,1},{4,6},{6,4},{5,7},{7,5},{8,10},{10,8},{9,1... | collective-permute-start | bytes 3145736 | tf_op jit(solution)/shard_map/ppermute | solution.py:28
  322.8 23.7 %collective-permute-start.31 = (bf16[2,256,1024]{2,1,0:T(8,128)(2,1)}, bf16[2,256,1024]{2,1,0:T(8,128)(2,1)}, u32[]{:S(2)}, u32[]{:S(2)}) collective-permute-start(bf16[2,256,1024]{2,1,0:T(8,128)(2,1)} %get-tuple-element.218), channel_id=1, source_target_pairs={{0,1},{1,0},{2,3},{3,2},{4,5},{5,4},{6,7},{7,6},{8,9},{9,8},{10,11... | collective-permute-start | bytes 3145736 | tf_op jit(solution)/shard_map/ppermute | solution.py:28
  323.5 28.9 %collective-permute-start.26 = (bf16[1,256,1024]{2,1,0:T(8,128)(2,1)}, bf16[1,256,1024]{2,1,0:T(8,128)(2,1)}, u32[]{:S(2)}, u32[]{:S(2)}) collective-permute-start(bf16[1,256,1024]{2,1,0:T(8,128)(2,1)} %get-tuple-element.211), channel_id=1, source_target_pairs={{0,1},{1,0},{2,3},{3,2},{4,5},{5,4},{6,7},{7,6},{8,9},{9,8},{10,11... | collective-permute-start | bytes 1572872 | tf_op jit(solution)/shard_map/ppermute | solution.py:28
  328.7 23.6 %collective-permute-start.30 = (bf16[1,256,1024]{2,1,0:T(8,128)(2,1)}, bf16[1,256,1024]{2,1,0:T(8,128)(2,1)S(1)}, u32[]{:S(2)}, u32[]{:S(2)}) collective-permute-start(bf16[1,256,1024]{2,1,0:T(8,128)(2,1)} %add_convert_fusion.8), channel_id=1, source_target_pairs={{0,2},{2,0},{1,3},{3,1},{4,6},{6,4},{5,7},{7,5},{8,10},{10,8},{9,1... | collective-permute-start | bytes 1572872 | tf_op jit(solution)/shard_map/ppermute | solution.py:28
  341.4 20.7 %collective-permute-start.33 = (bf16[4,128,768]{2,1,0:T(8,128)(2,1)}, bf16[4,128,768]{2,1,0:T(8,128)(2,1)S(1)}, u32[]{:S(2)}, u32[]{:S(2)}) collective-permute-start(bf16[4,128,768]{2,1,0:T(8,128)(2,1)} %get-tuple-element.238), channel_id=1, source_target_pairs={{0,4},{4,0},{1,5},{5,1},{2,6},{6,2},{3,7},{7,3},{8,12},{12,8},{9,1... | collective-permute-start | bytes 2359304 | tf_op jit(solution)/shard_map/ppermute | solution.py:28
  366.0 24.8 %collective-permute-start.44 = (bf16[128,768]{1,0:T(8,128)(2,1)S(1)}, bf16[128,768]{1,0:T(8,128)(2,1)S(1)}, u32[]{:S(2)}, u32[]{:S(2)}) collective-permute-start(bf16[128,768]{1,0:T(8,128)(2,1)S(1)} %get-tuple-element.258), channel_id=1, source_target_pairs={{0,16},{8,24},{16,0},{24,8},{1,17},{9,25},{17,1},{25,9},{2,18},{10... | collective-permute-start | bytes 589832 | tf_op jit(solution)/shard_map/ppermute | solution.py:808
  366.0 24.8 %collective-permute-start.43 = (bf16[128,768]{1,0:T(8,128)(2,1)S(1)}, bf16[128,768]{1,0:T(8,128)(2,1)S(1)}, u32[]{:S(2)}, u32[]{:S(2)}) collective-permute-start(bf16[128,768]{1,0:T(8,128)(2,1)S(1)} %get-tuple-element.256), channel_id=1, source_target_pairs={{0,8},{8,0},{16,24},{24,16},{1,9},{9,1},{17,25},{25,17},{2,10},{10... | collective-permute-start | bytes 589832 | tf_op jit(solution)/shard_map/ppermute | solution.py:808
  366.8 25.7 %collective-permute-start.34 = (bf16[38,1024]{1,0:T(8,128)(2,1)S(1)}, bf16[38,1024]{1,0:T(8,128)(2,1)S(1)}, u32[]{:S(2)}, u32[]{:S(2)}) collective-permute-start(bf16[38,1024]{1,0:T(8,128)(2,1)S(1)} %add_convert_fusion.12), channel_id=1, source_target_pairs={{0,2},{2,0},{1,3},{3,1},{4,6},{6,4},{5,7},{7,5},{8,10},{10,8},{9,1... | collective-permute-start | bytes 233480 | tf_op jit(solution)/shard_map/ppermute | solution.py:28
  419.7 22.1 %collective-permute-start.48 = (bf16[128,2048]{1,0:T(8,128)(2,1)S(1)}, bf16[128,2048]{1,0:T(8,128)(2,1)S(1)}, u32[]{:S(2)}, u32[]{:S(2)}) collective-permute-start(bf16[128,2048]{1,0:T(8,128)(2,1)S(1)} %pad_maximum_fusion.4.refs_5_), channel_id=1, source_target_pairs={{0,1},{1,0},{2,3},{3,2},{4,5},{5,4},{6,7},{7,6},{8,9},{9,8},{10,11... | collective-permute-start | bytes 1572872 | tf_op jit(solution)/shard_map/ppermute | solution.py:28
  419.8 22.0 %collective-permute-start.40 = (bf16[256,1024]{1,0:T(8,128)(2,1)S(1)}, bf16[256,1024]{1,0:T(8,128)(2,1)S(1)}, u32[]{:S(2)}, u32[]{:S(2)}) collective-permute-start(bf16[256,1024]{1,0:T(8,128)(2,1)S(1)} %add_convert_fusion.7.refs_1_), channel_id=1, source_target_pairs={{0,1},{1,0},{2,3},{3,2},{4,5},{5,4},{6,7},{7,6},{8,9},{9,8},{10,11... | collective-permute-start | bytes 1572872 | tf_op jit(solution)/shard_map/ppermute | solution.py:28
  (73 other events, 490.3 us)
Sparse Core Ops, SparseCore 0:
  233.9 28.2 reduce-scatter.3
  271.7 46.8 reduce-scatter.5
  346.6 35.7 reduce-scatter.7

commit v2 on v1

--- a/solution.py
+++ b/solution.py
@@ -21,7 +21,6 @@
 GELU_B = GELU_A * 0.044715
 BLOCK = 256
 VMEM = 60 * 1024 * 1024
-TIME_BIAS, GAIN1, BIAS1, OUT_BIAS, GAIN2, BIAS2, DOWN_BIAS, QKV_BIAS, UP_BIAS = (slice(n, n + 1) for n in (0, 1, 2, 3, 4, 5, 6, 7, 10))
 
 
 def swap(value, axis):
@@ -108,6 +107,10 @@
     )(*prefetch, *[array for array, _ in ins], *extra)
 
 
+def line(ref):
+    return ref[...].astype(F32).reshape(1, -1)
+
+
 def fixed(shape):
     return pl.BlockSpec(shape, lambda *_: (0,) * len(shape))
 
@@ -116,16 +119,16 @@
     return pl.BlockSpec(shape, lambda g, *_: tuple(start + g if n == axis else 0 for n in range(len(shape))))
 
 
-def norm1_body(x_ref, seg_ref, shift_ref, vec_ref, stream_ref, low_ref):
+def norm1_body(x_ref, seg_ref, shift_ref, time_ref, gain_ref, bias_ref, stream_ref, low_ref):
     seg = seg_ref[pl.ds(pl.program_id(0), 1)]
     slots = lax.broadcasted_iota(jnp.int32, (SEGS, seg.shape[-1]), 0) == seg
     onehot = slots.astype(F32).astype(BF16)
-    shift = shift_ref[0] + vec_ref[TIME_BIAS]
+    shift = shift_ref[0] + line(time_ref)
     added = dot(jnp.concatenate([onehot, onehot], axis=0), split_low(shift), 0, 0)
     stream = x_ref[0].astype(F32) + added
     hat, _ = centre(stream)
     stream_ref[0] = stream
-    low_ref[0] = (hat * vec_ref[GAIN1] + vec_ref[BIAS1]).astype(BF16)
+    low_ref[0] = (hat * line(gain_ref) + line(bias_ref)).astype(BF16)
 
 
 def norm1(x, seg, shift, vecs):
@@ -133,12 +136,13 @@
     block = along((1, shard, model))
     return call(
         norm1_body, "norm1", (), (rows,),
-        [(x, block), (seg, fixed(seg.shape)), (shift, along((1, SEGS, model))), (vecs, fixed(vecs.shape))],
+        [(x, block), (seg, fixed(seg.shape)), (shift, along((1, SEGS, model)))]
+        + [(vec, fixed(vec.shape)) for vec in vecs],
         [(x.shape, F32, block), (x.shape, BF16, block)],
     )
 
 
-def qkv_body(me_ref, a_ref, b_ref, w_ref, vec_ref, cos_ref, sin_ref, out_ref, own_ref):
+def qkv_body(me_ref, a_ref, b_ref, w_ref, bias_ref, cos_ref, sin_ref, out_ref, own_ref):
     rows, shard, model = a_ref.shape
     width = w_ref.shape[1]
     places = [(n, r) for n in range(2) for r in range(rows)]
@@ -146,7 +150,7 @@
 
     def run(turned):
         w = w_ref[...]
-        bias = vec_ref[pl.ds(QKV_BIAS.start + step, 1), pl.ds(pl.multiple_of(me_ref[0] * width, width), width)]
+        bias = bias_ref[...].astype(F32)
         later = dot(a_ref[0], w)
         for at, (n, r) in enumerate(places):
             values = later + bias
@@ -168,7 +172,7 @@
         run(False)
 
 
-def project_qkv(pair, parts, me, first, second, weight, vecs, cos_tab, sin_tab, held=(), deps=()):
+def project_qkv(pair, parts, me, first, second, weight, bias, cos_tab, sin_tab, held=(), deps=()):
     rows, shard, model = first.shape
     width = model // parts
     return call(
@@ -176,7 +180,7 @@
         [(first, fixed(first.shape)), (second, fixed(first.shape))]
         + [
             (weight, pl.BlockSpec((model, width), lambda g, m: (0, g * parts + m[0]))),
-            (vecs, fixed(vecs.shape)),
+            (bias, pl.BlockSpec((1, width), lambda g, m: (0, g * parts + m[0]))),
             (cos_tab, pl.BlockSpec((2, shard, 128), lambda g, m: (pair, 0, 0))),
             (sin_tab, pl.BlockSpec((2, shard, 128), lambda g, m: (pair, 0, 0))),
         ],
@@ -441,7 +445,7 @@
 
 
 def middle_body(
-    order_ref, a0, a1, a2, a3, w0, w1, w2, w3, stream_ref, vec_ref, mid_ref, low_ref, all_ref,
+    order_ref, a0, a1, a2, a3, w0, w1, w2, w3, stream_ref, bias_ref, gain_ref, shift_ref, mid_ref, low_ref, all_ref,
 ):
     _, shard, model = stream_ref.shape
     total = 0.0
@@ -449,10 +453,10 @@
         values = a[...].reshape(shard, a.shape[-1])
         total = total + dot(values, w[...])
         all_ref[0, :, n * a.shape[-1] : (n + 1) * a.shape[-1]] = values
-    mid = stream_ref[0] + (total + vec_ref[OUT_BIAS])
+    mid = stream_ref[0] + (total + line(bias_ref))
     hat, _ = centre(mid)
     mid_ref[0] = mid
-    low_ref[0] = (hat * vec_ref[GAIN2] + vec_ref[BIAS2]).astype(BF16)
+    low_ref[0] = (hat * line(gain_ref) + line(shift_ref)).astype(BF16)
 
 
 def out_blocks(weight, parts):
@@ -472,7 +476,8 @@
     first = [along((1, 1, shard, width), 1, start), one, along((1, 1, shard, width), 1), one]
     return call(
         middle_body, "middle", (order,), (count,),
-        list(zip(attended, first)) + out_blocks(weight, parts) + [(stream, block), (vecs, fixed(vecs.shape))],
+        list(zip(attended, first)) + out_blocks(weight, parts) + [(stream, block)]
+        + [(vec, fixed(vec.shape)) for vec in vecs],
         [
             (stream.shape, F32, block),
             ((count, shard, model), BF16, along((1, shard, model))),
@@ -533,12 +538,7 @@
     @pl.when(step < blocks)
     def _():
         up = up_ref[...]
-        if bias_ref.shape[1] == BLOCK:
-            bias = bias_ref[...]
-        else:
-            per = bias_ref.shape[1] // BLOCK
-            at = pl.multiple_of(blk_ref[step] % per * BLOCK, BLOCK)
-            bias = bias_ref[pl.ds(UP_BIAS.start + blk_ref[step] // per, 1), pl.ds(at, BLOCK)]
+        bias = bias_ref[...].astype(F32)
         total = 0.0
         later = dot(pieces[0][...].reshape(sizes[0], -1), up)
         for n, (start, size) in enumerate(zip(starts, sizes)):
@@ -584,7 +584,7 @@
             (grads, column),
             (up, pl.BlockSpec((model, BLOCK), lambda g, b: (0, first(g)))),
             (up, pl.BlockSpec((BLOCK, half), lambda g, b: (second(g), 0))),
-            (bias, line if bias.shape[0] == 1 else fixed(bias.shape)),
+            (bias, pl.BlockSpec((1, BLOCK), lambda g, b: (0, b[first(g)]))),
         ],
         [
             (grads.shape, BF16, column),
@@ -597,59 +597,46 @@
     )
 
 
-def sent_body(half_ref, both_ref, cot_ref, out_ref, keep_ref, act_ref, up0, up1, up_keep, down0, down1):
-    both = both_ref[...]
+def both_body(cot_ref, grad_ref, act_ref, tok_ref, out_ref):
+    half, rows, model = out_ref.shape[1], out_ref.shape[3], out_ref.shape[4]
+    size = act_ref.shape[1] // (2 * half)
+    rest = tok_ref.shape[1] // (2 * half)
     down = dot(act_ref[...], cot_ref[...], 0, 0).astype(BF16)
-    up = dot(both, out_ref[...], 0, 0).astype(BF16)
-
-    @pl.when(2 * pl.program_id(0) < pl.num_programs(0))
-    def _():
-        down0[...] = down
-        up0[...] = up
-
-    @pl.when(2 * pl.program_id(0) >= pl.num_programs(0))
-    def _():
-        down1[...] = down
-        up1[...] = up
-
-    up_keep[...] = dot(both, keep_ref[...], 0, 0).astype(BF16)
-
-
-def sent_grads(kept, both, cot, grad, act):
-    tokens, model = both.shape
-    half = grad.shape[1] // 2
-    steps = half // BLOCK
-    cut = steps // 2
-
-    def first(g):
-        return jnp.minimum(g, cut - 1)
-
-    def second(g):
-        return jnp.maximum(g - cut, 0)
-
-    return call(
-        sent_body, "sent_grads", (kept,), (steps,),
-        [
-            (both, fixed(both.shape)),
+    up = dot(tok_ref[...], grad_ref[...], 0, 0).astype(BF16)
+    for x in range(2):
+        for y in range(half):
+            n = half * x + y
+            out_ref[x, y, 0, 0:size] = down[n * size : (n + 1) * size]
+            for s in range(2):
+                at = size + s * rest
+                out_ref[x, y, 0, at : at + rest] = up[n * rest : (n + 1) * rest, s * model : (s + 1) * model]
+
+
+def both_grads(act, cot, tokens, grad, depth):
+    count, half = act.shape
+    model = cot.shape[1]
+    size, rest = half // (4 * depth), model // (4 * depth)
+    shape = (2, 2, depth, size + 2 * rest, model)
+    if rest % 16 or size % 16:
+        down = dot(act, cot, 0, 0).astype(BF16).reshape(depth, 2, 2, size, model)
+        up = dot(tokens, grad, 0, 0).astype(BF16).reshape(depth, 2, 2, rest, 2, model)
+        up = up.transpose(0, 1, 2, 4, 3, 5).reshape(depth, 2, 2, 2 * rest, model)
+        return jnp.concatenate([down, up], axis=3).transpose(1, 2, 0, 3, 4)
+    return call(
+        both_body, "both_grads", (), (depth,),
+        [
             (cot, fixed(cot.shape)),
-            (grad, pl.BlockSpec((tokens, BLOCK), lambda g, k: (0, (1 - k[0]) * steps + g))),
-            (grad, pl.BlockSpec((tokens, BLOCK), lambda g, k: (0, k[0] * steps + g))),
-            (act, along((tokens, BLOCK), 1)),
-        ],
-        [
-            ((model, half // 2), BF16, pl.BlockSpec((model, BLOCK), lambda g, k: (0, first(g)))),
-            ((model, half // 2), BF16, pl.BlockSpec((model, BLOCK), lambda g, k: (0, second(g)))),
-            ((model, half), BF16, along((model, BLOCK), 1)),
-            ((half // 2, model), BF16, pl.BlockSpec((BLOCK, model), lambda g, k: (first(g), 0))),
-            ((half // 2, model), BF16, pl.BlockSpec((BLOCK, model), lambda g, k: (second(g), 0))),
-        ],
-    )
-
-
-def kept_body(order_ref, act_ref, half_ref, cot_ref, down_ref, att_ref, low_ref, kept_ref, feed_ref, out_ref, keep_ref):
+            (grad, fixed(grad.shape)),
+            (act, along((count, half // depth), 1)),
+            (tokens, along((count, model // depth), 1)),
+        ],
+        [(shape, BF16, along((2, 2, 1) + shape[3:], 2))],
+    )[0]
+
+
+def feed_body(order_ref, act_ref, down_ref, att_ref, low_ref, feed_ref, out_ref, keep_ref):
     parts = order_ref.shape[0]
     width = att_ref.shape[1] // parts
-    kept_ref[...] = dot(half_ref[...], cot_ref[...], 0, 0).astype(BF16)
     feed_ref[...] = dot(act_ref[...], down_ref[...]).astype(BF16)
     grad = dot(att_ref[...], low_ref[...], 0, 0).astype(BF16)
     step, steps = pl.program_id(0), pl.num_programs(0)
@@ -668,16 +655,14 @@
         write(keep_ref)
 
 
-def kept_grads(order, act, cot, down, attended, low, c_at, deps=()):
+def feed_grads(order, act, down, attended, low, c_at, deps=()):
     tokens, half = act.shape
-    model = cot.shape[1]
+    own, model = attended.shape
     steps = model // BLOCK
-    rows = half // (2 * steps)
-    own = attended.shape[0]
     place = jnp.concatenate([order, c_at.astype(jnp.int32)[None]])
 
     def body(place_ref, *refs):
-        kept_body(place_ref.at[0 : order.shape[0]], *refs)
+        feed_body(place_ref.at[0 : order.shape[0]], *refs)
 
     def low_at(g, p):
         c = p[order.shape[0]]
@@ -685,17 +670,14 @@
         return 0, jnp.where(mine, c * (steps // 2) + g - steps // 2, (1 - c) * (steps // 2) + g)
 
     return call(
-        body, "kept_grads", (place,), (steps,),
+        body, "feed_grads", (place,), (steps,),
         [
             (act, fixed(act.shape)),
-            (act, along((tokens, rows), 1, steps)),
-            (cot, fixed(cot.shape)),
             (down, along((half, BLOCK), 1)),
             (attended, fixed(attended.shape)),
             (low, pl.BlockSpec((own, BLOCK), low_at)),
         ],
         [
-            ((half // 2, model), BF16, along((rows, model))),
             ((tokens, model), BF16, along((tokens, BLOCK), 1)),
             ((model, model // 2), BF16, pl.BlockSpec((model, BLOCK), lambda g, p: (0, jnp.minimum(g, steps // 2 - 1)))),
             ((model, model // 2), BF16, pl.BlockSpec((model, BLOCK), lambda g, p: (0, jnp.maximum(g - steps // 2, 0)))),
@@ -705,13 +687,13 @@
 
 
 def middle_back_body(
-    order_ref, part_ref, sent_ref, mid_ref, cot_ref, vec_ref, w0, w1, w2, w3,
+    order_ref, part_ref, sent_ref, mid_ref, cot_ref, gain_ref, w0, w1, w2, w3,
     grad_ref, low_ref, att0_ref, att1_ref, far_ref, sums_ref,
 ):
     grad = part_ref[...].astype(F32) + sent_ref[...].astype(F32)
     hat, inverse = centre(mid_ref[0])
     cot = cot_ref[0].astype(F32)
-    total = cot + norm_back(grad, vec_ref[GAIN2], hat, inverse)
+    total = cot + norm_back(grad, line(gain_ref), hat, inverse)
     low = total.astype(BF16)
     grad_ref[0] = total
     low_ref[0] = low
@@ -730,14 +712,14 @@
     sums_ref[3:4] += jnp.sum(cot, axis=0, keepdims=True)
 
 
-def middle_back(order, both, sent, mid, cot, vecs, weight, parts, deps=()):
+def middle_back(order, both, sent, mid, cot, gain, weight, parts, deps=()):
     rows, shard, model = mid.shape
     width = model // parts
     block, one = along((1, shard, model)), along((1, shard, width))
     flat = pl.BlockSpec((shard, model), lambda g, o: (g, 0))
     return call(
         middle_back_body, "middle_back", (order,), (rows,),
-        [(both, flat), (sent, flat), (mid, block), (cot, block), (vecs, fixed(vecs.shape))] + out_blocks(weight, parts),
+        [(both, flat), (sent, flat), (mid, block), (cot, block), (gain, fixed(gain.shape))] + out_blocks(weight, parts),
         [
             (mid.shape, F32, block),
             (mid.shape, BF16, block),
@@ -750,10 +732,10 @@
     )
 
 
-def norm1_back_body(start, part_ref, near_ref, far_ref, stream_ref, mid_ref, vec_ref, seg_ref, in_ref, shift_ref, sums_ref):
+def norm1_back_body(start, part_ref, near_ref, far_ref, stream_ref, mid_ref, gain_ref, seg_ref, in_ref, shift_ref, sums_ref):
     grad = part_ref[0].astype(F32) + near_ref[0].astype(F32) + far_ref[0].astype(F32)
     hat, inverse = centre(stream_ref[0])
-    total = mid_ref[0] + norm_back(grad, vec_ref[GAIN1], hat, inverse)
+    total = mid_ref[0] + norm_back(grad, line(gain_ref), hat, inverse)
     in_ref[0] = total.astype(BF16)
     seg = seg_ref[pl.ds(pl.program_id(0) + start, 1)]
     slots = lax.broadcasted_iota(jnp.int32, (SEGS, seg.shape[-1]), 0) == seg
@@ -768,12 +750,12 @@
     sums_ref[1:2] += jnp.sum(grad, axis=0, keepdims=True)
 
 
-def norm1_back(start, count, own, near, far, stream, mid, vecs, seg, held=(), deps=()):
+def norm1_back(start, count, own, near, far, stream, mid, gain, seg, held=(), deps=()):
     rows, shard, model = stream.shape
     block, own_block = along((1, shard, model), 0, start), along((1, shard, model))
     return call(
         functools.partial(norm1_back_body, start), "norm1_back", (), (count,),
-        [(own, own_block), (near, own_block), (far, own_block), (stream, block), (mid, block), (vecs, fixed(vecs.shape))]
+        [(own, own_block), (near, own_block), (far, own_block), (stream, block), (mid, block), (gain, fixed(gain.shape))]
         + [(seg, fixed(seg.shape))],
         [
             (stream.shape, BF16, block),
@@ -802,53 +784,58 @@
 
 def over_z(values, at, depth):
     if depth != 4:
-        return lax.psum_scatter(values, "z", scatter_dimension=0, tiled=False)
+        return lax.psum_scatter(values, "z", scatter_dimension=0, tiled=False), []
     parts = [lax.dynamic_index_in_dim(values, at ^ n, 0, keepdims=False) for n in range(depth)]
-    own = parts[0].astype(F32)
     sent = [lax.ppermute(parts[n], "z", [(i, i ^ n) for i in range(depth)]) for n in range(1, depth)]
-    return (own + sent[0].astype(F32) + sent[1].astype(F32) + sent[2].astype(F32)).astype(BF16)
+    return parts[0].astype(F32), sent
 
 
 def ordered(at, own, other, axis):
     return jnp.where(at == 0, jnp.concatenate([own, other], axis), jnp.concatenate([other, own], axis))
 
 
-def finish_body(blocks, at_ref, d0, d1, u0, u1, l0, l1, down_ref, up_ref, qkv_ref, out_ref):
+def finish_body(blocks, at_ref, g0, g1, l0, l1, down_ref, up_ref, qkv_ref, out_ref):
     c_at = at_ref[0]
-    width = u0.shape[1] // (2 * blocks)
-    depth = d0.shape[0]
+    width = up_ref.shape[1] // (4 * blocks)
+    rest = up_ref.shape[0] // 2
+    size = g0.shape[1] - 2 * rest
     for c in range(2):
         mine = c_at == c
-        down_ref[c * depth : (c + 1) * depth] = jnp.where(mine, d0[...], d1[...]).astype(F32)
-        up = jnp.where(mine, u0[...], u1[...]).astype(F32)
-        for x in range(2):
-            for z in range(blocks):
-                at, place = ((2 * z + x) * 2 + c) * width, (x * blocks + z) * width
-                up_ref[:, at : at + width] = up[:, place : place + width]
+        for y in range(2):
+            grads = jnp.where(mine, g0[y], g1[y]).astype(F32)
+            at = (2 * c + y) * size
+            down_ref[at : at + size] = grads[0:size]
+            for b in range(2 * blocks):
+                s, at = b // blocks, b % blocks * width
+                up_ref[y * rest : (y + 1) * rest, (2 * b + c) * width : (2 * b + c + 1) * width] = grads[
+                    size + s * rest : size + (s + 1) * rest, at : at + width
+                ]
         late = jnp.where(mine, l0[...], l1[...]).astype(F32)
         half = out_ref.shape[1] // 2
-        size = half // 2
-        out_ref[:, c * half : (c + 1) * half] = late[:, 6 * size :]
+        wide = half // 2
+        out_ref[:, c * half : (c + 1) * half] = late[:, 6 * wide :]
         for y in range(2):
             for n in range(3):
-                at = n * 4 * size + (2 * y + c) * size
-                qkv_ref[:, at : at + size] = late[:, (3 * y + n) * size : (3 * y + n + 1) * size]
-
-
-def finish(c_at, dp, piece, down, up, late, parts):
-    rows, model = up[0].shape[0], down[0].shape[1]
-    depth = dp // 2
+                at = n * 4 * wide + (2 * y + c) * wide
+                qkv_ref[:, at : at + wide] = late[:, (3 * y + n) * wide : (3 * y + n + 1) * wide]
+
+
+def finish(c_at, dp, piece, grads, late, parts):
+    rows, model = late[0].shape[0], grads[0].shape[2]
+    depth, rest = dp // 2, rows // 2
+    size = grads[0].shape[1] - 2 * rest
     if piece % 128 == 0:
         at = c_at.astype(jnp.int32)[None]
-        shapes = [(2 * down[0].shape[0], model), (rows, 2 * up[0].shape[1]), (rows, 3 * model), (rows, model)]
-        arrays = list(down) + list(up) + list(late)
+        shapes = [(4 * size, model), (rows, 2 * dp * piece), (rows, 3 * model), (rows, model)]
+        arrays = list(grads) + list(late)
         return call(
             functools.partial(finish_body, depth), "finish", (at,), (1,),
             [(array, fixed(array.shape)) for array in arrays], [(shape, F32, fixed(shape)) for shape in shapes],
         )
-    down_done = ordered(c_at, *down, 0).astype(F32)
-    up_done = ordered(c_at, up[0][None], up[1][None], 0).reshape(2, rows, 2, depth, piece)
-    up_done = up_done.transpose(1, 3, 2, 0, 4).reshape(rows, -1).astype(F32)
+    both = ordered(c_at, grads[0][None], grads[1][None], 0)
+    down_done = both[:, :, :size].reshape(4 * size, model).astype(F32)
+    up_done = both[:, :, size:].reshape(2, 2, 2, rest, depth, piece).transpose(1, 3, 2, 4, 0, 5)
+    up_done = up_done.reshape(rows, 2 * dp * piece).astype(F32)
     both = ordered(c_at, late[0][None], late[1][None], 0)
     width = model // parts
     qkv_done = both[:, :, : 6 * width].reshape(2, rows, 2, 3, width).transpose(1, 3, 2, 0, 4)
@@ -873,16 +860,13 @@
     z_at, x_at, y_at, c_at = (lax.axis_index(name) for name in ("z", "x", "y", "c"))
     me = 2 * y_at + c_at
 
-    vecs = [time_bias, norm1_gain, norm1_bias, out_bias, norm2_gain, norm2_bias, down_bias, qkv_bias, up_bias]
-    vecs = jnp.concatenate(vecs).astype(F32).reshape(-1, model)
-
     seg_two = swap(segment_ids, "y")
     segs = jnp.stack([segment_ids, swap(segment_ids, "c"), seg_two, swap(seg_two, "c")], axis=1)
 
     groups = [(0, rows - 1), (rows - 1, 1)] if rows > 1 else [(0, 1)]
     features = time_features(doc_times.reshape(rows * SEGS), jnp.arange(TEMB), TEMB // 2)
     time_shift = dot(features, time_weight).reshape(rows, SEGS, model)
-    stream, own1 = norm1(inputs, segment_ids, time_shift, vecs)
+    stream, own1 = norm1(inputs, segment_ids, time_shift, (time_bias, norm1_gain, norm1_bias))
     own1, segs = tie(own1, segs)
     two1 = swap(own1, "y")
     one1 = swap(own1, "c")
@@ -903,32 +887,28 @@
 
     cot = cotangent.reshape(tokens, model)
     cot_other = swap(cot, "c")
-    turned = jnp.stack([1 - x_at, x_at])
     if piece % BLOCK == 0:
-        blk = ((jnp.arange(depth)[None, :] * 2 + turned[:, None]) * 2 + c_at) * (piece // BLOCK)
-        blk = (blk[..., None] + jnp.arange(piece // BLOCK)).reshape(-1).astype(jnp.int32)
+        blk = (jnp.arange(dp)[:, None] * 2 + c_at) * (piece // BLOCK) + jnp.arange(piece // BLOCK)
+        blk = blk.reshape(-1).astype(jnp.int32)
         up_from, down_from = up_weight, down_weight
     else:
         blk = jnp.zeros((half // BLOCK,), jnp.int32)
-        up_from = up_weight.reshape(model, depth, 2, 2, piece)
-        up_from = lax.dynamic_index_in_dim(up_from, c_at, 3, keepdims=False)
-        up_from = jnp.where(x_at == 1, up_from, up_from[:, :, ::-1]).transpose(0, 2, 1, 3).reshape(model, half)
-        down_from = down_weight.reshape(depth, 2, 2, piece, model)
-        down_from = lax.dynamic_index_in_dim(down_from, c_at, 2, keepdims=False)
-        down_from = jnp.where(x_at == 1, down_from, down_from[:, ::-1]).transpose(1, 0, 2, 3).reshape(half, model)
+        up_from = lax.dynamic_index_in_dim(up_weight.reshape(model, dp, 2, piece), c_at, 2, keepdims=False)
+        down_from = lax.dynamic_index_in_dim(down_weight.reshape(dp, 2, piece, model), c_at, 1, keepdims=False)
+        up_from, down_from = up_from.reshape(model, half), down_from.reshape(half, model)
     grad_act, up_own, down_own, cot_both = cot_down(
         blk, cot, cot_other, up_from, down_from, piece % BLOCK != 0, half
     )
-    up_bias_own = vecs
+    up_bias_own, bias_blk = up_bias.reshape(1, hidden_width), blk
     if piece % BLOCK:
-        up_bias_own = lax.dynamic_index_in_dim(up_bias.reshape(depth, 2, 2, piece), c_at, 2, keepdims=False)
-        up_bias_own = jnp.where(x_at == 1, up_bias_own, up_bias_own[:, ::-1]).transpose(1, 0, 2)
-        up_bias_own = up_bias_own.reshape(1, half).astype(F32)
-
-    qkv, qkv_own = project_qkv(0, parts, me_list, own1, one1, qkv_weight, vecs, cos_tab, sin_tab, (), (grad_act,))
+        up_bias_own = lax.dynamic_index_in_dim(up_bias.reshape(dp, 2, piece), c_at, 1, keepdims=False)
+        up_bias_own, bias_blk = up_bias_own.reshape(1, half), jnp.arange(half // BLOCK, dtype=jnp.int32)
+
+    qkv_line = qkv_bias.reshape(1, 3 * model)
+    qkv, qkv_own = project_qkv(0, parts, me_list, own1, one1, qkv_weight, qkv_line, cos_tab, sin_tab, (), (grad_act,))
     two1, qkv = tie(two1, qkv)
     three1 = swap(two1, "c")
-    qkv, _ = project_qkv(1, parts, me_list, two1, three1, qkv_weight, vecs, cos_tab, sin_tab, (qkv,))
+    qkv, _ = project_qkv(1, parts, me_list, two1, three1, qkv_weight, qkv_line, cos_tab, sin_tab, (qkv,))
     o, lse, attended = None, None, []
     for start, count in groups:
         held = () if o is None else (o, lse)
@@ -939,86 +919,68 @@
         far, o = tie(values[1], o)
         values = exchange(o, values[0], far)
         middle, low, attended_all = middle_norm(
-            start, count, order_list, values, out_weight, stream, vecs, held
+            start, count, order_list, values, out_weight, stream, (out_bias, norm2_gain, norm2_bias), held
         )
         held = (middle, attended_all)
         normed2.append(low)
         normed2_other.append(swap(low, "c"))
 
     active, grad_hidden, up_b, normed2_both, part2 = hidden_units(
-        blk, normed2 + normed2_other, grad_act, up_own, up_bias_own
+        bias_blk, normed2 + normed2_other, grad_act, up_own, up_bias_own
     )
     part2_sent = swap(part2[tokens:], "c")
     grad_middle, grad_middle_low, att0, att1, far, sums2 = middle_back(
-        order_list, part2, part2_sent, middle, cotangent, vecs, out_weight, parts
+        order_list, part2, part2_sent, middle, cotangent, norm2_gain, out_weight, parts
     )
     far = swap(far, "y")
     sums2 = sums2[:4]
 
     active, grad_hidden, att0 = tie(active, grad_hidden, att0)
-    up_half = (x_at == y_at).astype(jnp.int32)
-    up_out, up_late, up_grad, down_out, down_late = sent_grads(
-        up_half[None], normed2_both, cot_both, grad_hidden, active
-    )
-    up_out, down_out, far = tie(up_out, down_out, far)
-    up_sent, down_sent = swap(up_out, "y"), swap(down_out, "x")
-    down_kept, feed, out_sent, out_grad = kept_grads(
-        order_list, active, cot_both, down_own, attended_all.reshape(tokens, model),
-        grad_middle_low.reshape(tokens, model), c_at, (down_out, far),
+    grads = both_grads(active, cot_both, normed2_both, grad_hidden, depth)
+    grads = lax.psum_scatter(grads.reshape((4,) + grads.shape[2:]), ("x", "y"), scatter_dimension=0, tiled=False)
+    feed, out_sent, out_grad = feed_grads(
+        order_list, active, down_own, attended_all.reshape(tokens, model), grad_middle_low.reshape(tokens, model), c_at,
+        (far,),
     )
     out_sent = swap(out_sent, "c")
-    down_kept, feed, up_sent, down_sent, up_late, down_late = tie(
-        down_kept, feed, up_sent, down_sent, up_late, down_late
-    )
-    up_sent = [up_sent, swap(up_late, "y")]
-    down_sent = [down_sent, swap(down_late, "x")]
     feed = feed[:tokens].astype(F32) + swap(feed[tokens:], "c").astype(F32) + down_bias.astype(F32)
     output = (middle + feed.reshape(rows, shard, model)).astype(BF16)
     up_rows = model // dp
     out_c = add_low(out_grad, out_sent)
 
-    down_kept, output, out_c, far = tie(down_kept, output, out_c, far)
-    out_z = lax.psum_scatter(out_c, "z", scatter_dimension=0, tiled=True)
+    output, out_c, far = tie(output, out_c, far)
     grad_o = exchange(att0, att1, far)
     grad_qkv, back = (), []
     for start, count in groups:
         grad_qkv, own, one, two, three = attend_back(
             start, count, cnt, idx, qkv, o, grad_o, lse, segs, cos_tab, sin_tab, qkv_own, grad_qkv,
-            (there, down_x, up_out) if back else (),
+            (there, out_x) if back else (),
         )
         grad_qkv = (grad_qkv,)
-        if not back:
-            own, up_grad, down_kept = tie(own, up_grad, down_kept)
-            down_x = add_low(down_kept, jnp.concatenate(down_sent, axis=0))
-            down_z = lax.psum_scatter(down_x, "z", scatter_dimension=0, tiled=True)
-            up_y = add_low(up_grad, jnp.concatenate(up_sent, axis=1)).reshape(depth, 2 * up_rows, half // 2)
-            up_out = cut(up_y, 1 - x_at, up_rows, 1)
-            up_sent = swap(up_out, "x")
         there = add_low(two, swap(three, "c"))
         if not back:
-            there, up_out = tie(there, up_out)
+            own, out_c = tie(own, out_c.reshape(depth, 2 * up_rows, model // 2))
+            out_x = cut(out_c, 1 - x_at, up_rows, 1)
         back.append((own, swap(one, "c"), swap(there, "y")))
-    grad_qkv, there, far, up_sent, up_y = tie(grad_qkv[0], there, back[0][2], up_sent, up_y)
+    grad_qkv, there, far = tie(grad_qkv[0], there, back[0][2])
     back[0] = back[0][:2] + (far,)
     back[-1] = back[-1][:2] + (swap(there, "y"),)
     qkv_out, qkv_kept, qkv_b = qkv_grads(x_at, [own1, one1, two1, three1], grad_qkv, depth)
     qkv_sent = swap(qkv_out, "x")
-    qkv_kept, up_y, up_sent, out_z = tie(qkv_kept, up_y, up_sent, out_z)
-    up_x = add_low(cut(up_y, x_at, up_rows, 1), up_sent)
-    up_z = lax.psum_scatter(up_x, "z", scatter_dimension=0, tiled=False)
-    out_x = add_low(cut(out_z, x_at, up_rows, 0), swap(cut(out_z, 1 - x_at, up_rows, 0), "x"))
+    qkv_kept, out_c, grads, out_x = tie(qkv_kept, out_c, grads, swap(out_x, "x"))
+    grads = lax.psum_scatter(grads, "z", scatter_dimension=0, tiled=False)
+    out_x = add_low(cut(out_c, x_at, up_rows, 1), out_x)
     held, grad_shift, sums1 = (), [], 0.0
     for (start, count), values in zip(groups, back):
         input_grad, found, sums = norm1_back(
-            start, count, *values, stream, grad_middle, vecs, segment_ids, held, (up_x if held else qkv_kept,)
+            start, count, *values, stream, grad_middle, norm1_gain, segment_ids, held, (out_x if held else qkv_kept,)
         )
         held = (input_grad,)
         grad_shift.append(found.reshape(count * SEGS, model))
         sums1 = sums1 + sums[:2]
-    qkv_x = add_low(qkv_kept, qkv_sent)
-
-    up_b = up_b.reshape(2, depth, 1, piece)
-    up_b = jnp.where(x_at == 1, up_b, up_b[::-1]).transpose(1, 0, 2, 3)
+    qkv_x = jnp.concatenate([add_low(qkv_kept, qkv_sent), out_x], axis=2)
+
+    up_b = up_b.reshape(dp, 1, piece)
     up_b = jnp.where(jnp.arange(2)[:, None] == c_at, up_b, 0.0).reshape(-1, model)
     qkv_b = jnp.where(jnp.arange(parts)[:, None] == me, qkv_b.reshape(3, 1, width), 0.0).reshape(3, model)
     times = doc_times.reshape(1, rows * SEGS)
@@ -1026,11 +988,9 @@
     times = jnp.pad(times, ((0, 0), (0, model - times.shape[1])))
     small = jnp.concatenate(grad_shift + [sums1, sums2, qkv_b, up_b, times], axis=0)
     small, qkv_x = tie(add_low(small, swap(small.astype(BF16), "c")), qkv_x)
+    late, late_parts = over_z(qkv_x, z_at, depth)
     small = add_low(small, swap(small, "y"))
-    small, down_z = tie(small, down_z)
-    down_y = add_low(down_z, swap(down_z, "y"))
-    small, down_y = tie(ordered(x_at, small[None], swap(small, "x")[None], 0), down_y)
-    down_other = swap(down_y, "c")
+    small = ordered(x_at, small[None], swap(small, "x")[None], 0)
     if depth == 4:
         others = [lax.ppermute(small, "z", [(i, i ^ n) for i in range(depth)]) for n in range(1, depth)]
         small = jnp.stack([small] + others)
@@ -1039,18 +999,18 @@
         small = lax.all_gather(small, "z")
     small = small.reshape(dp, small.shape[2], model)
 
-    small, up_z = tie(small, up_z)
-    up_done = ordered(y_at, up_z, swap(up_z, "y"), 1)
-    up_other = swap(up_done, "c")
-    late = jnp.concatenate([over_z(qkv_x, z_at, depth), out_x], axis=1)
+    small, late = tie(small, late)
+    late = (late + sum(part.astype(F32) for part in late_parts)).astype(BF16) if depth == 4 else late
     late_sent = swap(late, "y")
     qkv_y = ordered(y_at, late[None, :, : 3 * width], late_sent[None, :, : 3 * width], 0)
     out_y = add_low(late[:, 3 * width :], late_sent[:, 3 * width :])
     late = jnp.concatenate([qkv_y[0], qkv_y[1], out_y], axis=1)
     late_other = swap(late, "c")
+    grads = ordered(y_at, grads[None], swap(grads, "y")[None], 0)
+    grads_other = swap(grads, "c")
 
     down_done, up_done, qkv_done, out_done = finish(
-        c_at, dp, piece, (down_y, down_other), (up_done, up_other), (late, late_other), parts
+        c_at, dp, piece, (grads, grads_other), (late, late_other), parts
     )
 
     all_times = small[:, -1, : 2 * rows * SEGS].astype(F32) * 0.25

time: 463 us -> 472 us (1.019)
  waiting for transfers between devices: 115 us -> 143 us
  other arithmetic: 31.6 us -> 21.4 us
  Pallas kernels: 224 us -> 214 us
  starting transfers between devices: 34 us -> 39.7 us
  local copies, waits for them, and re-layouts: 33 us -> 27.7 us
    ppermute x3, waiting for transfers between devices: 8.81 us -> 25.7 us  [local(): lax.ppermute(small, 'z', [(i, i ^ n) for i in range(depth)])]
    pallas_call x18, Pallas kernels: 224 us -> 214 us  [call(): pl.pallas_call(kernel, grid_spec=pltpu.PrefetchScalarGridSpec(num_scalar_...]
    convert_element_type x12 -> x8, other arithmetic: 15.5 us -> 6.19 us  [add_low(): return (kept.astype(F32) + sent.astype(F32)).astype(BF16)]
    ppermute x3, starting transfers between devices: 4.45 us -> 12.5 us  [over_z(): lax.ppermute(parts[n], 'z', [(i, i ^ n) for i in range(depth)])]
    ppermute x43 -> x36, waiting for transfers between devices: 83.1 us -> 90.6 us  [swap(): return lax.ppermute(value, axis, [(0, 1), (1, 0)])]
    ppermute x43 -> x36, starting transfers between devices: 24.7 us -> 20.1 us  [swap(): return lax.ppermute(value, axis, [(0, 1), (1, 0)])]
    unnamed x101 -> x88, local copies, waits for them, and re-layouts: 16 us -> 12.7 us
  transfers between devices with their start and end apart: 52 -> 44, of which waited for: 28 -> 21; matrix products, arithmetic and copies ran while one was open for 10% -> 8% of each run, Pallas kernels for 35% -> 27%
where the time goes in v2:
time: 472 us; the launch traced here: 463 us
  Pallas kernels  214 us (45%)
  waiting for transfers between devices  143 us (30%)
  starting transfers between devices  39.7 us (8%)
  local copies, waits for them, and re-layouts  27.7 us (6%)
  other arithmetic  21.4 us (5%)
  between operations  15.2 us (3%)
    pallas_call x18, Pallas kernels, call(): pl.pallas_call(kernel, grid_spec=pltpu.PrefetchScalarGridSpec(num_scalar_...  214 us
    ppermute x36, waiting for transfers between devices, swap(): return lax.ppermute(value, axis, [(0, 1), (1, 0)])  90.6 us
    ppermute x3, waiting for transfers between devices, over_z(): lax.ppermute(parts[n], 'z', [(i, i ^ n) for i in range(depth)])  26.6 us
    ppermute x3, waiting for transfers between devices, local(): lax.ppermute(small, 'z', [(i, i ^ n) for i in range(depth)])  25.7 us
    ppermute x36, starting transfers between devices, swap(): return lax.ppermute(value, axis, [(0, 1), (1, 0)])  20.1 us
    unnamed x88, local copies, waits for them, and re-layouts  12.7 us
    ppermute x3, starting transfers between devices, over_z(): lax.ppermute(parts[n], 'z', [(i, i ^ n) for i in range(depth)])  12.5 us
  transfers between devices with their start and end apart: 44, of which 21 were waited for; matrix products, arithmetic and copies ran while one was open for 8% of the time, Pallas kernels for 27%

profile of v2, /device:TPU:0, one launch (start us, length us, event | category | flops | bytes accessed | tf_op | source)
XLA Modules:
  0.0 463.4 jit_solution(7967326752021387723)
XLA Ops:
  26.6 15.9 %cot_down.1 = (bf16[1536,2048]{1,0:T(8,128)(2,1)}, bf16[1024,2048]{1,0:T(8,128)(2,1)}, bf16[2048,1024]{1,0:T(8,128)(2,1)}, bf16[1536,1024]{1,0:T(8,128)(2,1)}) custom-call(s32[8]{0:T(128)} %multiply_add_fusion.refs_0_, bf16[768,1024]{1,0:T(8,128)(2,1)} %bitcast.84, bf16[768,1024]{1,0:T(8,128)(2,1)} %collective-permute-done.5.refs_2_, ...), custom_call_target="tpu_custom_call" | custom-call | tf_op jit(solution)/shard_map/cot_down/pallas_call | solution.py:94
  43.7 7.4 %qkv.2 = (bf16[3,4,3,256,256]{4,3,2,1,0:T(8,128)(2,1)}, bf16[768,1024]{1,0:T(8,128)(2,1)}) custom-call(s32[1]{0:T(128)} %bitcast.2.refs_0_, bf16[3,256,1024]{2,1,0:T(8,128)(2,1)} %get-tuple-element.113.refs_1_, bf16[3,256,1024]{2,1,0:T(8,128)(2,1)} %copy-done.5, bf16[1024,3072]{1,0:T(8,128)(2,1)} %refs_3_.7, bf16[1,3072]{1,0:T(2,128)(2,1)} %reshape.378.refs_4_, ...), custom_call_target="tpu_custom_call" | custom-call | tf_op jit(solution)/shard_map/qkv/pallas_call | solution.py:94
  51.1 4.9 %collective-permute-done.3.refs_1_.refs_3_ = bf16[3,256,1024]{2,1,0:T(8,128)(2,1)} collective-permute-done((bf16[3,256,1024]{2,1,0:T(8,128)(2,1)}, bf16[3,256,1024]{2,1,0:T(8,128)(2,1)}, u32[]{:S(2)}, u32[]{:S(2)}) %collective-permute-start.3) | collective-permute-done | bytes 1572896 | tf_op jit(solution)/shard_map/ppermute | solution.py:27
  60.7 7.4 %qkv.3 = (bf16[3,4,3,256,256]{4,3,2,1,0:T(8,128)(2,1)}, bf16[768,1024]{1,0:T(8,128)(2,1)}) custom-call(s32[1]{0:T(128)} %bitcast.2.refs_0_, bf16[3,256,1024]{2,1,0:T(8,128)(2,1)} %collective-permute-done.3.refs_1_.refs_3_, bf16[3,256,1024]{2,1,0:T(8,128)(2,1)} %copy-done.6, bf16[1024,3072]{1,0:T(8,128)(2,1)} %refs_3_.7, ...), custom_call_target="tpu_custom_call", output_to_operand_aliasing={{0}: (7, {})} | custom-call | tf_op jit(solution)/shard_map/qkv/pallas_call | solution.py:94
  68.2 16.1 %attend.2 = (bf16[4,3,256,256]{3,2,1,0:T(8,128)(2,1)}, bf16[2,256,256]{2,1,0:T(8,128)(2,1)}, bf16[2,2,256,256]{3,2,1,0:T(8,128)(2,1)}, f32[3,4,8,256]{3,2,1,0:T(8,128)}) custom-call(s32[12]{0:T(128)} %reshape.376.refs_0_, s32[48]{0:T(128)} %reshape.377.refs_1_, bf16[3,4,3,256,256]{4,3,2,1,0:T(8,128)(2,1)} %get-tuple-element.119.refs_2_, s32[3,4,256]{2,1,0:T(4,128)} %copy-done.25), custom_call_target="tpu_custom_call" | custom-call | tf_op jit(solution)/shard_map/attend/pallas_call | solution.py:94
  86.0 7.6 %attend.3 = (bf16[4,3,256,256]{3,2,1,0:T(8,128)(2,1)}, bf16[1,256,256]{2,1,0:T(8,128)(2,1)}, bf16[2,1,256,256]{3,2,1,0:T(8,128)(2,1)}, f32[3,4,8,256]{3,2,1,0:T(8,128)}) custom-call(s32[12]{0:T(128)} %reshape.376.refs_0_, s32[48]{0:T(128)} %reshape.377.refs_1_, ...), custom_call_target="tpu_custom_call", output_to_operand_aliasing={{0}: (4, {}), {3}: (5, {})} | custom-call | tf_op jit(solution)/shard_map/attend/pallas_call | solution.py:94
  93.5 4.9 %collective-permute-done.8.refs_3_ = bf16[2,2,256,256]{3,2,1,0:T(8,128)(2,1)S(1)} collective-permute-done((bf16[2,2,256,256]{3,2,1,0:T(8,128)(2,1)}, bf16[2,2,256,256]{3,2,1,0:T(8,128)(2,1)S(1)}, u32[]{:S(2)}, u32[]{:S(2)}) %collective-permute-start.8) | collective-permute-done | bytes 524320 | tf_op jit(solution)/shard_map/ppermute | solution.py:27
  101.7 6.1 %middle.2 = (f32[3,256,1024]{2,1,0:T(8,128)}, bf16[2,256,1024]{2,1,0:T(8,128)(2,1)}, bf16[3,256,1024]{2,1,0:T(8,128)(2,1)}) custom-call(s32[4]{0:T(128)} %pad_add_fusion.1.refs_0_, bf16[4,3,256,256]{3,2,1,0:T(8,128)(2,1)} %get-tuple-element.126.refs_1_.refs_3_, bf16[2,256,256]{2,1,0:T(8,128)(2,1)} %copy-done.26, bf16[2,2,256,256]{3,2,1,0:T(8,128)(2,1)} %copy-done.17, ...), custom_call_target="tpu_custom_call" | custom-call | tf_op jit(solution)/shard_map/middle/pallas_call | solution.py:94
  111.6 4.9 %middle.3 = (f32[3,256,1024]{2,1,0:T(8,128)}, bf16[1,256,1024]{2,1,0:T(8,128)(2,1)}, bf16[3,256,1024]{2,1,0:T(8,128)(2,1)}) custom-call(s32[4]{0:T(128)} %pad_add_fusion.1.refs_0_, bf16[4,3,256,256]{3,2,1,0:T(8,128)(2,1)} %get-tuple-element.126.refs_1_.refs_3_, bf16[1,256,256]{2,1,0:T(8,128)(2,1)} %copy-done.28, ...), custom_call_target="tpu_custom_call", output_to_operand_aliasing={{0}: (13, {}), {2}: (14, {})} | custom-call | tf_op jit(solution)/shard_map/middle/pallas_call | solution.py:94
  119.8 29.2 %hidden.1 = (bf16[1536,2048]{1,0:T(8,128)(2,1)}, bf16[1536,2048]{1,0:T(8,128)(2,1)}, f32[1,2048]{1,0:T(1,128)}, bf16[1536,1024]{1,0:T(8,128)(2,1)}, bf16[1536,1024]{1,0:T(8,128)(2,1)}) custom-call(s32[8]{0:T(128)} %multiply_add_fusion.refs_0_, bf16[2,256,1024]{2,1,0:T(8,128)(2,1)} %get-tuple-element.135.refs_1_, ...), custom_call_target="tpu_custom_call" | custom-call | tf_op jit(solution)/shard_map/hidden/pallas_call | solution.py:94
  155.2 9.8 %middle_back.1 = (f32[3,256,1024]{2,1,0:T(8,128)}, bf16[3,256,1024]{2,1,0:T(8,128)(2,1)}, bf16[3,256,256]{2,1,0:T(8,128)(2,1)}, bf16[3,256,256]{2,1,0:T(8,128)(2...) custom-call(s32[4]{0:T(128)} %pad_add_fusion.1.refs_0_, bf16[1536,1024]{1,0:T(8,128)(2,1)} %get-tuple-element.140.refs_1_, ...), custom_call_target="tpu_custom_call" | custom-call | tf_op jit(solution)/shard_map/middle_back/pallas_call | solution.py:94
  164.9 19.7 %both_grads.1 = bf16[2,2,4,256,1024]{4,3,2,1,0:T(8,128)(2,1)} custom-call(bf16[1536,1024]{1,0:T(8,128)(2,1)} %get-tuple-element.175.refs_0_, bf16[1536,2048]{1,0:T(8,128)(2,1)} %get-tuple-element.176.refs_1_, bf16[1536,2048]{1,0:T(8,128)(2,1)} %get-tuple-element.142.refs_1_.refs_2_, bf16[1536,1024]{1,0:T(8,128)(2,1)} %get-tuple-element.177.refs_3_), custom_call_target="tpu_custom_call" | custom-call | tf_op jit(solution)/shard_map/both_grads/pallas_call | solution.py:94
  187.1 30.6 %collective-permute-done.16.refs_5_.refs_6_ = bf16[2,3,256,256]{3,2,1,0:T(8,128)(2,1)S(1)} collective-permute-done((bf16[2,3,256,256]{3,2,1,0:T(8,128)(2,1)S(1)}, bf16[2,3,256,256]{3,2,1,0:T(8,128)(2,1)S(1)}, u32[]{:S(2)}, u32[]{:S(2)}) %collective-permute-start.16) | collective-permute-done | bytes 786464 | tf_op jit(solution)/shard_map/ppermute | solution.py:27
  218.6 15.2 %feed_grads.1 = (bf16[1536,1024]{1,0:T(8,128)(2,1)}, bf16[1024,512]{1,0:T(8,128)(2,1)}, bf16[1024,512]{1,0:T(8,128)(2,1)}) custom-call(s32[5]{0:T(128)} %concatenate.80.refs_0_, bf16[1536,2048]{1,0:T(8,128)(2,1)} %get-tuple-element.142.refs_1_.refs_2_, bf16[2048,1024]{1,0:T(8,128)(2,1)} %get-tuple-element.143.refs_2_, bf16[768,1024]{1,0:T(8,128)(2,1)} %bitcast.82, ...), custom_call_target="tpu_custom_call" | custom-call | tf_op jit(solution)/shard_map/feed_grads/pallas_call | solution.py:94
  247.1 30.8 %attend_back.2 = (bf16[4,3,256,768]{3,2,1,0:T(8,128)(2,1)}, bf16[2,256,1024]{2,1,0:T(8,128)(2,1)}, bf16[2,256,1024]{2,1,0:T(8,128)(2,1)}, bf16[2,256,1024]{2,1,0:T(8,128)(2,1)}, bf16[2,256,1024]{2,1,0:T(8,128)(2,1)}) custom-call(s32[12]{0:T(128)} %reshape.376.refs_0_, s32[48]{0:T(128)} %reshape.377.refs_1_, ...), custom_call_target="tpu_custom_call" | custom-call | tf_op jit(solution)/shard_map/attend_back/pallas_call | solution.py:94
  284.5 14.8 %attend_back.3 = (bf16[4,3,256,768]{3,2,1,0:T(8,128)(2,1)}, bf16[1,256,1024]{2,1,0:T(8,128)(2,1)}, bf16[1,256,1024]{2,1,0:T(8,128)(2,1)}, bf16[1,256,1024]{2,1,0:T(8,128)(2,1)}, bf16[1,256,1024]{2,1,0:T(8,128)(2,1)}) custom-call(s32[12]{0:T(128)} %reshape.376.refs_0_, s32[48]{0:T(128)} %reshape.377.refs_1_, ...), custom_call_target="tpu_custom_call", output_to_operand_aliasing={{0}: (13, {})} | custom-call | tf_op jit(solution)/shard_map/attend_back/pallas_call | solution.py:94
  309.0 10.5 %qkv_grads.1 = (bf16[4,128,768]{2,1,0:T(8,128)(2,1)}, bf16[4,128,768]{2,1,0:T(8,128)(2,1)}, f32[1,768]{1,0:T(1,128)}) custom-call(s32[1]{0:T(128)} %bitcast.15.refs_0_, bf16[3,256,1024]{2,1,0:T(8,128)(2,1)} %get-tuple-element.113.refs_1_, bf16[3,256,1024]{2,1,0:T(8,128)(2,1)} %copy-done.5, bf16[3,256,1024]{2,1,0:T(8,128)(2,1)} %collective-permute-done.3.refs_1_.refs_3_, ...), custom_call_target="tpu_custom_call" | custom-call | tf_op jit(solution)/shard_map/qkv_grads/pallas_call | solution.py:94
  320.4 5.7 %norm1_back.2 = (bf16[3,256,1024]{2,1,0:T(8,128)(2,1)}, f32[2,8,1024]{2,1,0:T(8,128)}, f32[8,1024]{1,0:T(8,128)}) custom-call(bf16[2,256,1024]{2,1,0:T(8,128)(2,1)} %get-tuple-element.170.refs_0_, bf16[2,256,1024]{2,1,0:T(8,128)(2,1)} %collective-permute-done.26.refs_1_, bf16[2,256,1024]{2,1,0:T(8,128)(2,1)} %collective-permute-done.24.refs_2_, ...), custom_call_target="tpu_custom_call" | custom-call | tf_op jit(solution)/shard_map/norm1_back/pallas_call | solution.py:94
  348.5 6.4 %collective-permute-start.34 = (bf16[2,38,1024]{2,1,0:T(8,128)(2,1)S(1)}, bf16[2,38,1024]{2,1,0:T(8,128)(2,1)S(1)}, u32[]{:S(2)}, u32[]{:S(2)}) collective-permute-start(bf16[2,38,1024]{2,1,0:T(8,128)(2,1)S(1)} %maximum_select_fusion.3), channel_id=1, source_target_pairs={{0,24},{8,16},{16,8},{24,0},{1,25},{9,17},{17,9},{25,1},{2,26},{10... | collective-permute-start | bytes 466952 | tf_op jit(solution)/shard_map/ppermute | solution.py:995
  363.5 8.7 %collective-permute-start.37 = (bf16[128,1280]{1,0:T(8,128)(2,1)S(1)}, bf16[128,1280]{1,0:T(8,128)(2,1)S(1)}, u32[]{:S(2)}, u32[]{:S(2)}) collective-permute-start(bf16[128,1280]{1,0:T(8,128)(2,1)S(1)} %get-tuple-element.206), channel_id=1, source_target_pairs={{0,8},{8,0},{16,24},{24,16},{1,9},{9,1},{17,25},{25,17},{2,10},{10... | collective-permute-start | bytes 983048 | tf_op jit(solution)/shard_map/ppermute | solution.py:789
  372.1 21.8 %collective-permute-done.33 = bf16[2,38,1024]{2,1,0:T(8,128)(2,1)S(1)} collective-permute-done((bf16[2,38,1024]{2,1,0:T(8,128)(2,1)S(1)}, bf16[2,38,1024]{2,1,0:T(8,128)(2,1)S(1)}, u32[]{:S(2)}, u32[]{:S(2)}) %collective-permute-start.33) | collective-permute-done | bytes 155680 | tf_op jit(solution)/shard_map/ppermute | solution.py:995
  397.4 26.6 %collective-permute-done.38 = bf16[128,1280]{1,0:T(8,128)(2,1)S(1)} collective-permute-done((bf16[128,1280]{1,0:T(8,128)(2,1)S(1)}, bf16[128,1280]{1,0:T(8,128)(2,1)S(1)}, u32[]{:S(2)}, u32[]{:S(2)}) %collective-permute-start.38) | collective-permute-done | bytes 327712 | tf_op jit(solution)/shard_map/ppermute | solution.py:789
  426.8 8.0 %collective-permute-done.40 = bf16[128,1280]{1,0:T(8,128)(2,1)S(1)} collective-permute-done((bf16[128,1280]{1,0:T(8,128)(2,1)S(1)}, bf16[128,1280]{1,0:T(8,128)(2,1)S(1)}, u32[]{:S(2)}, u32[]{:S(2)}) %collective-permute-start.40) | collective-permute-done | bytes 327712 | tf_op jit(solution)/shard_map/ppermute | solution.py:27
  435.0 9.7 %collective-permute-done.35 = bf16[256,1024]{1,0:T(8,128)(2,1)S(1)} collective-permute-done((bf16[256,1024]{1,0:T(8,128)(2,1)}, bf16[256,1024]{1,0:T(8,128)(2,1)S(1)}, u32[]{:S(2)}, u32[]{:S(2)}) %collective-permute-start.35) | collective-permute-done | bytes 524320 | tf_op jit(solution)/shard_map/ppermute | solution.py:27
  (271 shorter events, 125.7 us)
Async XLA Ops:
  7.2 313.2 %reduce-scatter.7.cloned.1.call-start = ((), (), s32[]{:S(2)}) async-start(), calls=%async_computation.3 | async-start | bytes 10485760
  10.3 16.3 %collective-permute-start.5 = (bf16[768,1024]{1,0:T(8,128)(2,1)}, bf16[768,1024]{1,0:T(8,128)(2,1)}, u32[]{:S(2)}, u32[]{:S(2)}) collective-permute-start(bf16[768,1024]{1,0:T(8,128)(2,1)} %bitcast.83), channel_id=1, source_target_pairs={{0,1},{1,0},{2,3},{3,2},{4,5},{5,4},{6,7},{7,6},{8,9},{9,8},{10,11... | collective-permute-start | bytes 4718600 | tf_op jit(solution)/shard_map/ppermute | solution.py:27
  18.5 24.0 %collective-permute-start.4 = (bf16[3,256,1024]{2,1,0:T(8,128)(2,1)}, bf16[3,256,1024]{2,1,0:T(8,128)(2,1)S(1)}, u32[]{:S(2)}, u32[]{:S(2)}) collective-permute-start(bf16[3,256,1024]{2,1,0:T(8,128)(2,1)} %get-tuple-element.113.refs_1_), channel_id=1, source_target_pairs={{0,1},{1,0},{2,3},{3,2},{4,5},{5,4},{6,7},{7,6},{8,9},{9,8},{10,11... | collective-permute-start | bytes 4718600 | tf_op jit(solution)/shard_map/ppermute | solution.py:27
  19.0 37.0 %collective-permute-start.3 = (bf16[3,256,1024]{2,1,0:T(8,128)(2,1)}, bf16[3,256,1024]{2,1,0:T(8,128)(2,1)}, u32[]{:S(2)}, u32[]{:S(2)}) collective-permute-start(bf16[3,256,1024]{2,1,0:T(8,128)(2,1)} %get-tuple-element.113.refs_1_), channel_id=1, source_target_pairs={{0,2},{2,0},{1,3},{3,1},{4,6},{6,4},{5,7},{7,5},{8,10},{10,8},{9,1... | collective-permute-start | bytes 4718600 | tf_op jit(solution)/shard_map/ppermute | solution.py:27
  84.2 14.2 %collective-permute-start.8 = (bf16[2,2,256,256]{3,2,1,0:T(8,128)(2,1)}, bf16[2,2,256,256]{3,2,1,0:T(8,128)(2,1)S(1)}, u32[]{:S(2)}, u32[]{:S(2)}) collective-permute-start(bf16[2,2,256,256]{3,2,1,0:T(8,128)(2,1)} %get-tuple-element.123), channel_id=1, source_target_pairs={{0,2},{2,0},{1,3},{3,1},{4,6},{6,4},{5,7},{7,5},{8,10},{10,8},{9,1... | collective-permute-start | bytes 1572872 | tf_op jit(solution)/shard_map/ppermute | solution.py:27
  86.0 14.9 %collective-permute-start.11 = (bf16[2,256,256]{2,1,0:T(8,128)(2,1)}, bf16[2,256,256]{2,1,0:T(8,128)(2,1)S(1)}, u32[]{:S(2)}, u32[]{:S(2)}) collective-permute-start(bf16[2,256,256]{2,1,0:T(8,128)(2,1)} %get-tuple-element.130), channel_id=1, source_target_pairs={{0,1},{1,0},{2,3},{3,2},{4,5},{5,4},{6,7},{7,6},{8,9},{9,8},{10,11... | collective-permute-start | bytes 786440 | tf_op jit(solution)/shard_map/ppermute | solution.py:27
  98.5 9.9 %collective-permute-start.7 = (bf16[2,1,256,256]{3,2,1,0:T(8,128)(2,1)}, bf16[2,1,256,256]{3,2,1,0:T(8,128)(2,1)S(1)}, u32[]{:S(2)}, u32[]{:S(2)}) collective-permute-start(bf16[2,1,256,256]{3,2,1,0:T(8,128)(2,1)} %get-tuple-element.122), channel_id=1, source_target_pairs={{0,2},{2,0},{1,3},{3,1},{4,6},{6,4},{5,7},{7,5},{8,10},{10,8},{9,1... | collective-permute-start | bytes 786440 | tf_op jit(solution)/shard_map/ppermute | solution.py:27
  107.9 10.7 %collective-permute-start.13 = (bf16[2,256,1024]{2,1,0:T(8,128)(2,1)}, bf16[2,256,1024]{2,1,0:T(8,128)(2,1)S(1)}, u32[]{:S(2)}, u32[]{:S(2)}) collective-permute-start(bf16[2,256,1024]{2,1,0:T(8,128)(2,1)} %get-tuple-element.135.refs_1_), channel_id=1, source_target_pairs={{0,1},{1,0},{2,3},{3,2},{4,5},{5,4},{6,7},{7,6},{8,9},{9,8},{10,11... | collective-permute-start | bytes 3145736 | tf_op jit(solution)/shard_map/ppermute | solution.py:27
  184.6 241.6 %reduce-scatter.5.cloned.1.call-start = ((), (), s32[]{:S(2)}) async-start(), calls=%async_computation.2 | async-start | bytes 2621440 | tf_op jit(solution)/shard_map/reduce_scatter | solution.py:971
  185.8 32.0 %collective-permute-start.16 = (bf16[2,3,256,256]{3,2,1,0:T(8,128)(2,1)S(1)}, bf16[2,3,256,256]{3,2,1,0:T(8,128)(2,1)S(1)}, u32[]{:S(2)}, u32[]{:S(2)}) collective-permute-start(bf16[2,3,256,256]{3,2,1,0:T(8,128)(2,1)S(1)} %copy-done.39), channel_id=1, source_target_pairs={{0,2},{2,0},{1,3},{3,1},{4,6},{6,4},{5,7},{7,5},{8,10},{10,8},{9,1... | collective-permute-start | bytes 2359304 | tf_op jit(solution)/shard_map/ppermute | solution.py:27
  282.5 25.5 %collective-permute-start.24 = (bf16[2,256,1024]{2,1,0:T(8,128)(2,1)S(1)}, bf16[2,256,1024]{2,1,0:T(8,128)(2,1)}, u32[]{:S(2)}, u32[]{:S(2)}) collective-permute-start(bf16[2,256,1024]{2,1,0:T(8,128)(2,1)S(1)} %add_convert_fusion.1.refs_14_), channel_id=1, source_target_pairs={{0,2},{2,0},{1,3},{3,1},{4,6},{6,4},{5,7},{7,5},{8,10},{10,8},{9,1... | collective-permute-start | bytes 3145736 | tf_op jit(solution)/shard_map/ppermute | solution.py:27
  299.5 20.9 %collective-permute-start.26 = (bf16[2,256,1024]{2,1,0:T(8,128)(2,1)}, bf16[2,256,1024]{2,1,0:T(8,128)(2,1)}, u32[]{:S(2)}, u32[]{:S(2)}) collective-permute-start(bf16[2,256,1024]{2,1,0:T(8,128)(2,1)} %get-tuple-element.171), channel_id=1, source_target_pairs={{0,1},{1,0},{2,3},{3,2},{4,5},{5,4},{6,7},{7,6},{8,9},{9,8},{10,11... | collective-permute-start | bytes 3145736 | tf_op jit(solution)/shard_map/ppermute | solution.py:27
  301.3 19.0 %collective-permute-start.27 = (bf16[4,128,512]{2,1,0:T(8,128)(2,1)S(1)}, bf16[4,128,512]{2,1,0:T(8,128)(2,1)}, u32[]{:S(2)}, u32[]{:S(2)}) collective-permute-start(bf16[4,128,512]{2,1,0:T(8,128)(2,1)S(1)} %copy-done.12), channel_id=1, source_target_pairs={{0,4},{4,0},{1,5},{5,1},{2,6},{6,2},{3,7},{7,3},{8,12},{12,8},{9,1... | collective-permute-start | bytes 1572872 | tf_op jit(solution)/shard_map/ppermute | solution.py:27
  301.4 26.7 %collective-permute-start.22 = (bf16[1,256,1024]{2,1,0:T(8,128)(2,1)}, bf16[1,256,1024]{2,1,0:T(8,128)(2,1)}, u32[]{:S(2)}, u32[]{:S(2)}) collective-permute-start(bf16[1,256,1024]{2,1,0:T(8,128)(2,1)} %get-tuple-element.164), channel_id=1, source_target_pairs={{0,1},{1,0},{2,3},{3,2},{4,5},{5,4},{6,7},{7,6},{8,9},{9,8},{10,11... | collective-permute-start | bytes 1572872 | tf_op jit(solution)/shard_map/ppermute | solution.py:27
  307.9 20.2 %collective-permute-start.25 = (bf16[1,256,1024]{2,1,0:T(8,128)(2,1)}, bf16[1,256,1024]{2,1,0:T(8,128)(2,1)S(1)}, u32[]{:S(2)}, u32[]{:S(2)}) collective-permute-start(bf16[1,256,1024]{2,1,0:T(8,128)(2,1)} %add_convert_fusion.5), channel_id=1, source_target_pairs={{0,2},{2,0},{1,3},{3,1},{4,6},{6,4},{5,7},{7,5},{8,10},{10,8},{9,1... | collective-permute-start | bytes 1572872 | tf_op jit(solution)/shard_map/ppermute | solution.py:27
  320.3 18.8 %collective-permute-start.29 = (bf16[4,128,768]{2,1,0:T(8,128)(2,1)}, bf16[4,128,768]{2,1,0:T(8,128)(2,1)S(1)}, u32[]{:S(2)}, u32[]{:S(2)}) collective-permute-start(bf16[4,128,768]{2,1,0:T(8,128)(2,1)} %get-tuple-element.191), channel_id=1, source_target_pairs={{0,4},{4,0},{1,5},{5,1},{2,6},{6,2},{3,7},{7,3},{8,12},{12,8},{9,1... | collective-permute-start | bytes 2359304 | tf_op jit(solution)/shard_map/ppermute | solution.py:27
  348.5 15.0 %collective-permute-start.34 = (bf16[2,38,1024]{2,1,0:T(8,128)(2,1)S(1)}, bf16[2,38,1024]{2,1,0:T(8,128)(2,1)S(1)}, u32[]{:S(2)}, u32[]{:S(2)}) collective-permute-start(bf16[2,38,1024]{2,1,0:T(8,128)(2,1)S(1)} %maximum_select_fusion.3), channel_id=1, source_target_pairs={{0,24},{8,16},{16,8},{24,0},{1,25},{9,17},{17,9},{25,1},{2,26},{10... | collective-permute-start | bytes 466952 | tf_op jit(solution)/shard_map/ppermute | solution.py:995
  354.9 39.0 %collective-permute-start.33 = (bf16[2,38,1024]{2,1,0:T(8,128)(2,1)S(1)}, bf16[2,38,1024]{2,1,0:T(8,128)(2,1)S(1)}, u32[]{:S(2)}, u32[]{:S(2)}) collective-permute-start(bf16[2,38,1024]{2,1,0:T(8,128)(2,1)S(1)} %maximum_select_fusion.3), channel_id=1, source_target_pairs={{0,16},{8,24},{16,0},{24,8},{1,17},{9,25},{17,1},{25,9},{2,18},{10... | collective-permute-start | bytes 466952 | tf_op jit(solution)/shard_map/ppermute | solution.py:995
  354.9 39.0 %collective-permute-start.32 = (bf16[2,38,1024]{2,1,0:T(8,128)(2,1)S(1)}, bf16[2,38,1024]{2,1,0:T(8,128)(2,1)S(1)}, u32[]{:S(2)}, u32[]{:S(2)}) collective-permute-start(bf16[2,38,1024]{2,1,0:T(8,128)(2,1)S(1)} %maximum_select_fusion.3), channel_id=1, source_target_pairs={{0,8},{8,0},{16,24},{24,16},{1,9},{9,1},{17,25},{25,17},{2,10},{10... | collective-permute-start | bytes 466952 | tf_op jit(solution)/shard_map/ppermute | solution.py:995
  355.7 41.7 %collective-permute-start.39 = (bf16[128,1280]{1,0:T(8,128)(2,1)S(1)}, bf16[128,1280]{1,0:T(8,128)(2,1)S(1)}, u32[]{:S(2)}, u32[]{:S(2)}) collective-permute-start(bf16[128,1280]{1,0:T(8,128)(2,1)S(1)} %get-tuple-element.207), channel_id=1, source_target_pairs={{0,24},{8,16},{16,8},{24,0},{1,25},{9,17},{17,9},{25,1},{2,26},{10... | collective-permute-start | bytes 983048 | tf_op jit(solution)/shard_map/ppermute | solution.py:789
  359.5 64.5 %collective-permute-start.38 = (bf16[128,1280]{1,0:T(8,128)(2,1)S(1)}, bf16[128,1280]{1,0:T(8,128)(2,1)S(1)}, u32[]{:S(2)}, u32[]{:S(2)}) collective-permute-start(bf16[128,1280]{1,0:T(8,128)(2,1)S(1)} %get-tuple-element.208), channel_id=1, source_target_pairs={{0,16},{8,24},{16,0},{24,8},{1,17},{9,25},{17,1},{25,9},{2,18},{10... | collective-permute-start | bytes 983048 | tf_op jit(solution)/shard_map/ppermute | solution.py:789
  363.5 60.5 %collective-permute-start.37 = (bf16[128,1280]{1,0:T(8,128)(2,1)S(1)}, bf16[128,1280]{1,0:T(8,128)(2,1)S(1)}, u32[]{:S(2)}, u32[]{:S(2)}) collective-permute-start(bf16[128,1280]{1,0:T(8,128)(2,1)S(1)} %get-tuple-element.206), channel_id=1, source_target_pairs={{0,8},{8,0},{16,24},{24,16},{1,9},{9,1},{17,25},{25,17},{2,10},{10... | collective-permute-start | bytes 983048 | tf_op jit(solution)/shard_map/ppermute | solution.py:789
  424.1 10.7 %collective-permute-start.40 = (bf16[128,1280]{1,0:T(8,128)(2,1)S(1)}, bf16[128,1280]{1,0:T(8,128)(2,1)S(1)}, u32[]{:S(2)}, u32[]{:S(2)}) collective-permute-start(bf16[128,1280]{1,0:T(8,128)(2,1)S(1)} %add_convert_fusion.6), channel_id=1, source_target_pairs={{0,2},{2,0},{1,3},{3,1},{4,6},{6,4},{5,7},{7,5},{8,10},{10,8},{9,1... | collective-permute-start | bytes 983048 | tf_op jit(solution)/shard_map/ppermute | solution.py:27
  426.2 18.4 %collective-permute-start.35 = (bf16[256,1024]{1,0:T(8,128)(2,1)}, bf16[256,1024]{1,0:T(8,128)(2,1)S(1)}, u32[]{:S(2)}, u32[]{:S(2)}) collective-permute-start(bf16[256,1024]{1,0:T(8,128)(2,1)} %bitcast.96), channel_id=1, source_target_pairs={{0,2},{2,0},{1,3},{3,1},{4,6},{6,4},{5,7},{7,5},{8,10},{10,8},{9,1... | collective-permute-start | bytes 1572872 | tf_op jit(solution)/shard_map/ppermute | solution.py:27
  (62 other events, 306.8 us)
Sparse Core Ops, SparseCore 0:
  184.8 98.5 reduce-scatter.6
  334.8 76.0 reduce-scatter.4

commit v3 on v2

--- a/solution.py
+++ b/solution.py
@@ -192,7 +192,7 @@
     )
 
 
-def qkv_grads(x_at, pieces, grad, blocks):
+def qkv_grads(x_at, pieces, grad, blocks, deps=()):
     rows, shard, model = pieces[0].shape
     tokens = rows * shard
     parts, columns = len(pieces), grad.shape[3]
@@ -225,6 +225,7 @@
         body, "qkv_grads", (x_at.astype(jnp.int32)[None],), (columns // BLOCK,),
         [(x, fixed(x.shape)) for x in pieces] + [(grad, along((parts, rows, shard, BLOCK), 3))],
         [(shape, BF16, block), (shape, BF16, block), ((1, columns), F32, along((1, BLOCK), 1))],
+        deps=deps,
     )
 
 
@@ -597,47 +598,35 @@
     )
 
 
-def both_body(cot_ref, grad_ref, act_ref, tok_ref, out_ref):
-    half, rows, model = out_ref.shape[1], out_ref.shape[3], out_ref.shape[4]
-    size = act_ref.shape[1] // (2 * half)
-    rest = tok_ref.shape[1] // (2 * half)
-    down = dot(act_ref[...], cot_ref[...], 0, 0).astype(BF16)
-    up = dot(tok_ref[...], grad_ref[...], 0, 0).astype(BF16)
-    for x in range(2):
-        for y in range(half):
-            n = half * x + y
-            out_ref[x, y, 0, 0:size] = down[n * size : (n + 1) * size]
-            for s in range(2):
-                at = size + s * rest
-                out_ref[x, y, 0, at : at + rest] = up[n * rest : (n + 1) * rest, s * model : (s + 1) * model]
-
-
-def both_grads(act, cot, tokens, grad, depth):
-    count, half = act.shape
-    model = cot.shape[1]
-    size, rest = half // (4 * depth), model // (4 * depth)
-    shape = (2, 2, depth, size + 2 * rest, model)
-    if rest % 16 or size % 16:
-        down = dot(act, cot, 0, 0).astype(BF16).reshape(depth, 2, 2, size, model)
-        up = dot(tokens, grad, 0, 0).astype(BF16).reshape(depth, 2, 2, rest, 2, model)
-        up = up.transpose(0, 1, 2, 4, 3, 5).reshape(depth, 2, 2, 2 * rest, model)
-        return jnp.concatenate([down, up], axis=3).transpose(1, 2, 0, 3, 4)
-    return call(
-        both_body, "both_grads", (), (depth,),
-        [
+def sent_body(other_ref, tok_ref, cot_ref, grad_ref, act_ref, up_ref, down_ref):
+    up_ref[...] = dot(tok_ref[...], grad_ref[...], 0, 0).astype(BF16)
+    down_ref[...] = dot(act_ref[...], cot_ref[...], 0, 0).astype(BF16)
+
+
+def sent_grads(other, tokens, cot, grad, act, steps):
+    count, model = tokens.shape
+    half = grad.shape[1]
+    size = half // (2 * steps)
+    wide = half // steps
+    return call(
+        sent_body, "sent_grads", (other,), (steps,),
+        [
+            (tokens, fixed(tokens.shape)),
             (cot, fixed(cot.shape)),
-            (grad, fixed(grad.shape)),
-            (act, along((count, half // depth), 1)),
-            (tokens, along((count, model // depth), 1)),
-        ],
-        [(shape, BF16, along((2, 2, 1) + shape[3:], 2))],
-    )[0]
-
-
-def feed_body(order_ref, act_ref, down_ref, att_ref, low_ref, feed_ref, out_ref, keep_ref):
+            (grad, along((count, wide), 1)),
+            (act, pl.BlockSpec((count, size), lambda g, o: (0, 2 * g + o[0]))),
+        ],
+        [((model, half), BF16, along((model, wide), 1)), ((half // 2, model), BF16, along((size, model)))],
+    )
+
+
+def feed_body(order_ref, act_ref, down_ref, att_ref, low_ref, half_ref, cot_ref, feed_ref, other_ref, out_ref, keep_ref, kept_ref):
     parts = order_ref.shape[0]
     width = att_ref.shape[1] // parts
-    feed_ref[...] = dot(act_ref[...], down_ref[...]).astype(BF16)
+    feed = dot(act_ref[...], down_ref[...]).astype(BF16)
+    feed_ref[...] = feed[: feed_ref.shape[0]]
+    other_ref[...] = feed[feed_ref.shape[0] :]
+    kept_ref[...] = dot(half_ref[...], cot_ref[...], 0, 0).astype(BF16)
     grad = dot(att_ref[...], low_ref[...], 0, 0).astype(BF16)
     step, steps = pl.program_id(0), pl.num_programs(0)
 
@@ -655,11 +644,12 @@
         write(keep_ref)
 
 
-def feed_grads(order, act, down, attended, low, c_at, deps=()):
+def feed_grads(order, act, down, attended, low, cot, c_at, x_at, deps=()):
     tokens, half = act.shape
     own, model = attended.shape
     steps = model // BLOCK
-    place = jnp.concatenate([order, c_at.astype(jnp.int32)[None]])
+    place = jnp.concatenate([order, jnp.stack([c_at, x_at]).astype(jnp.int32)])
+    size = half // (2 * steps)
 
     def body(place_ref, *refs):
         feed_body(place_ref.at[0 : order.shape[0]], *refs)
@@ -676,11 +666,15 @@
             (down, along((half, BLOCK), 1)),
             (attended, fixed(attended.shape)),
             (low, pl.BlockSpec((own, BLOCK), low_at)),
-        ],
-        [
-            ((tokens, model), BF16, along((tokens, BLOCK), 1)),
+            (act, pl.BlockSpec((tokens, size), lambda g, p: (0, 2 * g + p[order.shape[0] + 1]))),
+            (cot, fixed(cot.shape)),
+        ],
+        [
+            ((own, model), BF16, along((own, BLOCK), 1)),
+            ((own, model), BF16, along((own, BLOCK), 1)),
             ((model, model // 2), BF16, pl.BlockSpec((model, BLOCK), lambda g, p: (0, jnp.minimum(g, steps // 2 - 1)))),
             ((model, model // 2), BF16, pl.BlockSpec((model, BLOCK), lambda g, p: (0, jnp.maximum(g - steps // 2, 0)))),
+            ((half // 2, model), BF16, along((size, model))),
         ],
         deps=deps,
     )
@@ -794,22 +788,16 @@
     return jnp.where(at == 0, jnp.concatenate([own, other], axis), jnp.concatenate([other, own], axis))
 
 
-def finish_body(blocks, at_ref, g0, g1, l0, l1, down_ref, up_ref, qkv_ref, out_ref):
+def finish_body(blocks, at_ref, d0, d1, u0, u1, l0, l1, down_ref, up_ref, qkv_ref, out_ref):
     c_at = at_ref[0]
     width = up_ref.shape[1] // (4 * blocks)
-    rest = up_ref.shape[0] // 2
-    size = g0.shape[1] - 2 * rest
+    size = d0.shape[0]
     for c in range(2):
         mine = c_at == c
-        for y in range(2):
-            grads = jnp.where(mine, g0[y], g1[y]).astype(F32)
-            at = (2 * c + y) * size
-            down_ref[at : at + size] = grads[0:size]
-            for b in range(2 * blocks):
-                s, at = b // blocks, b % blocks * width
-                up_ref[y * rest : (y + 1) * rest, (2 * b + c) * width : (2 * b + c + 1) * width] = grads[
-                    size + s * rest : size + (s + 1) * rest, at : at + width
-                ]
+        down_ref[c * size : (c + 1) * size] = jnp.where(mine, d0[...], d1[...]).astype(F32)
+        up = jnp.where(mine, u0[...], u1[...]).astype(F32)
+        for b in range(2 * blocks):
+            up_ref[:, (2 * b + c) * width : (2 * b + c + 1) * width] = up[:, b * width : (b + 1) * width]
         late = jnp.where(mine, l0[...], l1[...]).astype(F32)
         half = out_ref.shape[1] // 2
         wide = half // 2
@@ -820,21 +808,19 @@
                 qkv_ref[:, at : at + wide] = late[:, (3 * y + n) * wide : (3 * y + n + 1) * wide]
 
 
-def finish(c_at, dp, piece, grads, late, parts):
-    rows, model = late[0].shape[0], grads[0].shape[2]
-    depth, rest = dp // 2, rows // 2
-    size = grads[0].shape[1] - 2 * rest
+def finish(c_at, dp, piece, down, up, late, parts):
+    rows, model = late[0].shape[0], down[0].shape[1]
+    depth, size = dp // 2, down[0].shape[0]
     if piece % 128 == 0:
         at = c_at.astype(jnp.int32)[None]
-        shapes = [(4 * size, model), (rows, 2 * dp * piece), (rows, 3 * model), (rows, model)]
-        arrays = list(grads) + list(late)
+        shapes = [(2 * size, model), (rows, 2 * dp * piece), (rows, 3 * model), (rows, model)]
+        arrays = list(down) + list(up) + list(late)
         return call(
             functools.partial(finish_body, depth), "finish", (at,), (1,),
             [(array, fixed(array.shape)) for array in arrays], [(shape, F32, fixed(shape)) for shape in shapes],
         )
-    both = ordered(c_at, grads[0][None], grads[1][None], 0)
-    down_done = both[:, :, :size].reshape(4 * size, model).astype(F32)
-    up_done = both[:, :, size:].reshape(2, 2, 2, rest, depth, piece).transpose(1, 3, 2, 4, 0, 5)
+    down_done = ordered(c_at, *down, 0).astype(F32)
+    up_done = ordered(c_at, up[0][None], up[1][None], 0).reshape(2, rows, dp, piece).transpose(1, 2, 0, 3)
     up_done = up_done.reshape(rows, 2 * dp * piece).astype(F32)
     both = ordered(c_at, late[0][None], late[1][None], 0)
     width = model // parts
@@ -936,44 +922,80 @@
     sums2 = sums2[:4]
 
     active, grad_hidden, att0 = tie(active, grad_hidden, att0)
-    grads = both_grads(active, cot_both, normed2_both, grad_hidden, depth)
-    grads = lax.psum_scatter(grads.reshape((4,) + grads.shape[2:]), ("x", "y"), scatter_dimension=0, tiled=False)
-    feed, out_sent, out_grad = feed_grads(
-        order_list, active, down_own, attended_all.reshape(tokens, model), grad_middle_low.reshape(tokens, model), c_at,
-        (far,),
-    )
+    up_rows = model // dp
+    small_blocks = piece % BLOCK != 0 or depth != model // BLOCK
+    if small_blocks:
+        up_grad = dot(normed2_both, grad_hidden, 0, 0).astype(BF16)
+        down_out = dot(active, cot_both, 0, 0).astype(BF16).reshape(depth, 2, piece, model)
+        down_kept = lax.dynamic_index_in_dim(down_out, x_at, 1, keepdims=False).reshape(half // 2, model)
+        down_out = lax.dynamic_index_in_dim(down_out, 1 - x_at, 1, keepdims=False).reshape(half // 2, model)
+    else:
+        up_grad, down_out = sent_grads(
+            1 - x_at[None].astype(jnp.int32), normed2_both, cot_both, grad_hidden, active, depth
+        )
+    up_grad, down_out, far = tie(up_grad, down_out, far)
+    up_z = lax.psum_scatter(up_grad, "z", scatter_dimension=0, tiled=True)
+    down_sent = swap(down_out[: half // 4], "x")
+    if small_blocks:
+        feed = dot(active, down_own).astype(BF16)
+        feed, feed_other = feed[:tokens], feed[tokens:]
+        out_grad = dot(attended_all.reshape(tokens, model), grad_middle_low.reshape(tokens, model), 0, 0).astype(BF16)
+        out_grad = jnp.concatenate([cut(out_grad, o_at, width, 0) for o_at in order], axis=0)
+        out_sent, out_grad = (cut(out_grad, at, model // 2, 1) for at in (1 - c_at, c_at))
+    else:
+        feed, feed_other, out_sent, out_grad, down_kept = feed_grads(
+            order_list, active, down_own, attended_all.reshape(tokens, model), grad_middle_low.reshape(tokens, model),
+            cot_both, c_at, x_at, (far, down_out),
+        )
+    feed, feed_other, out_sent, out_grad, down_kept, down_sent, down_out = tie(
+        feed, feed_other, out_sent, out_grad, down_kept, down_sent, down_out
+    )
+    down_late = swap(down_out[half // 4 :], "x")
     out_sent = swap(out_sent, "c")
-    feed = feed[:tokens].astype(F32) + swap(feed[tokens:], "c").astype(F32) + down_bias.astype(F32)
+    feed = feed.astype(F32) + swap(feed_other, "c").astype(F32) + down_bias.astype(F32)
     output = (middle + feed.reshape(rows, shard, model)).astype(BF16)
-    up_rows = model // dp
     out_c = add_low(out_grad, out_sent)
 
-    output, out_c, far = tie(output, out_c, far)
+    output, out_c, far, down_kept = tie(output, out_c, far, down_kept)
+    out_sent = swap(cut(out_c, 1 - y_at, width, 1), "y")
     grad_o = exchange(att0, att1, far)
-    grad_qkv, back = (), []
-    for start, count in groups:
-        grad_qkv, own, one, two, three = attend_back(
-            start, count, cnt, idx, qkv, o, grad_o, lse, segs, cos_tab, sin_tab, qkv_own, grad_qkv,
-            (there, out_x) if back else (),
+    back = []
+    (start, count), rest = groups[0], groups[1:]
+    found = attend_back(start, count, cnt, idx, qkv, o, grad_o, lse, segs, cos_tab, sin_tab, qkv_own)
+    *found, down_late, out_sent = tie(*found, down_late, out_sent)
+    grad_qkv, own, one, two, three = found
+    there = add_low(two, swap(three, "c"))
+    down_x = add_low(down_kept, jnp.concatenate([down_sent, down_late], axis=0))
+    down_z = lax.psum_scatter(down_x, "z", scatter_dimension=0, tiled=True)
+    out_y = add_low(cut(out_c, y_at, width, 1), out_sent).reshape(depth, 2 * up_rows, width)
+    out_sent = cut(out_y, 1 - x_at, up_rows, 1)
+    there, down_x, out_sent = tie(there, down_x, out_sent)
+    far, near = swap(there, "y"), swap(one, "c")
+    out_sent = swap(out_sent, "x")
+    if rest:
+        (start, count), = rest
+        found = attend_back(
+            start, count, cnt, idx, qkv, o, grad_o, lse, segs, cos_tab, sin_tab, qkv_own, (grad_qkv,),
+            (there, down_x),
         )
-        grad_qkv = (grad_qkv,)
-        there = add_low(two, swap(three, "c"))
-        if not back:
-            own, out_c = tie(own, out_c.reshape(depth, 2 * up_rows, model // 2))
-            out_x = cut(out_c, 1 - x_at, up_rows, 1)
-        back.append((own, swap(one, "c"), swap(there, "y")))
-    grad_qkv, there, far = tie(grad_qkv[0], there, back[0][2])
-    back[0] = back[0][:2] + (far,)
-    back[-1] = back[-1][:2] + (swap(there, "y"),)
-    qkv_out, qkv_kept, qkv_b = qkv_grads(x_at, [own1, one1, two1, three1], grad_qkv, depth)
+        *found, far, up_z, out_sent = tie(*found, far, up_z, out_sent)
+        back.append((own, near, far))
+        grad_qkv, own, one, two, three = found
+        there, far = tie(add_low(two, swap(three, "c")), far)
+        far, near = swap(there, "y"), swap(one, "c")
+        grad_qkv, there = tie(grad_qkv, there)
+    up_out = cut(up_z, 1 - x_at, up_rows, 0)
+    up_sent = swap(up_out, "x")
+    qkv_out, qkv_kept, qkv_b = qkv_grads(x_at, [own1, one1, two1, three1], grad_qkv, depth, (up_out,))
+    qkv_out, qkv_kept, far, up_sent = tie(qkv_out, qkv_kept, far, up_sent)
+    back.append((own, near, far))
     qkv_sent = swap(qkv_out, "x")
-    qkv_kept, out_c, grads, out_x = tie(qkv_kept, out_c, grads, swap(out_x, "x"))
-    grads = lax.psum_scatter(grads, "z", scatter_dimension=0, tiled=False)
-    out_x = add_low(cut(out_c, x_at, up_rows, 1), out_x)
+    up_x = add_low(cut(up_z, x_at, up_rows, 0), up_sent)
+    out_x = add_low(cut(out_y, x_at, up_rows, 1), out_sent)
     held, grad_shift, sums1 = (), [], 0.0
     for (start, count), values in zip(groups, back):
         input_grad, found, sums = norm1_back(
-            start, count, *values, stream, grad_middle, norm1_gain, segment_ids, held, (out_x if held else qkv_kept,)
+            start, count, *values, stream, grad_middle, norm1_gain, segment_ids, held, (out_x, up_x, qkv_kept)
         )
         held = (input_grad,)
         grad_shift.append(found.reshape(count * SEGS, model))
@@ -991,6 +1013,8 @@
     late, late_parts = over_z(qkv_x, z_at, depth)
     small = add_low(small, swap(small, "y"))
     small = ordered(x_at, small[None], swap(small, "x")[None], 0)
+    small, down_z, up_x = tie(small, down_z, up_x)
+    down_sent, up_sent = swap(down_z, "y"), swap(up_x, "y")
     if depth == 4:
         others = [lax.ppermute(small, "z", [(i, i ^ n) for i in range(depth)]) for n in range(1, depth)]
         small = jnp.stack([small] + others)
@@ -999,18 +1023,17 @@
         small = lax.all_gather(small, "z")
     small = small.reshape(dp, small.shape[2], model)
 
-    small, late = tie(small, late)
+    small, late, down_sent, up_sent = tie(small, late, down_sent, up_sent)
+    down_done, up_done = add_low(down_z, down_sent), add_low(up_x, up_sent)
+    down_other, up_other = swap(down_done, "c"), swap(up_done, "c")
     late = (late + sum(part.astype(F32) for part in late_parts)).astype(BF16) if depth == 4 else late
     late_sent = swap(late, "y")
-    qkv_y = ordered(y_at, late[None, :, : 3 * width], late_sent[None, :, : 3 * width], 0)
-    out_y = add_low(late[:, 3 * width :], late_sent[:, 3 * width :])
-    late = jnp.concatenate([qkv_y[0], qkv_y[1], out_y], axis=1)
+    both = ordered(y_at, late[None], late_sent[None], 0)
+    late = jnp.concatenate([both[0, :, : 3 * width], both[1, :, : 3 * width], both[0, :, 3 * width :], both[1, :, 3 * width :]], axis=1)
     late_other = swap(late, "c")
-    grads = ordered(y_at, grads[None], swap(grads, "y")[None], 0)
-    grads_other = swap(grads, "c")
 
     down_done, up_done, qkv_done, out_done = finish(
-        c_at, dp, piece, (grads, grads_other), (late, late_other), parts
+        c_at, dp, piece, (down_done, down_other), (up_done, up_other), (late, late_other), parts
     )
 
     all_times = small[:, -1, : 2 * rows * SEGS].astype(F32) * 0.25

time: 472 us -> 411 us (0.87)
  waiting for transfers between devices: 143 us -> 62.9 us
  starting transfers between devices: 39.7 us -> 49.1 us
  other arithmetic: 21.4 us -> 29.7 us
    ppermute x36 -> x42, waiting for transfers between devices: 90.6 us -> 40.5 us  [swap(): return lax.ppermute(value, axis, [(0, 1), (1, 0)])]
    ppermute x36 -> x42, starting transfers between devices: 20.1 us -> 38.4 us  [swap(): return lax.ppermute(value, axis, [(0, 1), (1, 0)])]
    ppermute x3, waiting for transfers between devices: 26.6 us -> 9.32 us  [over_z(): lax.ppermute(parts[n], 'z', [(i, i ^ n) for i in range(depth)])]
    ppermute x3, waiting for transfers between devices: 25.7 us -> 13 us  [local(): lax.ppermute(small, 'z', [(i, i ^ n) for i in range(depth)])]
    convert_element_type x8 -> x12, other arithmetic: 6.19 us -> 14.3 us  [add_low(): return (kept.astype(F32) + sent.astype(F32)).astype(BF16)]
    ppermute x3, starting transfers between devices: 12.5 us -> 4.94 us  [over_z(): lax.ppermute(parts[n], 'z', [(i, i ^ n) for i in range(depth)])]
    unnamed x88 -> x96, local copies, waits for them, and re-layouts: 12.7 us -> 10.7 us
  transfers between devices with their start and end apart: 44 -> 50, of which waited for: 21 -> 22; matrix products, arithmetic and copies ran while one was open for 8% -> 12% of each run, Pallas kernels for 27% -> 38%
where the time goes in v3:
time: 411 us; the launch traced here: 403 us
  Pallas kernels  217 us (53%)
  waiting for transfers between devices  62.9 us (15%)
  starting transfers between devices  49.1 us (12%)
  other arithmetic  29.7 us (7%)
  local copies, waits for them, and re-layouts  26.4 us (6%)
  between operations  15.3 us (4%)
    pallas_call x18, Pallas kernels, call(): pl.pallas_call(kernel, grid_spec=pltpu.PrefetchScalarGridSpec(num_scalar_...  217 us
    ppermute x42, waiting for transfers between devices, swap(): return lax.ppermute(value, axis, [(0, 1), (1, 0)])  40.5 us
    ppermute x42, starting transfers between devices, swap(): return lax.ppermute(value, axis, [(0, 1), (1, 0)])  38.4 us
    convert_element_type x12, other arithmetic, add_low(): return (kept.astype(F32) + sent.astype(F32)).astype(BF16)  14.3 us
    ppermute x3, waiting for transfers between devices, local(): lax.ppermute(small, 'z', [(i, i ^ n) for i in range(depth)])  13 us
    unnamed x96, local copies, waits for them, and re-layouts  10.7 us
    ppermute x3, waiting for transfers between devices, over_z(): lax.ppermute(parts[n], 'z', [(i, i ^ n) for i in range(depth)])  9.32 us
  transfers between devices with their start and end apart: 50, of which 22 were waited for; matrix products, arithmetic and copies ran while one was open for 12% of the time, Pallas kernels for 38%

profile of v3, /device:TPU:0, one launch (start us, length us, event | category | flops | bytes accessed | tf_op | source)
XLA Modules:
  0.0 403.5 jit_solution(15977534526309331018)
XLA Ops:
  13.7 4.6 %norm1.1 = (f32[3,256,1024]{2,1,0:T(8,128)}, bf16[3,256,1024]{2,1,0:T(8,128)(2,1)}) custom-call(bf16[3,256,1024]{2,1,0:T(8,128)(2,1)} %refs_0_.1, s32[3,256]{1,0:T(4,128)} %refs_6_.9, f32[3,8,1024]{2,1,0:T(8,128)} %convolution_bitcast_fusion.refs_2_, bf16[1024]{0:T(1024)(128)(2,1)} %refs_3_.4, bf16[1024]{0:T(1024)(128)(2,1)} %refs_5_.11, bf16[1024]{0:T(1024)(128)(2,1)} %refs_5_.6), custom_call_target="tpu_custom_call" | custom-call | tf_op jit(solution)/shard_map/norm1/pallas_call | solution.py:94
  26.7 15.8 %cot_down.1 = (bf16[1536,2048]{1,0:T(8,128)(2,1)}, bf16[1024,2048]{1,0:T(8,128)(2,1)}, bf16[2048,1024]{1,0:T(8,128)(2,1)}, bf16[1536,1024]{1,0:T(8,128)(2,1)}) custom-call(s32[8]{0:T(128)} %multiply_add_fusion.refs_0_, bf16[768,1024]{1,0:T(8,128)(2,1)} %bitcast.79, bf16[768,1024]{1,0:T(8,128)(2,1)} %collective-permute-done.5.refs_2_, ...), custom_call_target="tpu_custom_call" | custom-call | tf_op jit(solution)/shard_map/cot_down/pallas_call | solution.py:94
  43.6 7.4 %qkv.2 = (bf16[3,4,3,256,256]{4,3,2,1,0:T(8,128)(2,1)}, bf16[768,1024]{1,0:T(8,128)(2,1)}) custom-call(s32[1]{0:T(128)} %bitcast.2.refs_0_, bf16[3,256,1024]{2,1,0:T(8,128)(2,1)} %get-tuple-element.148.refs_1_, bf16[3,256,1024]{2,1,0:T(8,128)(2,1)} %copy-done.9, bf16[1024,3072]{1,0:T(8,128)(2,1)} %refs_3_.7, bf16[1,3072]{1,0:T(2,128)(2,1)} %reshape.316.refs_4_, ...), custom_call_target="tpu_custom_call" | custom-call | tf_op jit(solution)/shard_map/qkv/pallas_call | solution.py:94
  51.0 4.8 %collective-permute-done.3.refs_1_.refs_3_ = bf16[3,256,1024]{2,1,0:T(8,128)(2,1)S(1)} collective-permute-done((bf16[3,256,1024]{2,1,0:T(8,128)(2,1)}, bf16[3,256,1024]{2,1,0:T(8,128)(2,1)S(1)}, u32[]{:S(2)}, u32[]{:S(2)}) %collective-permute-start.3) | collective-permute-done | bytes 1572896 | tf_op jit(solution)/shard_map/ppermute | solution.py:27
  60.5 7.4 %qkv.3 = (bf16[3,4,3,256,256]{4,3,2,1,0:T(8,128)(2,1)}, bf16[768,1024]{1,0:T(8,128)(2,1)}) custom-call(s32[1]{0:T(128)} %bitcast.2.refs_0_, bf16[3,256,1024]{2,1,0:T(8,128)(2,1)} %copy-done.10, bf16[3,256,1024]{2,1,0:T(8,128)(2,1)} %copy-done.11, bf16[1024,3072]{1,0:T(8,128)(2,1)} %refs_3_.7, ...), custom_call_target="tpu_custom_call", output_to_operand_aliasing={{0}: (7, {})} | custom-call | tf_op jit(solution)/shard_map/qkv/pallas_call | solution.py:94
  67.9 13.8 %attend.2 = (bf16[4,3,256,256]{3,2,1,0:T(8,128)(2,1)}, bf16[2,256,256]{2,1,0:T(8,128)(2,1)}, bf16[2,2,256,256]{3,2,1,0:T(8,128)(2,1)}, f32[3,4,8,256]{3,2,1,0:T(8,128)}) custom-call(s32[12]{0:T(128)} %reshape.314.refs_0_, s32[48]{0:T(128)} %reshape.315.refs_1_, bf16[3,4,3,256,256]{4,3,2,1,0:T(8,128)(2,1)} %get-tuple-element.154.refs_2_, s32[3,4,256]{2,1,0:T(4,128)} %copy-done.34), custom_call_target="tpu_custom_call" | custom-call | tf_op jit(solution)/shard_map/attend/pallas_call | solution.py:94
  83.4 10.5 %attend.3 = (bf16[4,3,256,256]{3,2,1,0:T(8,128)(2,1)}, bf16[1,256,256]{2,1,0:T(8,128)(2,1)}, bf16[2,1,256,256]{3,2,1,0:T(8,128)(2,1)}, f32[3,4,8,256]{3,2,1,0:T(8,128)}) custom-call(s32[12]{0:T(128)} %reshape.314.refs_0_, s32[48]{0:T(128)} %reshape.315.refs_1_, ...), custom_call_target="tpu_custom_call", output_to_operand_aliasing={{0}: (4, {}), {3}: (5, {})} | custom-call | tf_op jit(solution)/shard_map/attend/pallas_call | solution.py:94
  99.2 6.1 %middle.2 = (f32[3,256,1024]{2,1,0:T(8,128)}, bf16[2,256,1024]{2,1,0:T(8,128)(2,1)}, bf16[3,256,1024]{2,1,0:T(8,128)(2,1)}) custom-call(s32[4]{0:T(128)} %pad_add_fusion.1.refs_0_, bf16[4,3,256,256]{3,2,1,0:T(8,128)(2,1)} %get-tuple-element.161.refs_1_.refs_3_, bf16[2,256,256]{2,1,0:T(8,128)(2,1)} %copy-done.35, bf16[2,2,256,256]{3,2,1,0:T(8,128)(2,1)} %copy-done.22, ...), custom_call_target="tpu_custom_call" | custom-call | tf_op jit(solution)/shard_map/middle/pallas_call | solution.py:94
  109.0 4.9 %middle.3 = (f32[3,256,1024]{2,1,0:T(8,128)}, bf16[1,256,1024]{2,1,0:T(8,128)(2,1)}, bf16[3,256,1024]{2,1,0:T(8,128)(2,1)}) custom-call(s32[4]{0:T(128)} %pad_add_fusion.1.refs_0_, bf16[4,3,256,256]{3,2,1,0:T(8,128)(2,1)} %get-tuple-element.161.refs_1_.refs_3_, bf16[1,256,256]{2,1,0:T(8,128)(2,1)} %copy-done.37, ...), custom_call_target="tpu_custom_call", output_to_operand_aliasing={{0}: (13, {}), {2}: (14, {})} | custom-call | tf_op jit(solution)/shard_map/middle/pallas_call | solution.py:94
  117.2 29.4 %hidden.1 = (bf16[1536,2048]{1,0:T(8,128)(2,1)}, bf16[1536,2048]{1,0:T(8,128)(2,1)}, f32[1,2048]{1,0:T(1,128)}, bf16[1536,1024]{1,0:T(8,128)(2,1)}, bf16[1536,1024]{1,0:T(8,128)(2,1)}) custom-call(s32[8]{0:T(128)} %multiply_add_fusion.refs_0_, bf16[2,256,1024]{2,1,0:T(8,128)(2,1)} %get-tuple-element.171.refs_1_, ...), custom_call_target="tpu_custom_call" | custom-call | tf_op jit(solution)/shard_map/hidden/pallas_call | solution.py:94
  152.7 9.7 %middle_back.1 = (f32[3,256,1024]{2,1,0:T(8,128)}, bf16[3,256,1024]{2,1,0:T(8,128)(2,1)}, bf16[3,256,256]{2,1,0:T(8,128)(2,1)}, bf16[3,256,256]{2,1,0:T(8,128)(2...) custom-call(s32[4]{0:T(128)} %pad_add_fusion.1.refs_0_, bf16[1536,1024]{1,0:T(8,128)(2,1)} %get-tuple-element.176.refs_1_, ...), custom_call_target="tpu_custom_call" | custom-call | tf_op jit(solution)/shard_map/middle_back/pallas_call | solution.py:94
  163.2 15.0 %sent_grads.1 = (bf16[1024,2048]{1,0:T(8,128)(2,1)}, bf16[1024,1024]{1,0:T(8,128)(2,1)}) custom-call(s32[1]{0:T(128)S(6)} %sub.19.refs_0_, bf16[1536,1024]{1,0:T(8,128)(2,1)} %get-tuple-element.183.refs_1_, bf16[1536,1024]{1,0:T(8,128)(2,1)} %get-tuple-element.182.refs_2_.refs_6_, bf16[1536,2048]{1,0:T(8,128)(2,1)} %get-tuple-element.184.refs_3_, ...), custom_call_target="tpu_custom_call" | custom-call | tf_op jit(solution)/shard_map/sent_grads/pallas_call | solution.py:94
  178.3 4.1 %collective-permute-done.16.refs_7_.refs_6_ = bf16[2,3,256,256]{3,2,1,0:T(8,128)(2,1)S(1)} collective-permute-done((bf16[2,3,256,256]{3,2,1,0:T(8,128)(2,1)}, bf16[2,3,256,256]{3,2,1,0:T(8,128)(2,1)S(1)}, u32[]{:S(2)}, u32[]{:S(2)}) %collective-permute-start.16) | collective-permute-done | bytes 786464 | tf_op jit(solution)/shard_map/ppermute | solution.py:27
  189.6 20.5 %feed_grads.1 = (bf16[768,1024]{1,0:T(8,128)(2,1)}, bf16[768,1024]{1,0:T(8,128)(2,1)}, bf16[1024,512]{1,0:T(8,128)(2,1)}, bf16[1024,512]{1,0:T(8,128)(2,1)}, bf16[1024,1024]{1,0:T(8,128)(2,1)}) custom-call(s32[6]{0:T(128)} %concatenate.55.refs_0_, bf16[1536,2048]{1,0:T(8,128)(2,1)} %get-tuple-element.178.refs_4_.refs_1_.refs_5_, ...), custom_call_target="tpu_custom_call" | custom-call | tf_op jit(solution)/shard_map/feed_grads/pallas_call | solution.py:94
  226.8 26.8 %attend_back.2 = (bf16[4,3,256,768]{3,2,1,0:T(8,128)(2,1)}, bf16[2,256,1024]{2,1,0:T(8,128)(2,1)}, bf16[2,256,1024]{2,1,0:T(8,128)(2,1)}, bf16[2,256,1024]{2,1,0:T(8,128)(2,1)}, bf16[2,256,1024]{2,1,0:T(8,128)(2,1)}) custom-call(s32[12]{0:T(128)} %reshape.314.refs_0_, s32[48]{0:T(128)} %reshape.315.refs_1_, ...), custom_call_target="tpu_custom_call" | custom-call | tf_op jit(solution)/shard_map/attend_back/pallas_call | solution.py:94
  255.0 4.7 %add_convert_fusion.refs_15_ = bf16[1024,1024]{1,0:T(8,128)(2,1)} fusion(bf16[1024,1024]{1,0:T(8,128)(2,1)} %get-tuple-element.217, bf16[512,1024]{1,0:T(8,128)(2,1)} %collective-permute-done.22, bf16[512,1024]{1,0:T(8,128)(2,1)} %collective-permute-done.17), kind=kLoop, calls=%fused_computation | loop fusion | flops 7340032 | bytes 6291456 | tf_op jit(solution)/shard_map/convert_element_type | solution.py:776
  262.9 5.9 %collective-permute-start.26 = (bf16[4,128,256]{2,1,0:T(8,128)(2,1)S(1)}, bf16[4,128,256]{2,1,0:T(8,128)(2,1)S(1)}, u32[]{:S(2)}, u32[]{:S(2)}) collective-permute-start(bf16[4,128,256]{2,1,0:T(8,128)(2,1)S(1)} %constant_dynamic-slice_fusion.11), channel_id=1, source_target_pairs={{0,4},{4,0},{1,5},{5,1},{2,6},{6,2},{3,7},{7,3},{8,12},{12,8},{9,1... | collective-permute-start | bytes 786440 | tf_op jit(solution)/shard_map/ppermute | solution.py:27
  269.0 20.3 %attend_back.3 = (bf16[4,3,256,768]{3,2,1,0:T(8,128)(2,1)}, bf16[1,256,1024]{2,1,0:T(8,128)(2,1)}, bf16[1,256,1024]{2,1,0:T(8,128)(2,1)}, bf16[1,256,1024]{2,1,0:T(8,128)(2,1)}, bf16[1,256,1024]{2,1,0:T(8,128)(2,1)}) custom-call(s32[12]{0:T(128)} %reshape.314.refs_0_, s32[48]{0:T(128)} %reshape.315.refs_1_, ...), custom_call_target="tpu_custom_call", output_to_operand_aliasing={{0}: (13, {})} | custom-call | tf_op jit(solution)/shard_map/attend_back/pallas_call | solution.py:94
  300.2 10.7 %qkv_grads.1 = (bf16[4,128,768]{2,1,0:T(8,128)(2,1)}, bf16[4,128,768]{2,1,0:T(8,128)(2,1)}, f32[1,768]{1,0:T(1,128)}) custom-call(s32[1]{0:T(128)} %bitcast.10.refs_0_, bf16[3,256,1024]{2,1,0:T(8,128)(2,1)} %get-tuple-element.148.refs_1_, bf16[3,256,1024]{2,1,0:T(8,128)(2,1)} %copy-done.9, bf16[3,256,1024]{2,1,0:T(8,128)(2,1)} %copy-done.10, ...), custom_call_target="tpu_custom_call" | custom-call | tf_op jit(solution)/shard_map/qkv_grads/pallas_call | solution.py:94
  314.6 5.5 %norm1_back.2 = (bf16[3,256,1024]{2,1,0:T(8,128)(2,1)}, f32[2,8,1024]{2,1,0:T(8,128)}, f32[8,1024]{1,0:T(8,128)}) custom-call(bf16[2,256,1024]{2,1,0:T(8,128)(2,1)} %get-tuple-element.243.refs_0_, bf16[2,256,1024]{2,1,0:T(8,128)(2,1)} %collective-permute-done.31.refs_1_, bf16[2,256,1024]{2,1,0:T(8,128)(2,1)} %copy-done.27, ...), custom_call_target="tpu_custom_call" | custom-call | tf_op jit(solution)/shard_map/norm1_back/pallas_call | solution.py:94
  340.7 5.0 %collective-permute-start.38 = (bf16[2,38,1024]{2,1,0:T(8,128)(2,1)S(1)}, bf16[2,38,1024]{2,1,0:T(8,128)(2,1)S(1)}, u32[]{:S(2)}, u32[]{:S(2)}) collective-permute-start(bf16[2,38,1024]{2,1,0:T(8,128)(2,1)S(1)} %maximum_select_fusion.1), channel_id=1, source_target_pairs={{0,24},{8,16},{16,8},{24,0},{1,25},{9,17},{17,9},{25,1},{2,26},{10... | collective-permute-start | bytes 466952 | tf_op jit(solution)/shard_map/ppermute | solution.py:1019
  354.6 11.0 %collective-permute-done.37 = bf16[2,38,1024]{2,1,0:T(8,128)(2,1)S(1)} collective-permute-done((bf16[2,38,1024]{2,1,0:T(8,128)(2,1)S(1)}, bf16[2,38,1024]{2,1,0:T(8,128)(2,1)S(1)}, u32[]{:S(2)}, u32[]{:S(2)}) %collective-permute-start.37) | collective-permute-done | bytes 155680 | tf_op jit(solution)/shard_map/ppermute | solution.py:1019
  369.2 9.3 %collective-permute-done.44 = bf16[128,1024]{1,0:T(8,128)(2,1)S(1)} collective-permute-done((bf16[128,1024]{1,0:T(8,128)(2,1)S(1)}, bf16[128,1024]{1,0:T(8,128)(2,1)S(1)}, u32[]{:S(2)}, u32[]{:S(2)}) %collective-permute-start.44) | collective-permute-done | bytes 262176 | tf_op jit(solution)/shard_map/ppermute | solution.py:783
  391.5 4.7 %finish.1 = (f32[512,1024]{1,0:T(8,128)}, f32[128,4096]{1,0:T(8,128)}, f32[128,3072]{1,0:T(8,128)}, f32[128,1024]{1,0:T(8,128)}) custom-call(s32[1]{0:T(128)} %bitcast.9.refs_0_, bf16[256,1024]{1,0:T(8,128)(2,1)} %copy-done.15, bf16[256,1024]{1,0:T(8,128)(2,1)} %copy-done.31, bf16[128,2048]{1,0:T(8,128)(2,1)} %copy-done.16, bf16[128,2048]{1,0:T(8,128)(2,1)} %copy-done.32, ...), custom_call_target="tpu_custom_call" | custom-call | tf_op jit(solution)/shard_map/finish/pallas_call | solution.py:94
  (295 shorter events, 130.1 us)
Async XLA Ops:
  7.2 282.2 %reduce-scatter.3.cloned.1.call-start = ((), (), s32[]{:S(2)}) async-start(), calls=%async_computation.2 | async-start | bytes 5242880 | tf_op jit(solution)/shard_map/reduce_scatter | solution.py:937
  10.3 16.4 %collective-permute-start.5 = (bf16[768,1024]{1,0:T(8,128)(2,1)}, bf16[768,1024]{1,0:T(8,128)(2,1)}, u32[]{:S(2)}, u32[]{:S(2)}) collective-permute-start(bf16[768,1024]{1,0:T(8,128)(2,1)} %bitcast.78), channel_id=1, source_target_pairs={{0,1},{1,0},{2,3},{3,2},{4,5},{5,4},{6,7},{7,6},{8,9},{9,8},{10,11... | collective-permute-start | bytes 4718600 | tf_op jit(solution)/shard_map/ppermute | solution.py:27
  18.5 24.0 %collective-permute-start.4 = (bf16[3,256,1024]{2,1,0:T(8,128)(2,1)}, bf16[3,256,1024]{2,1,0:T(8,128)(2,1)S(1)}, u32[]{:S(2)}, u32[]{:S(2)}) collective-permute-start(bf16[3,256,1024]{2,1,0:T(8,128)(2,1)} %get-tuple-element.148.refs_1_), channel_id=1, source_target_pairs={{0,1},{1,0},{2,3},{3,2},{4,5},{5,4},{6,7},{7,6},{8,9},{9,8},{10,11... | collective-permute-start | bytes 4718600 | tf_op jit(solution)/shard_map/ppermute | solution.py:27
  19.0 36.8 %collective-permute-start.3 = (bf16[3,256,1024]{2,1,0:T(8,128)(2,1)}, bf16[3,256,1024]{2,1,0:T(8,128)(2,1)S(1)}, u32[]{:S(2)}, u32[]{:S(2)}) collective-permute-start(bf16[3,256,1024]{2,1,0:T(8,128)(2,1)} %get-tuple-element.148.refs_1_), channel_id=1, source_target_pairs={{0,2},{2,0},{1,3},{3,1},{4,6},{6,4},{5,7},{7,5},{8,10},{10,8},{9,1... | collective-permute-start | bytes 4718600 | tf_op jit(solution)/shard_map/ppermute | solution.py:27
  83.4 14.9 %collective-permute-start.11 = (bf16[2,256,256]{2,1,0:T(8,128)(2,1)}, bf16[2,256,256]{2,1,0:T(8,128)(2,1)S(1)}, u32[]{:S(2)}, u32[]{:S(2)}) collective-permute-start(bf16[2,256,256]{2,1,0:T(8,128)(2,1)} %get-tuple-element.165), channel_id=1, source_target_pairs={{0,1},{1,0},{2,3},{3,2},{4,5},{5,4},{6,7},{7,6},{8,9},{9,8},{10,11... | collective-permute-start | bytes 786440 | tf_op jit(solution)/shard_map/ppermute | solution.py:27
  162.5 19.9 %collective-permute-start.16 = (bf16[2,3,256,256]{3,2,1,0:T(8,128)(2,1)}, bf16[2,3,256,256]{3,2,1,0:T(8,128)(2,1)S(1)}, u32[]{:S(2)}, u32[]{:S(2)}) collective-permute-start(bf16[2,3,256,256]{3,2,1,0:T(8,128)(2,1)} %get-tuple-element.187), channel_id=1, source_target_pairs={{0,2},{2,0},{1,3},{3,1},{4,6},{6,4},{5,7},{7,5},{8,10},{10,8},{9,1... | collective-permute-start | bytes 2359304 | tf_op jit(solution)/shard_map/ppermute | solution.py:27
  183.2 157.4 %reduce-scatter.5.cloned.1.call-start = ((), (), s32[]{:S(2)}) async-start(), calls=%async_computation.3 | async-start | bytes 2621440 | tf_op jit(solution)/shard_map/reduce_scatter | solution.py:969
  185.3 26.8 %collective-permute-start.17 = (bf16[512,1024]{1,0:T(8,128)(2,1)}, bf16[512,1024]{1,0:T(8,128)(2,1)}, u32[]{:S(2)}, u32[]{:S(2)}) collective-permute-start(bf16[512,1024]{1,0:T(8,128)(2,1)} %slice.81), channel_id=1, source_target_pairs={{0,4},{4,0},{1,5},{5,1},{2,6},{6,2},{3,7},{7,3},{8,12},{12,8},{9,1... | collective-permute-start | bytes 3145736 | tf_op jit(solution)/shard_map/ppermute | solution.py:27
  213.7 39.8 %collective-permute-start.22 = (bf16[512,1024]{1,0:T(8,128)(2,1)}, bf16[512,1024]{1,0:T(8,128)(2,1)}, u32[]{:S(2)}, u32[]{:S(2)}) collective-permute-start(bf16[512,1024]{1,0:T(8,128)(2,1)} %slice.83), channel_id=1, source_target_pairs={{0,4},{4,0},{1,5},{5,1},{2,6},{6,2},{3,7},{7,3},{8,12},{12,8},{9,1... | collective-permute-start | bytes 3145736 | tf_op jit(solution)/shard_map/ppermute | solution.py:27
  223.5 30.0 %collective-permute-start.23 = (bf16[1024,256]{1,0:T(8,128)(2,1)S(1)}, bf16[1024,256]{1,0:T(8,128)(2,1)}, u32[]{:S(2)}, u32[]{:S(2)}) collective-permute-start(bf16[1024,256]{1,0:T(8,128)(2,1)S(1)} %constant_dynamic-slice_fusion.12), channel_id=1, source_target_pairs={{0,2},{2,0},{1,3},{3,1},{4,6},{6,4},{5,7},{7,5},{8,10},{10,8},{9,1... | collective-permute-start | bytes 1572872 | tf_op jit(solution)/shard_map/ppermute | solution.py:27
  261.3 28.0 %collective-permute-start.25 = (bf16[2,256,1024]{2,1,0:T(8,128)(2,1)S(1)}, bf16[2,256,1024]{2,1,0:T(8,128)(2,1)S(1)}, u32[]{:S(2)}, u32[]{:S(2)}) collective-permute-start(bf16[2,256,1024]{2,1,0:T(8,128)(2,1)S(1)} %add_convert_fusion.2.refs_14_), channel_id=1, source_target_pairs={{0,2},{2,0},{1,3},{3,1},{4,6},{6,4},{5,7},{7,5},{8,10},{10,8},{9,1... | collective-permute-start | bytes 3145736 | tf_op jit(solution)/shard_map/ppermute | solution.py:27
  262.9 26.4 %collective-permute-start.26 = (bf16[4,128,256]{2,1,0:T(8,128)(2,1)S(1)}, bf16[4,128,256]{2,1,0:T(8,128)(2,1)S(1)}, u32[]{:S(2)}, u32[]{:S(2)}) collective-permute-start(bf16[4,128,256]{2,1,0:T(8,128)(2,1)S(1)} %constant_dynamic-slice_fusion.11), channel_id=1, source_target_pairs={{0,4},{4,0},{1,5},{5,1},{2,6},{6,2},{3,7},{7,3},{8,12},{12,8},{9,1... | collective-permute-start | bytes 786440 | tf_op jit(solution)/shard_map/ppermute | solution.py:27
  290.9 23.7 %collective-permute-start.31 = (bf16[2,256,1024]{2,1,0:T(8,128)(2,1)}, bf16[2,256,1024]{2,1,0:T(8,128)(2,1)}, u32[]{:S(2)}, u32[]{:S(2)}) collective-permute-start(bf16[2,256,1024]{2,1,0:T(8,128)(2,1)} %get-tuple-element.244), channel_id=1, source_target_pairs={{0,1},{1,0},{2,3},{3,2},{4,5},{5,4},{6,7},{7,6},{8,9},{9,8},{10,11... | collective-permute-start | bytes 3145736 | tf_op jit(solution)/shard_map/ppermute | solution.py:27
  291.4 28.7 %collective-permute-start.27 = (bf16[1,256,1024]{2,1,0:T(8,128)(2,1)}, bf16[1,256,1024]{2,1,0:T(8,128)(2,1)}, u32[]{:S(2)}, u32[]{:S(2)}) collective-permute-start(bf16[1,256,1024]{2,1,0:T(8,128)(2,1)} %get-tuple-element.231), channel_id=1, source_target_pairs={{0,1},{1,0},{2,3},{3,2},{4,5},{5,4},{6,7},{7,6},{8,9},{9,8},{10,11... | collective-permute-start | bytes 1572872 | tf_op jit(solution)/shard_map/ppermute | solution.py:27
  292.6 19.0 %collective-permute-start.30 = (bf16[128,2048]{1,0:T(8,128)(2,1)S(1)}, bf16[128,2048]{1,0:T(8,128)(2,1)}, u32[]{:S(2)}, u32[]{:S(2)}) collective-permute-start(bf16[128,2048]{1,0:T(8,128)(2,1)S(1)} %constant_dynamic-slice_fusion.10.refs_6_), channel_id=1, source_target_pairs={{0,4},{4,0},{1,5},{5,1},{2,6},{6,2},{3,7},{7,3},{8,12},{12,8},{9,1... | collective-permute-start | bytes 1572872 | tf_op jit(solution)/shard_map/ppermute | solution.py:27
  297.9 14.3 %collective-permute-start.29 = (bf16[1,256,1024]{2,1,0:T(8,128)(2,1)}, bf16[1,256,1024]{2,1,0:T(8,128)(2,1)}, u32[]{:S(2)}, u32[]{:S(2)}) collective-permute-start(bf16[1,256,1024]{2,1,0:T(8,128)(2,1)} %add_convert_fusion.8), channel_id=1, source_target_pairs={{0,2},{2,0},{1,3},{3,1},{4,6},{6,4},{5,7},{7,5},{8,10},{10,8},{9,1... | collective-permute-start | bytes 1572872 | tf_op jit(solution)/shard_map/ppermute | solution.py:27
  312.2 19.0 %collective-permute-start.33 = (bf16[4,128,768]{2,1,0:T(8,128)(2,1)}, bf16[4,128,768]{2,1,0:T(8,128)(2,1)S(1)}, u32[]{:S(2)}, u32[]{:S(2)}) collective-permute-start(bf16[4,128,768]{2,1,0:T(8,128)(2,1)} %get-tuple-element.258), channel_id=1, source_target_pairs={{0,4},{4,0},{1,5},{5,1},{2,6},{6,2},{3,7},{7,3},{8,12},{12,8},{9,1... | collective-permute-start | bytes 2359304 | tf_op jit(solution)/shard_map/ppermute | solution.py:27
  345.7 19.9 %collective-permute-start.37 = (bf16[2,38,1024]{2,1,0:T(8,128)(2,1)S(1)}, bf16[2,38,1024]{2,1,0:T(8,128)(2,1)S(1)}, u32[]{:S(2)}, u32[]{:S(2)}) collective-permute-start(bf16[2,38,1024]{2,1,0:T(8,128)(2,1)S(1)} %maximum_select_fusion.1), channel_id=1, source_target_pairs={{0,16},{8,24},{16,0},{24,8},{1,17},{9,25},{17,1},{25,9},{2,18},{10... | collective-permute-start | bytes 466952 | tf_op jit(solution)/shard_map/ppermute | solution.py:1019
  345.7 19.9 %collective-permute-start.36 = (bf16[2,38,1024]{2,1,0:T(8,128)(2,1)S(1)}, bf16[2,38,1024]{2,1,0:T(8,128)(2,1)S(1)}, u32[]{:S(2)}, u32[]{:S(2)}) collective-permute-start(bf16[2,38,1024]{2,1,0:T(8,128)(2,1)S(1)} %maximum_select_fusion.1), channel_id=1, source_target_pairs={{0,8},{8,0},{16,24},{24,16},{1,9},{9,1},{17,25},{25,17},{2,10},{10... | collective-permute-start | bytes 466952 | tf_op jit(solution)/shard_map/ppermute | solution.py:1019
  346.8 20.3 %collective-permute-start.39 = (bf16[256,1024]{1,0:T(8,128)(2,1)}, bf16[256,1024]{1,0:T(8,128)(2,1)S(1)}, u32[]{:S(2)}, u32[]{:S(2)}) collective-permute-start(bf16[256,1024]{1,0:T(8,128)(2,1)} %reduce-scatter.5.cloned.1.call-done), channel_id=1, source_target_pairs={{0,2},{2,0},{1,3},{3,1},{4,6},{6,4},{5,7},{7,5},{8,10},{10,8},{9,1... | collective-permute-start | bytes 1572872 | tf_op jit(solution)/shard_map/ppermute | solution.py:27
  348.2 19.8 %collective-permute-start.40 = (bf16[128,2048]{1,0:T(8,128)(2,1)S(1)}, bf16[128,2048]{1,0:T(8,128)(2,1)S(1)}, u32[]{:S(2)}, u32[]{:S(2)}) collective-permute-start(bf16[128,2048]{1,0:T(8,128)(2,1)S(1)} %copy-done.5), channel_id=1, source_target_pairs={{0,2},{2,0},{1,3},{3,1},{4,6},{6,4},{5,7},{7,5},{8,10},{10,8},{9,1... | collective-permute-start | bytes 1572872 | tf_op jit(solution)/shard_map/ppermute | solution.py:27
  351.0 18.2 %collective-permute-start.45 = (bf16[128,1024]{1,0:T(8,128)(2,1)S(1)}, bf16[128,1024]{1,0:T(8,128)(2,1)S(1)}, u32[]{:S(2)}, u32[]{:S(2)}) collective-permute-start(bf16[128,1024]{1,0:T(8,128)(2,1)S(1)} %get-tuple-element.277), channel_id=1, source_target_pairs={{0,24},{8,16},{16,8},{24,0},{1,25},{9,17},{17,9},{25,1},{2,26},{10... | collective-permute-start | bytes 786440 | tf_op jit(solution)/shard_map/ppermute | solution.py:783
  368.4 21.3 %collective-permute-start.41 = (bf16[256,1024]{1,0:T(8,128)(2,1)S(1)}, bf16[256,1024]{1,0:T(8,128)(2,1)S(1)}, u32[]{:S(2)}, u32[]{:S(2)}) collective-permute-start(bf16[256,1024]{1,0:T(8,128)(2,1)S(1)} %add_convert_fusion.6.refs_1_), channel_id=1, source_target_pairs={{0,1},{1,0},{2,3},{3,2},{4,5},{5,4},{6,7},{7,6},{8,9},{9,8},{10,11... | collective-permute-start | bytes 1572872 | tf_op jit(solution)/shard_map/ppermute | solution.py:27
  368.6 21.1 %collective-permute-start.42 = (bf16[128,2048]{1,0:T(8,128)(2,1)S(1)}, bf16[128,2048]{1,0:T(8,128)(2,1)S(1)}, u32[]{:S(2)}, u32[]{:S(2)}) collective-permute-start(bf16[128,2048]{1,0:T(8,128)(2,1)S(1)} %add_convert_fusion.5.refs_3_), channel_id=1, source_target_pairs={{0,1},{1,0},{2,3},{3,2},{4,5},{5,4},{6,7},{7,6},{8,9},{9,8},{10,11... | collective-permute-start | bytes 1572872 | tf_op jit(solution)/shard_map/ppermute | solution.py:27
  (72 other events, 512.4 us)
Sparse Core Ops, SparseCore 0:
  182.5 79.4 reduce-scatter.2
  265.0 47.8 reduce-scatter.4
